TPU v7x, 32 devices: a whole 2x2x4 slice. The times are simulated.
32 devices in a mesh: batch: 8 (over z, x), blk: 4 (over y, core).
Axes of the slice: x: 2, y: 2, z: 4, core: 2. Of those that a mesh axis runs over, the one named last changes fastest.
Arguments:
- tokens: bfloat16 [48, 512, 768], P('batch', 'blk'), may hold values from -6 to 6
- segment_ids: int32 [48, 512], P('batch'), may hold values from 0 to 2, as said below
- query_weight: bfloat16 [768, 768], replicated, may hold values from -0.21875 to 0.21875
- query_bias: bfloat16 [768], replicated, may hold values from -3 to 3
- key_weight: bfloat16 [768, 768], replicated, may hold values from -0.21875 to 0.21875
- value_weight: bfloat16 [768, 768], replicated, may hold values from -0.21875 to 0.21875
- value_bias: bfloat16 [768], replicated, may hold values from -3 to 3
- output_weight: bfloat16 [768, 768], replicated, may hold values from -0.625 to 0.625
- output_bias: bfloat16 [768], replicated, may hold values from -3 to 3
- attn_gain: bfloat16 [768], replicated, may hold values from 0.25 to 1.75
- attn_shift: bfloat16 [768], replicated, may hold values from -3 to 3
- inner_weight: bfloat16 [768, 3072], replicated, may hold values from -0.21875 to 0.21875
- inner_bias: bfloat16 [3072], replicated, may hold values from -3 to 3
- outer_weight: bfloat16 [3072, 768], replicated, may hold values from -0.15625 to 0.15625
- outer_bias: bfloat16 [768], replicated, may hold values from -3 to 3
- final_gain: bfloat16 [768], replicated, may hold values from 0.25 to 1.75
- final_shift: bfloat16 [768], replicated, may hold values from -3 to 3
- cotangent: bfloat16 [48, 512, 768], P('batch', 'blk'), may hold values from -6 to 6
Outputs:
- layer_output: bfloat16 [48, 512, 768], P('batch', 'blk')
- input_grad: bfloat16 [48, 512, 768], P('batch', 'blk')
- query_weight_grad: float32 [768, 768], P('batch')
- query_bias_grad: float32 [768], P('batch')
- key_weight_grad: float32 [768, 768], P('batch')
- value_weight_grad: float32 [768, 768], P('batch')
- value_bias_grad: float32 [768], P('batch')
- output_weight_grad: float32 [768, 768], P('batch')
- output_bias_grad: float32 [768], P('batch')
- attn_gain_grad: float32 [768], P('batch')
- attn_shift_grad: float32 [768], P('batch')
- inner_weight_grad: float32 [768, 3072], P('batch')
- inner_bias_grad: float32 [3072], P('batch')
- outer_weight_grad: float32 [3072, 768], P('batch')
- outer_bias_grad: float32 [768], P('batch')
- final_gain_grad: float32 [768], P('batch')
- final_shift_grad: float32 [768], P('batch')
Inputs may be any that keep to these rules, and one draw needn't show every extreme that they name: `segment_ids`: every row holds the ids 0, 1 and 2 in that order, each as one run of positions; positions attend only within their own id. Id 1 covers the positions from some position below 128 to some position at or past 512 - 128.
All inputs are finite; a program needn't handle non-finite values.
Results may differ from a plain program's by a relative error of at most 0.02.
Values may be sent and summed in bfloat16 or wider, within the bound.
No kernel may reach another device: no remote copies, remote signals or barrier semaphores. Data moves between devices by JAX's collectives and lax.ppermute only.
A program may use at most 192 MiB of HBM per device.

v0:
```python
import jax
import jax.numpy as jnp
from jax import lax
from jax.sharding import PartitionSpec as P

H = 12
HD = 64


EPSILON = 1e-12
NEGATIVE = -1e30


def norm_rows(hidden, gain, shift):
    center = hidden - jnp.mean(hidden, axis=-1, keepdims=True)
    spread = jnp.mean(center * center, axis=-1, keepdims=True)
    return center * lax.rsqrt(spread + EPSILON) * gain + shift


def gelu_exact(values):
    return jax.nn.gelu(values, approximate=False)


def forward_product(inputs, matrix):
    return jnp.einsum("std,de->ste", inputs, matrix, preferred_element_type=jnp.float32)


def weight_term(inputs, gradient):
    return jnp.einsum("std,ste->de", inputs, gradient, preferred_element_type=jnp.float32)


def back_product(gradient, matrix):
    return jnp.einsum("ste,de->std", gradient, matrix, preferred_element_type=jnp.float32)


def bias_term(gradient):
    return jnp.sum(gradient.astype(jnp.float32), axis=(0, 1))


def per_device(
    tokens,
    segment_ids,
    query_weight,
    query_bias,
    key_weight,
    value_weight,
    value_bias,
    output_weight,
    output_bias,
    attn_gain,
    attn_shift,
    inner_weight,
    inner_bias,
    outer_weight,
    outer_bias,
    final_gain,
    final_shift,
    cotangent,
):
    count, span, width = tokens.shape
    length = segment_ids.shape[1]
    scale = HD ** (-0.5)
    low_type = jnp.bfloat16
    own_segments = lax.dynamic_slice_in_dim(segment_ids, lax.axis_index("blk") * span, span, 1)
    inputs = tokens.astype(jnp.float32)
    query = (forward_product(tokens, query_weight) + query_bias).astype(low_type)
    keys = forward_product(tokens, key_weight).astype(low_type)
    values = (forward_product(tokens, value_weight) + value_bias).astype(low_type)
    query_heads = query.reshape(count, span, H, HD)

    def block_scores(key_piece, key_segments):
        positions = key_piece.shape[1]
        key_heads = key_piece.reshape(count, positions, H, HD)
        scores = (
            jnp.einsum(
                "sqhd,skhd->shqk", query_heads, key_heads, preferred_element_type=jnp.float32
            )
            * scale
        )
        allowed = own_segments[:, None, :, None] == key_segments[:, None, None, :]
        return (scores, allowed)

    highest = jnp.full((count, H, span), NEGATIVE, jnp.float32)
    key_piece = lax.all_gather(keys, "blk", axis=1, tiled=True)
    value_piece = lax.all_gather(values, "blk", axis=1, tiled=True)
    positions = key_piece.shape[1]
    key_segments = segment_ids
    scores, allowed = block_scores(key_piece, key_segments)
    new_highest = jnp.maximum(highest, jnp.max(jnp.where(allowed, scores, NEGATIVE), axis=-1))
    weights_now = jnp.where(allowed, jnp.exp(scores - new_highest[..., None]), 0.0)
    total = jnp.sum(weights_now, axis=-1)
    value_heads = value_piece.reshape(count, positions, H, HD)
    running = jnp.einsum(
        "shqk,skhd->shqd",
        weights_now.astype(low_type),
        value_heads,
        preferred_element_type=jnp.float32,
    )
    highest, total, running = (new_highest, total, running)
    mixed = jnp.transpose(running / total[..., None], (0, 2, 1, 3))
    logsum = highest + jnp.log(total)
    mixed_low = mixed.reshape(count, span, width).astype(low_type)
    branch = forward_product(mixed_low, output_weight) + output_bias
    first, first_pull = jax.vjp(
        norm_rows, inputs + branch, attn_gain.astype(jnp.float32), attn_shift.astype(jnp.float32)
    )
    first_low = first.astype(low_type)
    inner = forward_product(first_low, inner_weight) + inner_bias
    act, act_pull = jax.vjp(gelu_exact, inner)
    act_low = act.astype(low_type)
    second = first + forward_product(act_low, outer_weight) + outer_bias
    result, final_pull = jax.vjp(
        norm_rows, second, final_gain.astype(jnp.float32), final_shift.astype(jnp.float32)
    )
    d_second, final_gain_part, final_shift_part = final_pull(cotangent.astype(jnp.float32))
    d_outer = d_second.astype(low_type)
    outer_weight_part = weight_term(act_low, d_outer)
    outer_bias_part = bias_term(d_outer)
    (d_inner_full,) = act_pull(back_product(d_outer, outer_weight))
    d_inner = d_inner_full.astype(low_type)
    inner_weight_part = weight_term(first_low, d_inner)
    inner_bias_part = bias_term(d_inner)
    d_first = d_second + back_product(d_inner, inner_weight)
    d_attn, attn_gain_part, attn_shift_part = first_pull(d_first)
    d_branch = d_attn.astype(low_type)
    output_weight_part = weight_term(mixed_low, d_branch)
    output_bias_part = bias_term(d_branch)
    d_mixed = back_product(d_branch, output_weight).astype(low_type)
    grad_heads = d_mixed.reshape(count, span, H, HD)
    back_keys, back_values = (
        lax.all_gather(keys, "blk", axis=1, tiled=True),
        lax.all_gather(values, "blk", axis=1, tiled=True),
    )
    scores, allowed = block_scores(back_keys, segment_ids)
    probs = jnp.where(allowed, jnp.exp(scores - logsum[..., None]), 0.0)
    probs_low = probs.astype(low_type)
    key_heads = back_keys.reshape(count, length, H, HD)
    value_heads = back_values.reshape(count, length, H, HD)
    d_probs = jnp.einsum(
        "sqhd,skhd->shqk", grad_heads, value_heads, preferred_element_type=jnp.float32
    )
    inner_sum = jnp.sum(probs * d_probs, axis=-1)
    d_scores = (probs * (d_probs - inner_sum[..., None])).astype(low_type)
    d_query = (
        (
            jnp.einsum("shqk,skhd->sqhd", d_scores, key_heads, preferred_element_type=jnp.float32)
            * scale
        )
        .reshape(count, span, width)
        .astype(low_type)
    )
    rows_here = span * lax.axis_size("blk")
    key_term = (
        jnp.einsum("shqk,sqhd->kshd", d_scores, query_heads, preferred_element_type=jnp.float32)
        * scale
    )
    value_term = jnp.einsum(
        "shqk,sqhd->kshd", probs_low, grad_heads, preferred_element_type=jnp.float32
    )
    key_value_grad = lax.psum_scatter(
        jnp.concatenate(
            (
                key_term.reshape(rows_here, count, width),
                value_term.reshape(rows_here, count, width),
            ),
            axis=2,
        ).astype(jnp.bfloat16),
        "blk",
        scatter_dimension=0,
        tiled=True,
    ).astype(jnp.float32)
    d_key = key_value_grad[:, :, :width].astype(low_type)
    d_value = key_value_grad[:, :, width:].astype(low_type)
    query_weight_part = weight_term(tokens, d_query)
    query_bias_part = bias_term(d_query)
    key_weight_part = jnp.einsum("std,tse->de", tokens, d_key, preferred_element_type=jnp.float32)
    value_weight_part = jnp.einsum(
        "std,tse->de", tokens, d_value, preferred_element_type=jnp.float32
    )
    value_bias_part = bias_term(d_value)
    input_grad = (
        d_attn
        + back_product(d_query, query_weight)
        + jnp.einsum("tse,de->std", d_key, key_weight, preferred_element_type=jnp.float32)
        + jnp.einsum("tse,de->std", d_value, value_weight, preferred_element_type=jnp.float32)
    ).astype(low_type)
    pieces = (
        lax.psum_scatter(query_weight_part, "batch", scatter_dimension=0, tiled=True),
        lax.psum_scatter(query_bias_part, "batch", scatter_dimension=0, tiled=True),
        lax.psum_scatter(key_weight_part, "batch", scatter_dimension=0, tiled=True),
        lax.psum_scatter(value_weight_part, "batch", scatter_dimension=0, tiled=True),
        lax.psum_scatter(value_bias_part, "batch", scatter_dimension=0, tiled=True),
        lax.psum_scatter(output_weight_part, "batch", scatter_dimension=0, tiled=True),
        lax.psum_scatter(output_bias_part, "batch", scatter_dimension=0, tiled=True),
        lax.psum_scatter(attn_gain_part, "batch", scatter_dimension=0, tiled=True),
        lax.psum_scatter(attn_shift_part, "batch", scatter_dimension=0, tiled=True),
        lax.psum_scatter(inner_weight_part, "batch", scatter_dimension=0, tiled=True),
        lax.psum_scatter(inner_bias_part, "batch", scatter_dimension=0, tiled=True),
        lax.psum_scatter(outer_weight_part, "batch", scatter_dimension=0, tiled=True),
        lax.psum_scatter(outer_bias_part, "batch", scatter_dimension=0, tiled=True),
        lax.psum_scatter(final_gain_part, "batch", scatter_dimension=0, tiled=True),
        lax.psum_scatter(final_shift_part, "batch", scatter_dimension=0, tiled=True),
    )
    summed = (
        lax.psum(pieces[0].astype(jnp.bfloat16), "blk").astype(jnp.float32),
        lax.psum(pieces[1].astype(jnp.bfloat16), "blk").astype(jnp.float32),
        lax.psum(pieces[2].astype(jnp.bfloat16), "blk").astype(jnp.float32),
        lax.psum(pieces[3].astype(jnp.bfloat16), "blk").astype(jnp.float32),
        lax.psum(pieces[4].astype(jnp.bfloat16), "blk").astype(jnp.float32),
        lax.psum(pieces[5].astype(jnp.bfloat16), "blk").astype(jnp.float32),
        lax.psum(pieces[6].astype(jnp.bfloat16), "blk").astype(jnp.float32),
        lax.psum(pieces[7].astype(jnp.bfloat16), "blk").astype(jnp.float32),
        lax.psum(pieces[8].astype(jnp.bfloat16), "blk").astype(jnp.float32),
        lax.psum(pieces[9].astype(jnp.bfloat16), "blk").astype(jnp.float32),
        lax.psum(pieces[10].astype(jnp.bfloat16), "blk").astype(jnp.float32),
        lax.psum(pieces[11].astype(jnp.bfloat16), "blk").astype(jnp.float32),
        lax.psum(pieces[12].astype(jnp.bfloat16), "blk").astype(jnp.float32),
        lax.psum(pieces[13].astype(jnp.bfloat16), "blk").astype(jnp.float32),
        lax.psum(pieces[14].astype(jnp.bfloat16), "blk").astype(jnp.float32),
    )
    return (
        result.astype(low_type),
        input_grad,
        summed[0],
        summed[1],
        summed[2],
        summed[3],
        summed[4],
        summed[5],
        summed[6],
        summed[7],
        summed[8],
        summed[9],
        summed[10],
        summed[11],
        summed[12],
        summed[13],
        summed[14],
    )


def solution(mesh):
    return jax.shard_map(
        per_device,
        mesh=mesh,
        in_specs=(
            P("batch", "blk", None),
            P("batch", None),
            P(),
            P(),
            P(),
            P(),
            P(),
            P(),
            P(),
            P(),
            P(),
            P(),
            P(),
            P(),
            P(),
            P(),
            P(),
            P("batch", "blk", None),
        ),
        out_specs=(
            P("batch", "blk", None),
            P("batch", "blk", None),
            P("batch", None),
            P("batch"),
            P("batch", None),
            P("batch", None),
            P("batch"),
            P("batch", None),
            P("batch"),
            P("batch"),
            P("batch"),
            P("batch", None),
            P("batch"),
            P("batch", None),
            P("batch"),
            P("batch"),
            P("batch"),
        ),
        check_vma=False,
    )
```

profile of v0, /device:TPU:0, one launch (start us, length us, event | category | flops | bytes accessed | tf_op | source)
XLA Modules:
  0.0 1017.6 jit_solution(3032457995498872442)
XLA Ops:
  7.3 3.9 convolution_convert_fusion.1
  11.3 2.1 add_convert_fusion.2
  20.0 2.5 add_convert_fusion.3
  24.2 27.3 %all-gather.3.cloned.1.call-done = bf16[6,512,768]{2,1,0:T(8,128)(2,1)} async-done(((bf16[6,128,768]{2,1,0:T(8,128)(2,1)}), bf16[6,512,768]{2,1,0:T(8,128)(2,1)}) %all-gather.3.cloned.1.call-update) | async-done | bytes 4718608 | tf_op jit(solution)/shard_map/all_gather | solution.py:84
  51.5 6.6 copy.70
  58.1 7.8 select_reduce_fusion
  66.0 5.4 fusion
  73.1 18.1 %all-gather.5.cloned.1.call-done = bf16[6,512,768]{2,1,0:T(8,128)(2,1)} async-done(((bf16[6,128,768]{2,1,0:T(8,128)(2,1)}), bf16[6,512,768]{2,1,0:T(8,128)(2,1)}) %all-gather.5.cloned.1.call-update) | async-done | bytes 4718608 | tf_op jit(solution)/shard_map/all_gather | solution.py:85
  91.1 6.6 copy.71
  97.8 10.6 %fusion.36 = bf16[6,128,12,64]{1,3,2,0:T(8,128)(2,1)S(1)} fusion(bf16[6,512,12,64]{1,3,2,0:T(8,128)(2,1)} %bitcast.123, f32[6,12,128,512]{3,2,1,0:T(8,128)} %copy-done.2, f32[6,12,128]{2,1,0:T(8,128)S(1)} %broadcast_maximum_fusion, pred[6,128,512]{2,1,0:T(8,128)(4,1)S(1)} %broadcast_compare_fusion, f32[6,128,12]{1,2,0:T(8,128)S(1)} %bitcast.135), kind=kOutput, calls=%fused_computation.65 | convolution fusion | flops 624033792 | bytes 25239552 | tf_op jit(solution)/shard_map/shqk,skhd->shqd/dot_general | solution.py:93
  110.4 9.2 fusion.38
  119.6 22.9 %multiply_convert_fusion.2 = (bf16[6,128,3072]{2,1,0:T(8,128)(2,1)S(1)}, f32[6,128,3072]{2,1,0:T(8,128)}) fusion(f32[6,128,3072]{2,1,0:T(8,128)S(1)} %get-tuple-element.117, f32[3072]{0:T(1024)S(1)} %copy-done.27, u8[128,3072]{1,0:T(8,128)(4,1)S(1)} %get-tuple-element.69, u8[128,3072]{1,0:T(8,128)(4,1)S(1)} %get-tuple-element.68), kind=kLoop, calls=%fused_computation.22 | loop fusion | flops 167510016 | bytes 24391680 | tf_op jit(solution)/shard_map/convert_element_type | solution.py:110
  142.6 4.1 fusion.72
  146.7 1.5 fusion.33
  148.3 1.9 fusion.34
  150.1 2.5 convert_reduce_fusion.2
  152.7 12.9 %convert_reduce_fusion = (f32[3072]{0:T(1024)}, bf16[6,128,3072]{2,1,0:T(8,128)(2,1)}) fusion(f32[6,128,3072]{2,1,0:T(8,128)} %get-tuple-element.109, bf16[6,128,768]{2,1,0:T(8,128)(2,1)S(1)} %get-tuple-element.103, bf16[3072,768]{1,0:T(8,128)(2,1)} %param.31, f32[6,128,3072]{2,1,0:T(8,128)S(1)} %get-tuple-element.117, f32[3072]{0:T(1024)S(1)} %copy-done.27), kind=kOutput, calls=%fused_computation.18 | convolution fusion | flops 3663983616 | bytes 29515776 | tf_op jit(solution)/shard_map/ste,de->std/dot_general | solution.py:33
  165.5 8.9 multiply_reduce_fusion.1
  175.3 1.4 copy-done.4
  178.6 2.1 convolution_convert_fusion
  180.7 2.4 copy.73
  183.1 10.5 %fusion.28 = bf16[6,12,64,512]{3,2,1,0:T(8,128)(2,1)} fusion(bf16[6,128,12,64]{1,3,2,0:T(8,128)(2,1)} %bitcast.128, f32[6,12,128,512]{3,2,1,0:T(8,128)} %copy-done.2, f32[6,12,128]{2,1,0:T(8,128)S(1)} %copy-done.25, pred[6,128,512]{2,1,0:T(8,128)(4,1)S(1)} %copy-done.8), kind=kOutput, calls=%fused_computation.56 | convolution fusion | flops 625213440 | bytes 25202688 | tf_op jit(solution)/shard_map/shqk,sqhd->kshd/dot_general | solution.py:157
  193.6 15.4 %multiply_reduce_fusion = (f32[6,12,128]{2,1,0:T(8,128)}, f32[6,12,128,512]{3,2,1,0:T(8,128)}) fusion(f32[6,12,128,512]{3,2,1,0:T(8,128)} %copy-done.2, f32[6,12,128]{2,1,0:T(8,128)S(1)} %copy-done.25, pred[6,128,512]{2,1,0:T(8,128)(4,1)S(1)} %copy-done.8, bf16[6,128,12,64]{1,3,2,0:T(8,128)(2,1)S(1)} %bitcast.129, bf16[6,512,12,64]{1,3,2,0:T(8,128)(2,1)} %bitcast.124), kind=kOutput, calls=%fused_computation.1 | convolution fusion | flops 627563520 | bytes 44113920 | tf_op jit(solution)/shard_map/sqhd,skhd->shqk/dot_general | solution.py:139
  209.0 6.6 copy.76
  215.7 13.6 %multiply_convert_fusion = bf16[6,12,128,512]{3,2,1,0:T(8,128)(2,1)S(1)} fusion(f32[6,12,128,512]{3,2,1,0:T(8,128)} %get-tuple-element.122, f32[6,12,128,512]{3,2,1,0:T(8,128)} %copy-done.2, f32[6,12,128]{2,1,0:T(8,128)} %get-tuple-element.121, f32[6,12,128]{2,1,0:T(8,128)} %log_add_fusion, pred[6,128,512]{2,1,0:T(8,128)(4,1)} %copy-done.7), kind=kLoop, calls=%fused_computation | loop fusion | flops 28311552 | bytes 47652864 | tf_op jit(solution)/shard_map/convert_element_type | solution.py:143
  229.3 3.5 multiply_convert_fusion.1
  232.8 1.5 copy-done.3
  234.3 6.6 copy.75
  240.9 9.0 pad_maximum_fusion
  251.2 3.9 convolution_bitcast_fusion.2
  255.6 11.7 %convert_reduce_fusion.5 = (f32[12,64]{1,0:T(8,128)}, bf16[6,12,64,128]{3,2,1,0:T(8,128)(2,1)S(1)}) fusion(bf16[6,512,12,64]{1,3,2,0:T(8,128)(2,1)} %bitcast.122, bf16[6,12,128,512]{3,2,1,0:T(8,128)(2,1)} %copy-done.3), kind=kOutput, calls=%fused_computation.70 | convolution fusion | flops 606338304 | bytes 15338496 | tf_op jit(solution)/shard_map/shqk,skhd->sqhd/dot_general | solution.py:146
  267.3 2.5 convolution_bitcast_fusion.5
  269.8 3.0 copy.90
  272.9 9.7 convolution_bitcast_fusion.1
  283.9 8.8 convolution_bitcast_fusion
  292.8 35.7 %reduce-scatter.14.cloned.1.call-done = bf16[128,6,1536]{2,0,1:T(8,128)(2,1)} async-done(((bf16[512,6,1536]{2,0,1:T(8,128)(2,1)}), bf16[128,6,1536]{2,0,1:T(8,128)(2,1)}) %reduce-scatter.14.cloned.1.call-update) | async-done | bytes 2359312 | tf_op jit(solution)/shard_map/reduce_scatter | solution.py:160
  328.5 2.7 convolution_bitcast_fusion.3
  331.2 2.0 copy.94
  333.3 1.6 copy-done.12
  334.9 3.8 convolution_bitcast_fusion.4
  338.7 3.1 copy.92
  344.4 3.8 fusion.53
  348.2 52.6 %reduce-scatter.16.cloned.1.call-done = f32[96,768]{1,0:T(8,128)} async-done(((f32[768,768]{1,0:T(8,128)}), f32[96,768]{1,0:T(8,128)}) %reduce-scatter.16.cloned.1.call-update) | async-done | bytes 294928 | tf_op jit(solution)/shard_map/reduce_scatter | solution.py:193
  400.8 1.6 convert_element_type.245
  402.4 69.8 %reduce-scatter.22.cloned.1.call-done = f32[96,768]{1,0:T(8,128)} async-done(((f32[768,768]{1,0:T(8,128)}), f32[96,768]{1,0:T(8,128)}) %reduce-scatter.22.cloned.1.call-update) | async-done | bytes 294928
  472.2 1.8 copy.91
  474.2 38.2 %all-reduce.9 = (bf16[768]{0:T(1024)(128)(2,1)S(1)}, bf16[768]{0:T(1024)(128)(2,1)S(1)}, bf16[768]{0:T(1024)(128)(2,1)S(1)}, bf16[768]{0:T(1024)(128)(2,1)S(1)},...) all-reduce(f32[768]{0:T(1024)S(1)} %reduce_sum.216, ...), channel_id=4, replica_groups=mesh['batch'=8,'blk'=4] {'batch'}, use_global_device_ids=true, to_apply=%region_15.16.clone | all-reduce | flops 9216 | bytes 55296
  513.1 6.3 all-reduce.10
  524.1 114.7 %reduce-scatter.18.cloned.1.call-done = f32[96,3072]{1,0:T(8,128)} async-done(((f32[768,3072]{1,0:T(8,128)}), f32[96,3072]{1,0:T(8,128)}) %reduce-scatter.18.cloned.1.call-update) | async-done | bytes 1179664 | tf_op jit(solution)/shard_map/reduce_scatter | solution.py:197
  638.8 2.2 convert_element_type.254
  641.0 163.9 %reduce-scatter.20.cloned.1.call-done = f32[384,768]{1,0:T(8,128)} async-done(((f32[3072,768]{1,0:T(8,128)}), f32[384,768]{1,0:T(8,128)}) %reduce-scatter.20.cloned.1.call-update) | async-done | bytes 1179664 | tf_op jit(solution)/shard_map/reduce_scatter | solution.py:199
  804.9 2.2 convert_element_type.259
  807.1 69.1 %reduce-scatter.26.cloned.1.call-done = f32[96,768]{1,0:T(8,128)} async-done(((f32[768,768]{1,0:T(8,128)}), f32[96,768]{1,0:T(8,128)}) %reduce-scatter.26.cloned.1.call-update) | async-done | bytes 294928
  876.2 1.8 copy.95
  878.0 69.8 %reduce-scatter.24.cloned.1.call-done = f32[96,768]{1,0:T(8,128)} async-done(((f32[768,768]{1,0:T(8,128)}), f32[96,768]{1,0:T(8,128)}) %reduce-scatter.24.cloned.1.call-update) | async-done | bytes 294928
  947.8 1.8 copy.93
  949.6 2.5 fusion.50
  952.3 2.2 fusion.35
  954.5 45.7 %all-reduce.14.cloned.1.call-done = (bf16[96,768]{0,1:T(8,128)(2,1)}, bf16[96,768]{0,1:T(8,128)(2,1)}, bf16[96,768]{0,1:T(8,128)(2,1)}, bf16[96,768]{1,0:T(8,128...) async-done(((bf16[96,768]{0,1:T(8,128)(2,1)}, bf16[96,768]{0,1:T(8,128)(2,1)}, bf16[96,768]{0,1:T(8,128)(2,1)}, bf16[96,768]{1,0:T(8,128)(2,1)}, ...) | async-done | bytes 1769488 | tf_op jit(solution)/shard_map/psum | solution.py:205
  1000.2 1.8 copy.81
  1002.0 1.9 copy.82
  1003.9 1.8 copy.83
  1005.6 1.6 convert_element_type.246
  1007.3 2.2 convert_element_type.255
  (151 shorter events, 26.1 us)
Async XLA Ops:
  7.2 101.2 %copy-start = (bf16[768,768]{1,0:T(8,128)(2,1)S(1)}, bf16[768,768]{1,0:T(8,128)(2,1)}, u32[]{:S(2)}) copy-start(bf16[768,768]{1,0:T(8,128)(2,1)} %param.25) | copy-start | bytes 3538948
  7.2 4.1 copy-start.20
  7.2 4.0 copy-start.37
  7.2 4.0 copy-start.14
  7.2 44.3 %all-gather.3.cloned.1.call-start = ((), (), s32[]{:S(2)}) async-start(), calls=%async_computation.7 | async-start | bytes 5898240 | tf_op jit(solution)/shard_map/all_gather | solution.py:84
  11.2 79.9 %all-gather.5.cloned.1.call-start = ((), (), s32[]{:S(2)}) async-start(), calls=%async_computation.8 | async-start | bytes 5898240 | tf_op jit(solution)/shard_map/all_gather | solution.py:85
  11.3 2.2 copy-start.38
  11.3 2.2 copy-start.39
  13.4 315.1 %reduce-scatter.14.cloned.1.call-start = ((), (), s32[]{:S(2)}) async-start(), calls=%async_computation.9 | async-start | bytes 11796480 | tf_op jit(solution)/shard_map/reduce_scatter | solution.py:160
  22.5 1.4 copy-start.31
  24.2 73.6 %copy-start.7 = (pred[6,128,512]{2,1,0:T(8,128)(4,1)}, pred[6,128,512]{2,1,0:T(8,128)(4,1)S(1)}, u32[]{:S(2)}) copy-start(pred[6,128,512]{2,1,0:T(8,128)(4,1)S(1)} %broadcast_compare_fusion) | copy-start | bytes 1179652
  66.0 6.5 copy-start.2
  97.8 10.6 %copy-start.21 = (bf16[6,128,768]{2,1,0:T(8,128)(2,1)S(1)}, bf16[6,128,768]{2,1,0:T(8,128)(2,1)}, u32[]{:S(2)}) copy-start(bf16[6,128,768]{2,1,0:T(8,128)(2,1)} %param.18) | copy-start | bytes 3538948
  108.4 1.3 copy-start.23
  109.7 0.7 copy-start.27
  109.7 32.8 %slice-start = ((s8[4718592]{0:T(1024)(128)(4,1)}), s8[4194304]{0:T(1024)(128)(4,1)S(1)}, s32[]{:S(2)}) async-start(s8[4718592]{0:T(1024)(128)(4,1)} %bitcast.136), calls=%async_computation.17 | async-start | bytes 8388608
  110.4 32.1 %slice-start.1 = ((s8[4718592]{0:T(1024)(128)(4,1)}), s8[524288]{0:T(1024)(128)(4,1)S(1)}, s32[]{:S(2)}) async-start(s8[4718592]{0:T(1024)(128)(4,1)} %bitcast.136), calls=%async_computation.18 | async-start | bytes 1048576
  119.6 22.9 %copy-start.36 = (f32[768]{0:T(1024)S(1)}, f32[768]{0:T(1024)}, u32[]{:S(2)}) copy-start(f32[768]{0:T(1024)} %convert_element_type.218) | copy-start | bytes 9220
  142.5 4.2 copy-start.11
  142.5 4.2 copy-start.9
  142.5 4.2 copy-start.26
  148.2 1.9 copy-start.32
  152.7 12.9 %copy-start.16 = (bf16[6,128,768]{2,1,0:T(8,128)(2,1)}, bf16[6,128,768]{2,1,0:T(8,128)(2,1)S(1)}, u32[]{:S(2)}) copy-start(bf16[6,128,768]{2,1,0:T(8,128)(2,1)S(1)} %get-tuple-element.103) | copy-start | bytes 3538948
  175.2 1.5 copy-start.4
  175.2 2.3 copy-start.28
  177.5 1.0 copy-start.18
  180.7 2.4 copy-start.8
  180.7 2.4 copy-start.25
  183.1 10.5 %copy-start.10 = (bf16[6,128,768]{1,2,0:T(8,128)(2,1)S(1)}, bf16[6,128,768]{1,2,0:T(8,128)(2,1)}, u32[]{:S(2)}) copy-start(bf16[6,128,768]{1,2,0:T(8,128)(2,1)} %copy.73) | copy-start | bytes 3538948
  215.7 13.6 %copy-start.6 = (bf16[6,128,768]{1,2,0:T(8,128)(2,1)S(1)}, bf16[6,128,768]{1,2,0:T(8,128)(2,1)}, u32[]{:S(2)}) copy-start(bf16[6,128,768]{1,2,0:T(8,128)(2,1)} %copy.69) | copy-start | bytes 3538948
  229.3 5.0 copy-start.3
  249.9 1.3 copy-start.19
  250.0 150.8 %reduce-scatter.16.cloned.1.call-start = ((), (), s32[]{:S(2)}) async-start(), calls=%async_computation.10 | async-start | bytes 2654208 | tf_op jit(solution)/shard_map/reduce_scatter | solution.py:193
  255.1 217.1 %reduce-scatter.22.cloned.1.call-start = ((), (), s32[]{:S(2)}) async-start(), calls=%async_computation.13 | async-start | bytes 2654208
  255.6 11.7 %copy-start.22 = (bf16[6,128,768]{2,1,0:T(8,128)(2,1)S(1)}, bf16[6,128,768]{2,1,0:T(8,128)(2,1)}, u32[]{:S(2)}) copy-start(bf16[6,128,768]{2,1,0:T(8,128)(2,1)} %param.18) | copy-start | bytes 3538948
  272.9 366.0 %reduce-scatter.18.cloned.1.call-start = ((), (), s32[]{:S(2)}) async-start(), calls=%async_computation.11 | async-start | bytes 10616832 | tf_op jit(solution)/shard_map/reduce_scatter | solution.py:197
  282.6 1.3 copy-start.17
  282.7 522.2 %reduce-scatter.20.cloned.1.call-start = ((), (), s32[]{:S(2)}) async-start(), calls=%async_computation.12 | async-start | bytes 10616832 | tf_op jit(solution)/shard_map/reduce_scatter | solution.py:199
  292.8 583.5 %reduce-scatter.26.cloned.1.call-start = ((), (), s32[]{:S(2)}) async-start(), calls=%async_computation.15 | async-start | bytes 2654208
  333.2 1.7 copy-start.12
  333.3 614.5 %reduce-scatter.24.cloned.1.call-start = ((), (), s32[]{:S(2)}) async-start(), calls=%async_computation.14 | async-start | bytes 2654208
  341.8 0.7 copy-start.40
  341.8 2.5 copy-start.30
  341.8 658.4 %all-reduce.14.cloned.1.call-start = ((), (), s32[]{:S(2)}) async-start(), calls=%async_computation.16 | async-start | bytes 3833856 | tf_op jit(solution)/shard_map/psum | solution.py:205
  344.4 129.8 %copy-start.33 = (f32[768]{0:T(1024)S(1)}, f32[768]{0:T(1024)}, u32[]{:S(2)}) copy-start(f32[768]{0:T(1024)} %get-tuple-element.72) | copy-start | bytes 9220
  344.4 129.8 %copy-start.34 = (f32[768]{0:T(1024)S(1)}, f32[768]{0:T(1024)}, u32[]{:S(2)}) copy-start(f32[768]{0:T(1024)} %get-tuple-element.102) | copy-start | bytes 9220
  344.4 129.8 %copy-start.35 = (f32[768]{0:T(1024)S(1)}, f32[768]{0:T(1024)}, u32[]{:S(2)}) copy-start(f32[768]{0:T(1024)} %get-tuple-element.104) | copy-start | bytes 9220
  804.9 147.3 %copy-start.15 = (bf16[768,768]{1,0:T(8,128)(2,1)S(1)}, bf16[768,768]{1,0:T(8,128)(2,1)}, u32[]{:S(2)}) copy-start(bf16[768,768]{1,0:T(8,128)(2,1)} %param.23) | copy-start | bytes 3538948
  949.6 2.6 copy-start.5
  949.6 2.7 copy-start.13
  949.6 2.7 copy-start.29
  1000.2 9.3 copy-start.24
  1002.0 8.6 copy-start.1
Sparse Core Ops, SparseCore 0:
  11.3 40.1 all-gather.2
  53.6 37.4 all-gather.4
  250.1 78.3 reduce-scatter.13
  331.8 68.8 reduce-scatter.15
  404.1 68.0 reduce-scatter.21
  475.6 163.1 reduce-scatter.17
  642.4 162.3 reduce-scatter.19
  808.3 67.8 reduce-scatter.25
  879.7 68.0 reduce-scatter.23
  951.6 48.5 all-reduce.13
where the time goes:
time: 1030 us; the launch traced here: 1020 us
  waiting for transfers between devices  667 us (65%)
  matrix products  146 us (14%)
  other arithmetic  82.2 us (8%)
  local copies, waits for them, and re-layouts  60.7 us (6%)
  blocking collectives  44.5 us (4%)
  between operations  16.2 us (2%)
    unnamed x13, waiting for transfers between devices  209 us
    reduce_scatter x1, waiting for transfers between devices, per_device(): lax.psum_scatter(outer_weight_part, 'batch', scatter_dimension=0, tiled=T...  164 us
    reduce_scatter x1, waiting for transfers between devices, per_device(): lax.psum_scatter(inner_weight_part, 'batch', scatter_dimension=0, tiled=T...  115 us
    reduce_scatter x1, waiting for transfers between devices, per_device(): lax.psum_scatter(output_weight_part, 'batch', scatter_dimension=0, tiled=...  52.6 us
    psum x1, waiting for transfers between devices, per_device(): lax.psum(pieces[0].astype(jnp.bfloat16), 'blk').astype(jnp.float32)  45.7 us
    unnamed x1, blocking collectives  38.2 us
    reduce_scatter x1, waiting for transfers between devices, per_device(): lax.psum_scatter(jnp.concatenate((key_term.reshape(rows_here, count, widt...  35.7 us
    unnamed x105, local copies, waits for them, and re-layouts  30.3 us
  transfers between devices with their start and end apart: 10, of which 10 were waited for; matrix products, arithmetic and copies ran while one was open for 11% of the time, Pallas kernels for 0%

commit v1 on v0

v1 whole, which is shorter than its diff:
```python
import functools

import jax
import jax.numpy as jnp
from jax import lax
from jax.experimental import pallas as pl
from jax.experimental.pallas import tpu as pltpu
from jax.sharding import PartitionSpec as P

H = 12
HD = 64
EPSILON = 1e-12
NEGATIVE = -1e30
LOW = jnp.bfloat16
F32 = jnp.float32
LOG2E = 1.4426950408889634
MIB = 1024 * 1024


def dot_nn(a, b):
    return lax.dot_general(a, b, (((1,), (0,)), ((), ())), preferred_element_type=F32)


def dot_nt(a, b):
    return lax.dot_general(a, b, (((1,), (1,)), ((), ())), preferred_element_type=F32)


def dot_tn(a, b):
    return lax.dot_general(a, b, (((0,), (0,)), ((), ())), preferred_element_type=F32)


def params(mib):
    return pltpu.CompilerParams(vmem_limit_bytes=mib * MIB)


def attend_kernel(
    where, own, sib, seg_row, seg_col, wq, wk, wv, bq, bv,
    q_out, k_out, v_out, e_out, inv_out, mix_own, mix_sib,
):
    half = own.shape[1]
    x = jnp.concatenate([own[0], sib[0]], axis=0)
    q = (dot_nn(x, wq[...]) + bq[...].astype(F32)).astype(LOW)
    k = dot_nn(x, wk[...]).astype(LOW)
    v = (dot_nn(x, wv[...]) + bv[...].astype(F32)).astype(LOW)
    q_out[0] = q
    k_out[0] = k
    v_out[0] = v
    bias = jnp.where(seg_col[0] == seg_row[0], 0.0, NEGATIVE)
    heads = q.shape[1] // HD
    parts = []
    for h in range(heads):
        cols = slice(h * HD, (h + 1) * HD)
        s = dot_nt(q[:, cols], k[:, cols]) + bias
        top = jnp.max(s, axis=1, keepdims=True)
        e = jnp.exp2((s - top) * (LOG2E * HD**-0.5))
        low = e.astype(LOW)
        total = jnp.sum(e, axis=1, keepdims=True)
        inv = 1.0 / total
        e_out[0, h] = low
        inv_out[0, :, h : h + 1] = inv
        parts.append(dot_nn(low, v[:, cols]) * inv)
    mixed = jnp.concatenate(parts, axis=1).astype(LOW)
    mix_own[0] = mixed[:half]
    mix_sib[0] = mixed[half:]


def attend(c, own, sib, seg_row, seg_col, wq, wk, wv, bq, bv):
    rows, half, width = own.shape
    length = 2 * half
    cols = width // 2
    heads = cols // HD
    row3 = lambda shape: pl.BlockSpec((1,) + shape, lambda r, w: (r, 0, 0))
    weight = pl.BlockSpec((width, cols), lambda r, w: (0, w[0]))
    bias = pl.BlockSpec((1, cols), lambda r, w: (0, w[0]))
    sds = jax.ShapeDtypeStruct
    return pl.pallas_call(
        attend_kernel,
        grid_spec=pltpu.PrefetchScalarGridSpec(
            num_scalar_prefetch=1,
            grid=(rows,),
            in_specs=[
                row3((half, width)), row3((half, width)), row3((1, length)), row3((length, 1)),
                weight, weight, weight, bias, bias,
            ],
            out_specs=[
                row3((length, cols)), row3((length, cols)), row3((length, cols)),
                pl.BlockSpec((1, heads, length, length), lambda r, w: (r, 0, 0, 0)),
                row3((length, heads)), row3((half, cols)), row3((half, cols)),
            ],
        ),
        out_shape=[
            sds((rows, length, cols), LOW), sds((rows, length, cols), LOW),
            sds((rows, length, cols), LOW), sds((rows, heads, length, length), LOW),
            sds((rows, length, heads), F32), sds((rows, half, cols), LOW),
            sds((rows, half, cols), LOW),
        ],
        compiler_params=params(56),
        name="attend",
    )(c, own, sib, seg_row, seg_col, wq, wk, wv, bq, bv)


def norm_parts(v):
    center = v - jnp.mean(v, axis=1, keepdims=True)
    spread = jnp.mean(center * center, axis=1, keepdims=True)
    scale = lax.rsqrt(spread + EPSILON)
    return center * scale, scale


def norm_back(dn, n, scale):
    return scale * (
        dn - jnp.mean(dn, axis=1, keepdims=True) - n * jnp.mean(dn * n, axis=1, keepdims=True)
    )


def gelu_parts(v):
    phi_core = jnp.exp2(v * v * (-0.5 * LOG2E))
    t = 1.0 / (1.0 + (0.3275911 * 0.7071067811865476) * jnp.abs(v))
    poly = t * (
        0.5 * 0.254829592
        + t * (-0.5 * 0.284496736 + t * (0.5 * 1.421413741 + t * (-0.5 * 1.453152027 + t * (0.5 * 1.061405429))))
    )
    tail = poly * phi_core
    big = jnp.where(v >= 0, 1.0 - tail, tail)
    return v * big, big + v * (phi_core * 0.3989422804014327)


def col_sum(v):
    return jnp.sum(v, axis=0, keepdims=True)


def middle_kernel(
    where, own, mix_own, mix_sib, cot, wo_own, wo_sib, w1, w2, bo, ag, ash, b1, b2, fg, fsh,
    out, act, dinner, firstT, douterT, dattn, dbranch, dmix_own, dmix_sib,
    v_ob, v_b1, v_b2, v_ag, v_as, v_fg, v_fs,
    slope,
):
    i = pl.program_id(0)
    x = own[0].astype(F32)
    branch = dot_nn(mix_own[0], wo_own[...]) + dot_nn(mix_sib[0], wo_sib[...])
    n1, s1 = norm_parts(x + (branch + bo[...].astype(F32)))
    first = n1 * ag[...].astype(F32) + ash[...].astype(F32)
    first_low = first.astype(LOW)
    firstT[...] = first_low.T
    second = first + b2[...].astype(F32)
    hidden = w1.shape[1]
    step = 512
    for j in range(0, hidden, step):
        cols = slice(j, j + step)
        inner = dot_nn(first_low, w1[:, cols]) + b1[:, cols].astype(F32)
        a, d = gelu_parts(inner)
        a_low = a.astype(LOW)
        act[0, :, cols] = a_low
        slope[:, cols] = d
        second = second + dot_nn(a_low, w2[cols, :])
    n2, s2 = norm_parts(second)
    gain = fg[...].astype(F32)
    out[0] = (n2 * gain + fsh[...].astype(F32)).astype(LOW)
    g = cot[0].astype(F32)
    d_second = norm_back(g * gain, n2, s2)
    d_outer = d_second.astype(LOW)
    douterT[...] = d_outer.T
    sums = {}
    sums[0] = (v_fg, col_sum(g * n2))
    sums[1] = (v_fs, col_sum(g))
    sums[2] = (v_b2, col_sum(d_outer.astype(F32)))
    d_first = d_second
    parts = []
    for j in range(0, hidden, step):
        cols = slice(j, j + step)
        di = (dot_nt(d_outer, w2[cols, :]) * slope[:, cols]).astype(LOW)
        dinner[0, :, cols] = di
        parts.append(col_sum(di.astype(F32)))
        d_first = d_first + dot_nt(di, w1[:, cols])
    sums[3] = (v_b1, jnp.concatenate(parts, axis=1))
    sums[4] = (v_ag, col_sum(d_first * n1))
    sums[5] = (v_as, col_sum(d_first))
    d_attn = norm_back(d_first * ag[...].astype(F32), n1, s1)
    dattn[0] = d_attn
    d_branch = d_attn.astype(LOW)
    dbranch[0] = d_branch
    sums[6] = (v_ob, col_sum(d_branch.astype(F32)))
    dmix_own[0] = dot_nt(d_branch, wo_own[...]).astype(LOW)
    dmix_sib[0] = dot_nt(d_branch, wo_sib[...]).astype(LOW)

    @pl.when(i == 0)
    def _():
        for ref, value in sums.values():
            ref[...] = value

    @pl.when(i > 0)
    def _():
        for ref, value in sums.values():
            ref[...] += value


def middle(c, own, mix_own, mix_sib, cot, wo, w1, w2, bo, ag, ash, b1, b2, fg, fsh):
    rows, half, width = own.shape
    hidden = w1.shape[1]
    cols = width // 2
    row3 = lambda n: pl.BlockSpec((1, half, n), lambda r, w: (r, 0, 0))
    one = pl.Buffered(1)
    fixed = lambda *s: pl.BlockSpec(s, lambda r, w: (0,) * len(s), pipeline_mode=one)
    tr = pl.BlockSpec((width, half), lambda r, w: (0, r))
    vec = lambda n: pl.BlockSpec((1, n), lambda r, w: (0, 0))
    sds = jax.ShapeDtypeStruct
    tokens = rows * half
    return pl.pallas_call(
        middle_kernel,
        grid_spec=pltpu.PrefetchScalarGridSpec(
            num_scalar_prefetch=1,
            grid=(rows,),
            in_specs=[
                row3(width), row3(cols), row3(cols), row3(width),
                pl.BlockSpec((cols, width), lambda r, w: (w[0], 0), pipeline_mode=one),
                pl.BlockSpec((cols, width), lambda r, w: (1 - w[0], 0), pipeline_mode=one),
                fixed(width, hidden), fixed(hidden, width),
                vec(width), vec(width), vec(width), vec(hidden), vec(width), vec(width), vec(width),
            ],
            out_specs=[
                row3(width), row3(hidden), row3(hidden), tr, tr, row3(width), row3(width),
                row3(cols), row3(cols),
                vec(width), vec(hidden), vec(width), vec(width), vec(width), vec(width), vec(width),
            ],
            scratch_shapes=[pltpu.VMEM((half, hidden), F32)],
        ),
        out_shape=[
            sds((rows, half, width), LOW), sds((rows, half, hidden), LOW),
            sds((rows, half, hidden), LOW), sds((width, tokens), LOW), sds((width, tokens), LOW),
            sds((rows, half, width), F32), sds((rows, half, width), LOW),
            sds((rows, half, cols), LOW), sds((rows, half, cols), LOW),
            sds((1, width), F32), sds((1, hidden), F32), sds((1, width), F32),
            sds((1, width), F32), sds((1, width), F32), sds((1, width), F32), sds((1, width), F32),
        ],
        compiler_params=params(60),
        name="middle",
    )(c, own, mix_own, mix_sib, cot, wo, wo, w1, w2, bo, ag, ash, b1, b2, fg, fsh)


def attend_back_kernel(
    where, own, sib, q_ref, k_ref, v_ref, e_ref, inv_ref, mix_own, mix_sib, dm_own, dm_sib,
    wq, wk, wv,
    in_own, in_sib, gq, gk, gv, v_qb, v_vb,
    aq, ak, av,
):
    i = pl.program_id(0)
    half = own.shape[1]
    scale = HD**-0.5
    q, k, v = q_ref[0], k_ref[0], v_ref[0]
    mixed = jnp.concatenate([mix_own[0], mix_sib[0]], axis=0)
    dm = jnp.concatenate([dm_own[0], dm_sib[0]], axis=0)
    heads = q.shape[1] // HD
    dq, dk, dv = [], [], []
    for h in range(heads):
        cols = slice(h * HD, (h + 1) * HD)
        inv = inv_ref[0, :, h : h + 1]
        d_out = dm[:, cols].astype(F32) * inv
        delta = jnp.sum(d_out * mixed[:, cols].astype(F32), axis=1, keepdims=True)
        d_low = d_out.astype(LOW)
        e = e_ref[0, h]
        dp = dot_nt(d_low, v[:, cols])
        ds = (e.astype(F32) * (dp - delta)).astype(LOW)
        dq.append(dot_nn(ds, k[:, cols]) * scale)
        dk.append(dot_tn(ds, q[:, cols]) * scale)
        dv.append(dot_tn(e, d_low))
    dq = jnp.concatenate(dq, axis=1).astype(LOW)
    dk = jnp.concatenate(dk, axis=1).astype(LOW)
    dv = jnp.concatenate(dv, axis=1).astype(LOW)
    back = dot_nt(dq, wq[...]) + dot_nt(dk, wk[...]) + dot_nt(dv, wv[...])
    in_own[0] = back[:half]
    in_sib[0] = back[half:].astype(LOW)
    x = jnp.concatenate([own[0], sib[0]], axis=0)
    tq, tk, tv = dot_tn(x, dq), dot_tn(x, dk), dot_tn(x, dv)
    sq, sv = col_sum(dq.astype(F32)), col_sum(dv.astype(F32))

    @pl.when(i == 0)
    def _():
        aq[...] = tq
        ak[...] = tk
        av[...] = tv
        v_qb[...] = sq
        v_vb[...] = sv

    @pl.when(i > 0)
    def _():
        aq[...] += tq
        ak[...] += tk
        av[...] += tv
        v_qb[...] += sq
        v_vb[...] += sv

    @pl.when(i == pl.num_programs(0) - 1)
    def _():
        shards, size = gq.shape[0], gq.shape[1]
        for s in range(shards):
            at = where[1 + s]
            part = slice(s * size, (s + 1) * size)
            gq[at] = aq[part].astype(LOW)
            gk[at] = ak[part].astype(LOW)
            gv[at] = av[part].astype(LOW)


def attend_back(where, shards, own, sib, q, k, v, e, inv, mix_own, mix_sib, dm_own, dm_sib, wq, wk, wv):
    rows, half, width = own.shape
    length = 2 * half
    cols = width // 2
    heads = cols // HD
    row3 = lambda a, n: pl.BlockSpec((1, a, n), lambda r, w: (r, 0, 0))
    weight = pl.BlockSpec((width, cols), lambda r, w: (0, w[0]))
    sds = jax.ShapeDtypeStruct
    size = width // shards
    grad = pl.BlockSpec((shards, size, cols), lambda r, w: (0, 0, 0))
    vec = pl.BlockSpec((1, cols), lambda r, w: (0, 0))
    return pl.pallas_call(
        attend_back_kernel,
        grid_spec=pltpu.PrefetchScalarGridSpec(
            num_scalar_prefetch=1,
            grid=(rows,),
            in_specs=[
                row3(half, width), row3(half, width),
                row3(length, cols), row3(length, cols), row3(length, cols),
                pl.BlockSpec((1, heads, length, length), lambda r, w: (r, 0, 0, 0)),
                row3(length, heads),
                row3(half, cols), row3(half, cols), row3(half, cols), row3(half, cols),
                weight, weight, weight,
            ],
            out_specs=[row3(half, width), row3(half, width), grad, grad, grad, vec, vec],
            scratch_shapes=[pltpu.VMEM((width, cols), F32)] * 3,
        ),
        out_shape=[
            sds((rows, half, width), F32), sds((rows, half, width), LOW),
            sds((shards, size, cols), LOW), sds((shards, size, cols), LOW),
            sds((shards, size, cols), LOW), sds((1, cols), F32), sds((1, cols), F32),
        ],
        compiler_params=params(60),
        name="attend_back",
    )(where, own, sib, q, k, v, e, inv, mix_own, mix_sib, dm_own, dm_sib, wq, wk, wv)


def rows_kernel(where, left, right, keep, send, *, base):
    h = pl.program_id(0)
    value = dot_nn(left[...], right[...])
    shards, size = keep.shape[0], keep.shape[1]

    def put(ref):
        for s in range(shards):
            ref[where[1 + s]] = value[s * size : (s + 1) * size].astype(LOW)

    pl.when(h == 1)(lambda: put(keep))
    pl.when(h == 0)(lambda: put(send))


def rows_grad(where, shards, left, right, tile):
    m, tokens = left.shape
    n = right.shape[1]
    half = n // 2
    tiles = half // tile
    size = m // shards
    sds = jax.ShapeDtypeStruct

    def right_at(h, j, w):
        return (0, jnp.where(h == 1, w[0], 1 - w[0]) * tiles + j)

    return pl.pallas_call(
        functools.partial(rows_kernel, base=0),
        grid_spec=pltpu.PrefetchScalarGridSpec(
            num_scalar_prefetch=1,
            grid=(2, tiles),
            in_specs=[
                pl.BlockSpec((m, tokens), lambda h, j, w: (0, 0)),
                pl.BlockSpec((tokens, tile), right_at),
            ],
            out_specs=[
                pl.BlockSpec((shards, size, tile), lambda h, j, w: (0, 0, jnp.where(h == 1, j, 0))),
                pl.BlockSpec((shards, size, tile), lambda h, j, w: (0, 0, jnp.where(h == 0, j, tiles - 1))),
            ],
        ),
        out_shape=[sds((shards, size, half), LOW)] * 2,
        compiler_params=params(48),
        name="rows_grad",
    )(where, left, right)


def cols_kernel(where, left, right, keep, send, *, group):
    h = pl.program_id(0)
    value = dot_nn(left[...], right[...]).astype(LOW)
    size = value.shape[1] // group
    j = pl.program_id(1)

    def put(ref):
        for g in range(group):
            ref[where[1 + j * group + g]] = value[:, g * size : (g + 1) * size]

    pl.when(h == 1)(lambda: put(keep))
    pl.when(h == 0)(lambda: put(send))


def cols_grad(where, shards, left, right):
    m, tokens = left.shape
    n = right.shape[1]
    half = m // 2
    size = n // shards
    group = 2 if shards % 2 == 0 else 1
    sds = jax.ShapeDtypeStruct
    whole = pl.BlockSpec((shards, half, size), lambda h, j, w: (0, 0, 0))
    return pl.pallas_call(
        functools.partial(cols_kernel, group=group),
        grid_spec=pltpu.PrefetchScalarGridSpec(
            num_scalar_prefetch=1,
            grid=(2, shards // group),
            in_specs=[
                pl.BlockSpec((half, tokens), lambda h, j, w: (jnp.where(h == 1, w[0], 1 - w[0]), 0)),
                pl.BlockSpec((tokens, group * size), lambda h, j, w: (0, j)),
            ],
            out_specs=[whole, whole],
        ),
        out_shape=[sds((shards, half, size), LOW)] * 2,
        compiler_params=params(48),
        name="cols_grad",
    )(where, left, right)


def flip_order(v, index, bits):
    rest = v.shape[1:]
    v = v.reshape((2,) * bits + rest)
    for axis in range(bits):
        bit = (index >> (bits - 1 - axis)) & 1
        v = jnp.where(bit == 1, jnp.flip(v, axis), v)
    order = tuple(range(bits))[::-1] + tuple(range(bits, bits + len(rest)))
    return jnp.transpose(v, order).reshape((2**bits,) + rest)


def swap(v, axis, mask, size):
    return lax.ppermute(v, axis, [(i, i ^ mask) for i in range(size)])


def add_low(*terms):
    total = terms[0].astype(F32)
    for t in terms[1:]:
        total = total + t.astype(F32)
    return total.astype(LOW)


def fix(v):
    return lax.optimization_barrier(v)


def solution(mesh):
    batch_size = mesh.shape["batch"]
    blk_size = mesh.shape["blk"]
    bits = batch_size.bit_length() - 1
    direct = batch_size == 2**bits and 768 % (16 * batch_size) == 0 and 3072 % (128 * batch_size) == 0
    shards = batch_size if direct else 1

    def blk_swap(v, mask):
        return swap(v, "blk", mask, blk_size)

    def reduce_batch(g):
        for k in range(bits):
            half = g.shape[0] // 2
            got = swap(g[half:], "batch", 1 << k, batch_size)
            g = fix(add_low(g[:half], got))
        return g[0]

    def reduce_y(g):
        return add_low(g, blk_swap(g, 2))

    def per_device(
        tokens, segment_ids, query_weight, query_bias, key_weight, value_weight, value_bias,
        output_weight, output_bias, attn_gain, attn_shift, inner_weight, inner_bias,
        outer_weight, outer_bias, final_gain, final_shift, cotangent,
    ):
        count, span, width = tokens.shape
        rows = count // 2
        me = lax.axis_index("blk")
        b = lax.axis_index("batch")
        core = me & 1
        y = (me >> 1) & 1
        if direct:
            rel = [b ^ s for s in range(shards)]
            places = [sum(((r >> k) & 1) << (bits - 1 - k) for k in range(bits)) for r in rel]
        else:
            places = [0]
        where = jnp.stack([core] + [jnp.asarray(p) for p in places]).astype(jnp.int32)

        def mine(v):
            return lax.dynamic_slice_in_dim(v, y * rows, rows, 0)

        def other(v):
            return lax.dynamic_slice_in_dim(v, (1 - y) * rows, rows, 0)

        def gather_rows(v):
            return jnp.concatenate([mine(v), blk_swap(other(v), 2)], axis=1)

        def return_rows(v):
            keep, got = v[:, :span], blk_swap(v[:, span:], 2)
            return jnp.where(
                y == 0, jnp.concatenate([keep, got], axis=0), jnp.concatenate([got, keep], axis=0)
            )

        def halves(mine_half, got, axis):
            return jnp.where(
                core == 0,
                jnp.concatenate([mine_half, got], axis=axis),
                jnp.concatenate([got, mine_half], axis=axis),
            )

        own = gather_rows(tokens)
        sib = blk_swap(own, 1)
        cot = gather_rows(cotangent)
        seg = mine(segment_ids).reshape(rows, 4, span)
        seg = jnp.concatenate(
            [lax.dynamic_index_in_dim(seg, me ^ r, 1, keepdims=False) for r in (0, 2, 1, 3)], axis=1
        )
        row = lambda v: v.reshape(1, -1)
        q, k, v, e, inv, mix_own, mix_out = attend(
            where, own, sib, seg[:, None, :], seg[:, :, None],
            query_weight, key_weight, value_weight, row(query_bias), row(value_bias),
        )
        mix_sib = blk_swap(mix_out, 1)
        (
            out, act, dinner, first_t, douter_t, dattn, dbranch, dm_own, dm_out,
            v_ob, v_b1, v_b2, v_ag, v_as, v_fg, v_fs,
        ) = middle(
            where, own, mix_own, mix_sib, cot, output_weight, inner_weight, outer_weight,
            row(output_bias), row(attn_gain), row(attn_shift), row(inner_bias), row(outer_bias),
            row(final_gain), row(final_shift),
        )
        result = return_rows(out)
        dm_sib = blk_swap(dm_out, 1)
        flat = lambda v: v.reshape(-1, v.shape[-1])
        outer_keep, outer_send = cols_grad(where, shards, douter_t, flat(act))
        inner_keep, inner_send = rows_grad(where, shards, first_t, flat(dinner), 512)
        mix_t = halves(flat(mix_own), flat(mix_sib), 1).T
        branch_keep, branch_send = rows_grad(where, shards, mix_t, flat(dbranch), 384)
        outer_part = add_low(outer_keep, blk_swap(outer_send, 1))
        inner_part = add_low(inner_keep, blk_swap(inner_send, 1))
        branch_part = add_low(branch_keep, blk_swap(branch_send, 1))
        in_own, in_out, gq, gk, gv, v_qb, v_vb = attend_back(
            where, shards, own, sib, q, k, v, e, inv, mix_own, mix_out, dm_own, dm_sib,
            query_weight, key_weight, value_weight,
        )
        in_grad = (dattn + in_own + blk_swap(in_out, 1).astype(F32)).astype(LOW)
        input_grad = return_rows(in_grad)

        half_cols = width // 2
        zero = jnp.zeros((1, half_cols), F32)

        def spread(v):
            return jnp.where(
                core == 0, jnp.concatenate([v, zero], axis=1), jnp.concatenate([zero, v], axis=1)
            )

        vectors = [spread(v_qb), spread(v_vb), v_ob, v_ag, v_as, v_b1, v_b2, v_fg, v_fs]
        packed = jnp.concatenate([v.reshape(batch_size, -1) for v in vectors], axis=1)
        extra = packed.shape[1]

        def join(v, axis):
            v = fix(v)
            return halves(v, blk_swap(v, 1), axis).astype(F32)

        if direct:
            size = width // shards
            lanes = half_cols
            extra_rows = -(-extra // lanes)
            padded = -(-extra_rows // 16) * 16
            packed = jnp.pad(packed, ((0, 0), (0, padded * lanes - extra))).astype(LOW)
            packed = flip_order(packed, b, bits).reshape(shards, padded, lanes)
            outer_done = reduce_y(reduce_batch(outer_part))
            inner_done = reduce_y(reduce_batch(inner_part))
            last = jnp.concatenate([gq, gk, gv, packed], axis=1)
            branch_done = reduce_y(reduce_batch(branch_part))
            last_done = reduce_y(reduce_batch(last))
            outer_grad = join(outer_done, 0).T
            inner_grad = join(inner_done, 1)
            output_grad = join(branch_done, 1)
            last_done = fix(last_done)
            last_got = blk_swap(last_done, 1)
            three = halves(last_done[: 3 * size], last_got[: 3 * size], 1).astype(F32)
            query_grad, key_grad, value_grad = three[:size], three[size : 2 * size], three[2 * size :]
            total = last_done[3 * size :].astype(F32) + last_got[3 * size :].astype(F32)
            total = total.reshape(-1)[:extra]
        else:
            def whole(v):
                return reduce_y(lax.psum_scatter(v, "batch", scatter_dimension=0, tiled=True))

            outer_grad = join(whole(outer_part[0].T), 1)
            inner_grad = join(whole(inner_part[0]), 1)
            output_grad = join(whole(branch_part[0]), 1)
            query_grad = join(whole(gq[0]), 1)
            key_grad = join(whole(gk[0]), 1)
            value_grad = join(whole(gv[0]), 1)
            total = lax.psum(lax.psum_scatter(packed, "batch", scatter_dimension=0, tiled=True), "blk")
            total = total.reshape(-1)
        sizes = [v.shape[1] // batch_size for v in vectors]
        pieces = []
        at = 0
        for n in sizes:
            pieces.append(total[at : at + n])
            at += n
        g_qb, g_vb, g_ob, g_ag, g_as, g_b1, g_b2, g_fg, g_fs = pieces
        return (
            result, input_grad, query_grad, g_qb, key_grad, value_grad, g_vb, output_grad, g_ob,
            g_ag, g_as, inner_grad, g_b1, outer_grad, g_b2, g_fg, g_fs,
        )

    tok = P("batch", "blk", None)
    mat = P("batch", None)
    vec = P("batch")
    return jax.shard_map(
        per_device,
        mesh=mesh,
        in_specs=(tok, P("batch", None)) + (P(),) * 15 + (tok,),
        out_specs=(
            tok, tok, mat, vec, mat, mat, vec, mat, vec, vec, vec, mat, vec, mat, vec, vec, vec,
        ),
        check_vma=False,
    )
```

time: 1030 us -> 316 us (0.31)
  waiting for transfers between devices: 667 us -> 99.1 us
  matrix products: 146 us -> 0 us
  Pallas kernels: 0 us -> 123 us
  other arithmetic: 82.2 us -> 20 us
  blocking collectives: 44.5 us -> 0 us
  starting transfers between devices: 0.82 us -> 26.6 us
  local copies, waits for them, and re-layouts: 60.7 us -> 39.5 us
  between operations: 16.2 us -> 1.8 us
    reduce_scatter x4 -> x0, waiting for transfers between devices: 367 us -> none  [the longest x1 164 us: per_device(): lax.psum_scatter(outer_weight_part, 'batch', scatter_dimension=0, tiled=T...]
    unnamed x13 -> x0, waiting for transfers between devices: 209 us -> none
    dot_general x24 -> x0, matrix products: 146 us -> none  [the longest x4 27.7 us: back_product(): jnp.einsum('ste,de->std', gradient, matrix, preferred_element_type=jnp.fl...]
    pallas_call x0 -> x6, Pallas kernels: none -> 123 us  [the longest x1 42.5 us: attend_back(): pl.pallas_call(attend_back_kernel, grid_spec=pltpu.PrefetchScalarGridSpec...]
    ppermute x0 -> x31, waiting for transfers between devices: none -> 99.1 us  [swap(): return lax.ppermute(v, axis, [(i, i ^ mask) for i in range(size)])]
    convert_element_type x26 -> x23, other arithmetic: 58.6 us -> 12.8 us  [the longest x19 10.2 us: add_low(): return total.astype(LOW)]
    psum x1 -> x0, waiting for transfers between devices: 45.7 us -> none  [per_device(): lax.psum(pieces[0].astype(jnp.bfloat16), 'blk').astype(jnp.float32)]
    all_gather x2 -> x0, waiting for transfers between devices: 45.4 us -> none  [the longest x1 27.3 us: per_device(): key_piece = lax.all_gather(keys, 'blk', axis=1, tiled=True)]
  transfers between devices with their start and end apart: 10 -> 31, of which waited for: 10 -> 13; matrix products, arithmetic and copies ran while one was open for 11% -> 16% of each run, Pallas kernels for 0% -> 26%
where the time goes in v1:
time: 316 us; the launch traced here: 310 us
  Pallas kernels  123 us (39%)
  waiting for transfers between devices  99.1 us (31%)
  local copies, waits for them, and re-layouts  39.5 us (12%)
  starting transfers between devices  26.6 us (8%)
  other arithmetic  20 us (6%)
    ppermute x31, waiting for transfers between devices, swap(): return lax.ppermute(v, axis, [(i, i ^ mask) for i in range(size)])  99.1 us
    pallas_call x1, Pallas kernels, attend_back(): pl.pallas_call(attend_back_kernel, grid_spec=pltpu.PrefetchScalarGridSpec...  42.5 us
    pallas_call x1, Pallas kernels, middle(): pl.pallas_call(middle_kernel, grid_spec=pltpu.PrefetchScalarGridSpec(num_...  40.3 us
    ppermute x31, starting transfers between devices, swap(): return lax.ppermute(v, axis, [(i, i ^ mask) for i in range(size)])  26.6 us
    pallas_call x1, Pallas kernels, attend(): pl.pallas_call(attend_kernel, grid_spec=pltpu.PrefetchScalarGridSpec(num_...  17 us
    unnamed x92, local copies, waits for them, and re-layouts  13.4 us
    pallas_call x2, Pallas kernels, rows_grad(): pl.pallas_call(functools.partial(rows_kernel, base=0), grid_spec=pltpu.Pr...  12.3 us
    pallas_call x1, Pallas kernels, cols_grad(): pl.pallas_call(functools.partial(cols_kernel, group=group), grid_spec=plt...  10.8 us
  transfers between devices with their start and end apart: 31, of which 13 were waited for; matrix products, arithmetic and copies ran while one was open for 16% of the time, Pallas kernels for 26%

profile of v1, /device:TPU:0, one launch (start us, length us, event | category | flops | bytes accessed | tf_op | source)
XLA Modules:
  0.0 309.8 jit_solution(15621630245025548630)
XLA Ops:
  0.7 1.3 constant_dynamic-slice_fusion.7
  2.0 3.0 collective-permute-start
  5.0 13.3 %collective-permute-done = bf16[3,128,768]{2,1,0:T(8,128)(2,1)S(1)} collective-permute-done((bf16[3,128,768]{2,1,0:T(8,128)(2,1)S(1)}, bf16[3,128,768]{2,1,0:T(8,128)(2,1)S(1)}, u32[]{:S(2)}, u32[]{:S(2)}) %collective-permute-start) | collective-permute-done | bytes 589856 | tf_op jit(solution)/shard_map/ppermute | solution.py:433
  18.5 1.5 copy-done.17
  20.2 1.8 collective-permute-start.3
  22.6 1.3 reshape.121.bq
  23.8 1.3 reshape.122.bv
  25.1 0.7 fusion.13
  26.4 1.2 copy.39.seg_col
  28.3 1.0 copy-done.13
  29.3 17.0 %attend.1 = (bf16[3,512,384]{2,1,0:T(8,128)(2,1)}, bf16[3,512,384]{2,1,0:T(8,128)(2,1)}, bf16[3,512,384]{2,1,0:T(8,128)(2,1)}, bf16[3,6,512,512]{3,2,1,0:T(8,128...) custom-call(s32[9]{0:T(128)} %stack.39.where, ...), custom_call_target="tpu_custom_call" | custom-call | tf_op jit(solution)/shard_map/attend/pallas_call | solution.py:76
  50.5 2.2 pad_maximum_fusion.1.cot
  53.8 40.3 %middle.1 = (bf16[3,256,768]{2,1,0:T(8,128)(2,1)}, bf16[3,256,3072]{2,1,0:T(8,128)(2,1)}, bf16[3,256,3072]{2,1,0:T(8,128)(2,1)}, bf16[768,768]{1,0:T(8,128)(2,1)...) custom-call(s32[9]{0:T(128)} %stack.39.where, ...), custom_call_target="tpu_custom_call" | custom-call | tf_op jit(solution)/shard_map/middle/pallas_call | solution.py:207
  94.1 1.3 copy-done.4
  95.4 3.2 %rows_grad.2 = (bf16[8,96,384]{2,1,0:T(8,128)(2,1)S(1)}, bf16[8,96,384]{2,1,0:T(8,128)(2,1)}) custom-call(s32[9]{0:T(128)S(1)} %copy-done.9, bf16[768,768]{1,0:T(8,128)(2,1)S(1)} %fusion.left, bf16[768,768]{1,0:T(8,128)(2,1)S(1)} %bitcast.40), custom_call_target="tpu_custom_call" | custom-call | tf_op jit(solution)/shard_map/rows_grad/pallas_call | solution.py:363
  98.7 0.8 copy-done.7
  100.0 0.7 reshape.133
  104.0 10.8 %cols_grad.1 = (bf16[8,384,384]{2,1,0:T(8,128)(2,1)S(1)}, bf16[8,384,384]{2,1,0:T(8,128)(2,1)}) custom-call(s32[9]{0:T(128)S(1)} %copy-done.9, bf16[768,768]{1,0:T(8,128)(2,1)S(1)} %copy-done.6, bf16[768,3072]{1,0:T(8,128)(2,1)} %bitcast.43), custom_call_target="tpu_custom_call" | custom-call | tf_op jit(solution)/shard_map/cols_grad/pallas_call | solution.py:405
  115.3 1.2 add_convert_fusion.8
  116.5 0.7 slice.204
  117.3 1.5 collective-permute-start.14
  118.8 42.5 %attend_back.1 = (f32[3,256,768]{2,1,0:T(8,128)}, bf16[3,256,768]{2,1,0:T(8,128)(2,1)}, bf16[8,96,384]{2,1,0:T(8,128)(2,1)}, bf16[8,96,384]{2,1,0:T(8,128)(2,1)}...) custom-call(s32[9]{0:T(128)} %stack.39.where, bf16[3,256,768]{2,1,0:T(8,128)(2,1)} %copy-done.11, ...), custom_call_target="tpu_custom_call" | custom-call | tf_op jit(solution)/shard_map/attend_back/pallas_call | solution.py:313
  161.3 0.8 fusion.6
  162.7 1.5 rev.14
  164.2 2.0 constant_dynamic-update-slice_fusion.3
  166.4 0.9 constant_dynamic-update-slice_fusion.2
  167.3 0.7 copy.40
  168.0 1.6 reshape_reshape.3
  169.6 1.0 constant_dynamic-update-slice_fusion.1
  170.6 0.7 constant_dynamic-update-slice_fusion
  171.2 2.2 slice.187
  174.0 9.1 %rows_grad.3 = (bf16[8,96,1536]{2,1,0:T(8,128)(2,1)S(1)}, bf16[8,96,1536]{2,1,0:T(8,128)(2,1)}) custom-call(s32[9]{0:T(128)S(1)} %copy-done.10, bf16[768,768]{1,0:T(8,128)(2,1)S(1)} %copy-done.5, bf16[768,3072]{1,0:T(8,128)(2,1)} %bitcast.42), custom_call_target="tpu_custom_call" | custom-call | tf_op jit(solution)/shard_map/rows_grad/pallas_call | solution.py:363
  183.1 1.4 copy-done.2
  184.5 1.1 add_convert_fusion.14
  185.7 1.6 collective-permute-start.15
  188.0 4.0 %collective-permute-done.15 = bf16[2,96,384]{2,1,0:T(8,128)(2,1)S(1)} collective-permute-done((bf16[2,96,384]{2,1,0:T(8,128)(2,1)S(1)}, bf16[2,96,384]{2,1,0:T(8,128)(2,1)S(1)}, u32[]{:S(2)}, u32[]{:S(2)}) %collective-permute-start.15) | collective-permute-done | bytes 147488 | tf_op jit(solution)/shard_map/ppermute | solution.py:433
  192.1 4.1 %collective-permute-done.8 = bf16[4,304,384]{2,1,0:T(8,128)(2,1)} collective-permute-done((bf16[4,304,384]{2,1,0:T(8,128)(2,1)}, bf16[4,304,384]{2,1,0:T(8,128)(2,1)}, u32[]{:S(2)}, u32[]{:S(2)}) %collective-permute-start.8) | collective-permute-done | bytes 933920 | tf_op jit(solution)/shard_map/ppermute | solution.py:433
  196.1 2.6 collective-permute-start.16
  198.7 1.7 add_convert_fusion.5
  200.5 0.9 collective-permute-done.16
  201.4 1.6 collective-permute-start.9
  203.6 1.2 maximum_select_fusion
  204.8 2.6 collective-permute-done.17
  207.5 4.2 %collective-permute-done.9 = bf16[2,304,384]{2,1,0:T(8,128)(2,1)S(1)} collective-permute-done((bf16[2,304,384]{2,1,0:T(8,128)(2,1)S(1)}, bf16[2,304,384]{2,1,0:T(8,128)(2,1)S(1)}, u32[]{:S(2)}, u32[]{:S(2)}) %collective-permute-start.9) | collective-permute-done | bytes 466976 | tf_op jit(solution)/shard_map/ppermute | solution.py:433
  211.9 3.4 %collective-permute-start.10 = (bf16[1,304,384]{2,1,0:T(8,128)(2,1)S(1)}, bf16[1,304,384]{2,1,0:T(8,128)(2,1)S(1)}, u32[]{:S(2)}, u32[]{:S(2)}) collective-permute-start(bf16[1,304,384]{2,1,0:T(8,128)(2,1)S(1)} %slice.191), channel_id=1, source_target_pairs={{0,16},{4,20},{8,24},{12,28},{16,0},{20,4},{24,8},{28,12},{1,17},{... | collective-permute-start | bytes 700424 | tf_op jit(solution)/shard_map/ppermute | solution.py:433
  215.3 2.2 add_convert_fusion
  218.3 0.9 copy-done.3
  219.3 2.4 add_convert_fusion.1
  222.5 0.9 copy-done.15
  224.7 1.6 collective-permute-start.7
  226.3 6.5 %collective-permute-done.11 = bf16[304,384]{1,0:T(8,128)(2,1)S(1)} collective-permute-done((bf16[304,384]{1,0:T(8,128)(2,1)S(1)}, bf16[304,384]{1,0:T(8,128)(2,1)S(1)}, u32[]{:S(2)}, u32[]{:S(2)}) %collective-permute-start.11) | collective-permute-done | bytes 233504 | tf_op jit(solution)/shard_map/ppermute | solution.py:433
  232.9 13.8 %collective-permute-done.26 = bf16[4,384,384]{2,1,0:T(8,128)(2,1)S(1)} collective-permute-done((bf16[4,384,384]{2,1,0:T(8,128)(2,1)S(1)}, bf16[4,384,384]{2,1,0:T(8,128)(2,1)S(1)}, u32[]{:S(2)}, u32[]{:S(2)}) %collective-permute-start.26) | collective-permute-done | bytes 1179680 | tf_op jit(solution)/shard_map/ppermute | solution.py:433
  247.1 1.5 collective-permute-start.27
  248.5 18.9 %collective-permute-done.20 = bf16[4,96,1536]{2,1,0:T(8,128)(2,1)S(1)} collective-permute-done((bf16[4,96,1536]{2,1,0:T(8,128)(2,1)S(1)}, bf16[4,96,1536]{2,1,0:T(8,128)(2,1)S(1)}, u32[]{:S(2)}, u32[]{:S(2)}) %collective-permute-start.20) | collective-permute-done | bytes 1179680 | tf_op jit(solution)/shard_map/ppermute | solution.py:433
  267.7 1.5 collective-permute-start.21
  269.3 0.7 fusion.3
  270.0 1.2 maximum_select_fusion.1
  272.0 13.0 %collective-permute-done.21 = bf16[2,96,1536]{2,1,0:T(8,128)(2,1)S(1)} collective-permute-done((bf16[2,96,1536]{2,1,0:T(8,128)(2,1)S(1)}, bf16[2,96,1536]{2,1,0:T(8,128)(2,1)S(1)}, u32[]{:S(2)}, u32[]{:S(2)}) %collective-permute-start.21) | collective-permute-done | bytes 589856 | tf_op jit(solution)/shard_map/ppermute | solution.py:433
  285.3 0.9 fusion.16
  286.2 0.9 collective-permute-done.28
  287.8 9.8 %collective-permute-done.22 = bf16[1,96,1536]{2,1,0:T(8,128)(2,1)S(1)} collective-permute-done((bf16[1,96,1536]{2,1,0:T(8,128)(2,1)S(1)}, bf16[1,96,1536]{2,1,0:T(8,128)(2,1)S(1)}, u32[]{:S(2)}, u32[]{:S(2)}) %collective-permute-start.22) | collective-permute-done | bytes 294944 | tf_op jit(solution)/shard_map/ppermute | solution.py:433
  299.0 6.9 %collective-permute-done.23 = bf16[96,1536]{1,0:T(8,128)(2,1)S(1)} collective-permute-done((bf16[96,1536]{1,0:T(8,128)(2,1)S(1)}, bf16[96,1536]{1,0:T(8,128)(2,1)S(1)}, u32[]{:S(2)}, u32[]{:S(2)}) %collective-permute-start.23) | collective-permute-done | bytes 294944 | tf_op jit(solution)/shard_map/ppermute | solution.py:433
  306.8 1.4 copy.45
  308.2 1.2 fusion.1
  (192 shorter events, 22.0 us)
Async XLA Ops:
  0.7 21.3 %copy-start = (s32[6,512]{1,0:T(8,128)S(1)}, s32[6,512]{1,0:T(8,128)}, u32[]{:S(2)}) copy-start(s32[6,512]{1,0:T(8,128)} %param.19) | copy-start | bytes 36868
  2.0 16.4 %collective-permute-start = (bf16[3,128,768]{2,1,0:T(8,128)(2,1)S(1)}, bf16[3,128,768]{2,1,0:T(8,128)(2,1)S(1)}, u32[]{:S(2)}, u32[]{:S(2)}) collective-permute-start(bf16[3,128,768]{2,1,0:T(8,128)(2,1)S(1)} %get-tuple-element.130), channel_id=1, source_target_pairs={{0,2},{1,3},{2,0},{3,1},{4,6},{5,7},{6,4},{7,5},{8,10},{9,11},{10,... | collective-permute-start | bytes 1769480 | tf_op jit(solution)/shard_map/ppermute | solution.py:433
  18.5 9.8 %collective-permute-start.1 = (bf16[3,256,768]{2,1,0:T(8,128)(2,1)S(1)}, bf16[3,256,768]{2,1,0:T(8,128)(2,1)S(1)}, u32[]{:S(2)}, u32[]{:S(2)}) collective-permute-start(bf16[3,256,768]{2,1,0:T(8,128)(2,1)S(1)} %pad_maximum_fusion.own), channel_id=1, source_target_pairs={{0,1},{1,0},{2,3},{3,2},{4,5},{5,4},{6,7},{7,6},{8,9},{9,8},{10,11... | collective-permute-start | bytes 3538952 | tf_op jit(solution)/shard_map/ppermute | solution.py:433
  20.2 30.4 %collective-permute-start.3 = (bf16[3,128,768]{2,1,0:T(8,128)(2,1)S(1)}, bf16[3,128,768]{2,1,0:T(8,128)(2,1)}, u32[]{:S(2)}, u32[]{:S(2)}) collective-permute-start(bf16[3,128,768]{2,1,0:T(8,128)(2,1)S(1)} %get-tuple-element.128), channel_id=1, source_target_pairs={{0,2},{1,3},{2,0},{3,1},{4,6},{5,7},{6,4},{7,5},{8,10},{9,11},{10,... | collective-permute-start | bytes 1769480 | tf_op jit(solution)/shard_map/ppermute | solution.py:433
  28.3 18.1 %copy-start.37 = (bf16[768]{0:T(1024)(128)(2,1)S(1)}, bf16[768]{0:T(1024)(128)(2,1)}, u32[]{:S(2)}) copy-start(bf16[768]{0:T(1024)(128)(2,1)} %param.26) | copy-start | bytes 4612
  28.3 18.7 %copy-start.38 = (bf16[768]{0:T(1024)(128)(2,1)S(1)}, bf16[768]{0:T(1024)(128)(2,1)}, u32[]{:S(2)}) copy-start(bf16[768]{0:T(1024)(128)(2,1)} %param.27) | copy-start | bytes 4612
  28.3 21.6 %copy-start.30 = (bf16[3072]{0:T(1024)(128)(2,1)S(1)}, bf16[3072]{0:T(1024)(128)(2,1)}, u32[]{:S(2)}) copy-start(bf16[3072]{0:T(1024)(128)(2,1)} %param.30) | copy-start | bytes 18436
  29.3 18.2 %copy-start.39 = (bf16[768]{0:T(1024)(128)(2,1)S(1)}, bf16[768]{0:T(1024)(128)(2,1)}, u32[]{:S(2)}) copy-start(bf16[768]{0:T(1024)(128)(2,1)} %param.28) | copy-start | bytes 4612
  29.3 18.8 %copy-start.40 = (bf16[768]{0:T(1024)(128)(2,1)S(1)}, bf16[768]{0:T(1024)(128)(2,1)}, u32[]{:S(2)}) copy-start(bf16[768]{0:T(1024)(128)(2,1)} %param.32) | copy-start | bytes 4612
  29.3 19.4 %copy-start.41 = (bf16[768]{0:T(1024)(128)(2,1)S(1)}, bf16[768]{0:T(1024)(128)(2,1)}, u32[]{:S(2)}) copy-start(bf16[768]{0:T(1024)(128)(2,1)} %param.33) | copy-start | bytes 4612
  29.3 20.0 %copy-start.42 = (bf16[768]{0:T(1024)(128)(2,1)S(1)}, bf16[768]{0:T(1024)(128)(2,1)}, u32[]{:S(2)}) copy-start(bf16[768]{0:T(1024)(128)(2,1)} %param.34) | copy-start | bytes 4612
  46.3 6.7 %collective-permute-start.2 = (bf16[3,256,384]{2,1,0:T(8,128)(2,1)}, bf16[3,256,384]{2,1,0:T(8,128)(2,1)S(1)}, u32[]{:S(2)}, u32[]{:S(2)}) collective-permute-start(bf16[3,256,384]{2,1,0:T(8,128)(2,1)} %get-tuple-element.54.mix_sib), channel_id=1, source_target_pairs={{0,1},{1,0},{2,3},{3,2},{4,5},{5,4},{6,7},{7,6},{8,9},{9,8},{10,11... | collective-permute-start | bytes 1769480 | tf_op jit(solution)/shard_map/ppermute | solution.py:433
  53.8 40.3 %copy-start.9 = (s32[9]{0:T(128)S(1)}, s32[9]{0:T(128)}, u32[]{:S(2)}) copy-start(s32[9]{0:T(128)} %stack.39.where) | copy-start | bytes 112
  95.4 4.6 %copy-start.35 = (f32[1,768]{1,0:T(1,128)S(1)}, f32[1,768]{1,0:T(1,128)}, u32[]{:S(2)}) copy-start(f32[1,768]{1,0:T(1,128)} %get-tuple-element.71) | copy-start | bytes 9220
  95.4 4.6 %copy-start.36 = (f32[1,768]{1,0:T(1,128)S(1)}, f32[1,768]{1,0:T(1,128)}, u32[]{:S(2)}) copy-start(f32[1,768]{1,0:T(1,128)} %get-tuple-element.72) | copy-start | bytes 9220
  95.4 6.0 %copy-start.33 = (f32[1,768]{1,0:T(1,128)S(1)}, f32[1,768]{1,0:T(1,128)}, u32[]{:S(2)}) copy-start(f32[1,768]{1,0:T(1,128)} %get-tuple-element.75) | copy-start | bytes 9220
  95.4 6.0 %copy-start.34 = (f32[1,768]{1,0:T(1,128)S(1)}, f32[1,768]{1,0:T(1,128)}, u32[]{:S(2)}) copy-start(f32[1,768]{1,0:T(1,128)} %get-tuple-element.73) | copy-start | bytes 9220
  95.4 7.3 %copy-start.31 = (f32[1,768]{1,0:T(1,128)S(1)}, f32[1,768]{1,0:T(1,128)}, u32[]{:S(2)}) copy-start(f32[1,768]{1,0:T(1,128)} %get-tuple-element.76) | copy-start | bytes 9220
  95.4 7.3 %copy-start.32 = (f32[1,768]{1,0:T(1,128)S(1)}, f32[1,768]{1,0:T(1,128)}, u32[]{:S(2)}) copy-start(f32[1,768]{1,0:T(1,128)} %get-tuple-element.77) | copy-start | bytes 9220
  95.4 8.5 %copy-start.23 = (f32[1,3072]{1,0:T(1,128)S(1)}, f32[1,3072]{1,0:T(1,128)}, u32[]{:S(2)}) copy-start(f32[1,3072]{1,0:T(1,128)} %get-tuple-element.74) | copy-start | bytes 36868
  95.4 8.6 %copy-start.6 = (bf16[768,768]{1,0:T(8,128)(2,1)S(1)}, bf16[768,768]{1,0:T(8,128)(2,1)}, u32[]{:S(2)}) copy-start(bf16[768,768]{1,0:T(8,128)(2,1)} %get-tuple-element.85.left) | copy-start | bytes 3538948
  99.5 15.8 %collective-permute-start.13 = (bf16[8,96,384]{2,1,0:T(8,128)(2,1)}, bf16[8,96,384]{2,1,0:T(8,128)(2,1)}, u32[]{:S(2)}, u32[]{:S(2)}) collective-permute-start(bf16[8,96,384]{2,1,0:T(8,128)(2,1)} %get-tuple-element.80), channel_id=1, source_target_pairs={{0,1},{1,0},{2,3},{3,2},{4,5},{5,4},{6,7},{7,6},{8,9},{9,8},{10,11... | collective-permute-start | bytes 1769480 | tf_op jit(solution)/shard_map/ppermute | solution.py:433
  101.3 17.5 %collective-permute-start.5 = (bf16[3,256,384]{2,1,0:T(8,128)(2,1)}, bf16[3,256,384]{2,1,0:T(8,128)(2,1)}, u32[]{:S(2)}, u32[]{:S(2)}) collective-permute-start(bf16[3,256,384]{2,1,0:T(8,128)(2,1)} %get-tuple-element.63), channel_id=1, source_target_pairs={{0,1},{1,0},{2,3},{3,2},{4,5},{5,4},{6,7},{7,6},{8,9},{9,8},{10,11... | collective-permute-start | bytes 1769480 | tf_op jit(solution)/shard_map/ppermute | solution.py:433
  104.0 11.3 %copy-start.8 = (bf16[8,96,384]{2,1,0:T(8,128)(2,1)S(1)}, bf16[8,96,384]{2,1,0:T(8,128)(2,1)}, u32[]{:S(2)}) copy-start(bf16[8,96,384]{2,1,0:T(8,128)(2,1)} %copy-done.7) | copy-start | bytes 1769476
  114.8 100.5 %collective-permute-start.25 = (bf16[8,384,384]{2,1,0:T(8,128)(2,1)}, bf16[8,384,384]{2,1,0:T(8,128)(2,1)}, u32[]{:S(2)}, u32[]{:S(2)}) collective-permute-start(bf16[8,384,384]{2,1,0:T(8,128)(2,1)} %get-tuple-element.88), channel_id=1, source_target_pairs={{0,1},{1,0},{2,3},{3,2},{4,5},{5,4},{6,7},{7,6},{8,9},{9,8},{10,11... | collective-permute-start | bytes 7077896 | tf_op jit(solution)/shard_map/ppermute | solution.py:433
  117.3 67.2 %collective-permute-start.14 = (bf16[4,96,384]{2,1,0:T(8,128)(2,1)}, bf16[4,96,384]{2,1,0:T(8,128)(2,1)}, u32[]{:S(2)}, u32[]{:S(2)}) collective-permute-start(bf16[4,96,384]{2,1,0:T(8,128)(2,1)} %slice.204), channel_id=1, source_target_pairs={{0,4},{4,0},{8,12},{12,8},{16,20},{20,16},{24,28},{28,24},{1,5},{5... | collective-permute-start | bytes 884744 | tf_op jit(solution)/shard_map/ppermute | solution.py:433
  118.8 43.5 %copy-start.24 = (bf16[8,96]{1,0:T(8,128)(2,1)S(1)}, bf16[8,96]{1,0:T(8,128)(2,1)}, u32[]{:S(2)}) copy-start(bf16[8,96]{1,0:T(8,128)(2,1)} %reshape.133) | copy-start | bytes 4612
  118.8 43.5 %copy-start.25 = (bf16[8,96]{1,0:T(8,128)(2,1)S(1)}, bf16[8,96]{1,0:T(8,128)(2,1)}, u32[]{:S(2)}) copy-start(bf16[8,96]{1,0:T(8,128)(2,1)} %reshape.132) | copy-start | bytes 4612
  118.8 43.5 %copy-start.26 = (bf16[8,96]{1,0:T(8,128)(2,1)S(1)}, bf16[8,96]{1,0:T(8,128)(2,1)}, u32[]{:S(2)}) copy-start(bf16[8,96]{1,0:T(8,128)(2,1)} %reshape.136) | copy-start | bytes 4612
  118.8 43.5 %copy-start.27 = (bf16[8,96]{1,0:T(8,128)(2,1)S(1)}, bf16[8,96]{1,0:T(8,128)(2,1)}, u32[]{:S(2)}) copy-start(bf16[8,96]{1,0:T(8,128)(2,1)} %reshape.134) | copy-start | bytes 4612
  118.8 43.5 %copy-start.28 = (bf16[8,96]{1,0:T(8,128)(2,1)S(1)}, bf16[8,96]{1,0:T(8,128)(2,1)}, u32[]{:S(2)}) copy-start(bf16[8,96]{1,0:T(8,128)(2,1)} %reshape.138) | copy-start | bytes 4612
  118.8 43.5 %copy-start.29 = (bf16[8,96]{1,0:T(8,128)(2,1)S(1)}, bf16[8,96]{1,0:T(8,128)(2,1)}, u32[]{:S(2)}) copy-start(bf16[8,96]{1,0:T(8,128)(2,1)} %reshape.137) | copy-start | bytes 4612
  166.3 3.3 %copy-start.19 = (bf16[8,96,384]{2,1,0:T(8,128)(2,1)S(1)}, bf16[8,96,384]{2,1,0:T(8,128)(2,1)}, u32[]{:S(2)}) copy-start(bf16[8,96,384]{2,1,0:T(8,128)(2,1)} %get-tuple-element.68) | copy-start | bytes 1769476
  170.6 3.4 %copy-start.5 = (bf16[768,768]{1,0:T(8,128)(2,1)S(1)}, bf16[768,768]{1,0:T(8,128)(2,1)}, u32[]{:S(2)}) copy-start(bf16[768,768]{1,0:T(8,128)(2,1)} %get-tuple-element.81.left) | copy-start | bytes 3538948
  170.6 3.4 %copy-start.10 = (s32[9]{0:T(128)S(1)}, s32[9]{0:T(128)}, u32[]{:S(2)}) copy-start(s32[9]{0:T(128)} %stack.39.where) | copy-start | bytes 112
  173.4 22.7 %collective-permute-start.8 = (bf16[4,304,384]{2,1,0:T(8,128)(2,1)}, bf16[4,304,384]{2,1,0:T(8,128)(2,1)}, u32[]{:S(2)}, u32[]{:S(2)}) collective-permute-start(bf16[4,304,384]{2,1,0:T(8,128)(2,1)} %slice.187), channel_id=1, source_target_pairs={{0,4},{4,0},{8,12},{12,8},{16,20},{20,16},{24,28},{28,24},{1,5},{5... | collective-permute-start | bytes 2801672 | tf_op jit(solution)/shard_map/ppermute | solution.py:433
  184.5 33.8 %collective-permute-start.19 = (bf16[8,96,1536]{2,1,0:T(8,128)(2,1)}, bf16[8,96,1536]{2,1,0:T(8,128)(2,1)}, u32[]{:S(2)}, u32[]{:S(2)}) collective-permute-start(bf16[8,96,1536]{2,1,0:T(8,128)(2,1)} %get-tuple-element.84), channel_id=1, source_target_pairs={{0,1},{1,0},{2,3},{3,2},{4,5},{5,4},{6,7},{7,6},{8,9},{9,8},{10,11... | collective-permute-start | bytes 7077896 | tf_op jit(solution)/shard_map/ppermute | solution.py:433
  184.5 2.8 copy-start.18
  185.7 6.3 %collective-permute-start.15 = (bf16[2,96,384]{2,1,0:T(8,128)(2,1)S(1)}, bf16[2,96,384]{2,1,0:T(8,128)(2,1)S(1)}, u32[]{:S(2)}, u32[]{:S(2)}) collective-permute-start(bf16[2,96,384]{2,1,0:T(8,128)(2,1)S(1)} %slice.206), channel_id=1, source_target_pairs={{0,8},{4,12},{8,0},{12,4},{16,24},{20,28},{24,16},{28,20},{1,9},{5... | collective-permute-start | bytes 442376 | tf_op jit(solution)/shard_map/ppermute | solution.py:433
  187.3 4.7 %copy-start.43 = (bf16[3,256,768]{2,1,0:T(8,128)(2,1)S(1)}, bf16[3,256,768]{2,1,0:T(8,128)(2,1)}, u32[]{:S(2)}) copy-start(bf16[3,256,768]{2,1,0:T(8,128)(2,1)} %get-tuple-element.65) | copy-start | bytes 3538948
  187.4 15.6 %collective-permute-start.4 = (bf16[3,128,768]{2,1,0:T(8,128)(2,1)S(1)}, bf16[3,128,768]{2,1,0:T(8,128)(2,1)S(1)}, u32[]{:S(2)}, u32[]{:S(2)}) collective-permute-start(bf16[3,128,768]{2,1,0:T(8,128)(2,1)S(1)} %get-tuple-element.126), channel_id=1, source_target_pairs={{0,2},{1,3},{2,0},{3,1},{4,6},{5,7},{6,4},{7,5},{8,10},{9,11},{10,... | collective-permute-start | bytes 1769480 | tf_op jit(solution)/shard_map/ppermute | solution.py:433
  192.0 30.5 %collective-permute-start.6 = (bf16[3,256,768]{2,1,0:T(8,128)(2,1)S(1)}, bf16[3,256,768]{2,1,0:T(8,128)(2,1)S(1)}, u32[]{:S(2)}, u32[]{:S(2)}) collective-permute-start(bf16[3,256,768]{2,1,0:T(8,128)(2,1)S(1)} %copy-done.43), channel_id=1, source_target_pairs={{0,1},{1,0},{2,3},{3,2},{4,5},{5,4},{6,7},{7,6},{8,9},{9,8},{10,11... | collective-permute-start | bytes 3538952 | tf_op jit(solution)/shard_map/ppermute | solution.py:433
  196.1 5.3 %collective-permute-start.16 = (bf16[1,96,384]{2,1,0:T(8,128)(2,1)S(1)}, bf16[1,96,384]{2,1,0:T(8,128)(2,1)S(1)}, u32[]{:S(2)}, u32[]{:S(2)}) collective-permute-start(bf16[1,96,384]{2,1,0:T(8,128)(2,1)S(1)} %slice.208), channel_id=1, source_target_pairs={{0,16},{4,20},{8,24},{12,28},{16,0},{20,4},{24,8},{28,12},{1,17},{... | collective-permute-start | bytes 221192 | tf_op jit(solution)/shard_map/ppermute | solution.py:433
  201.4 10.4 %collective-permute-start.9 = (bf16[2,304,384]{2,1,0:T(8,128)(2,1)S(1)}, bf16[2,304,384]{2,1,0:T(8,128)(2,1)S(1)}, u32[]{:S(2)}, u32[]{:S(2)}) collective-permute-start(bf16[2,304,384]{2,1,0:T(8,128)(2,1)S(1)} %slice.189), channel_id=1, source_target_pairs={{0,8},{4,12},{8,0},{12,4},{16,24},{20,28},{24,16},{28,20},{1,9},{5... | collective-permute-start | bytes 1400840 | tf_op jit(solution)/shard_map/ppermute | solution.py:433
  203.0 4.4 %collective-permute-start.17 = (bf16[96,384]{1,0:T(8,128)(2,1)S(1)}, bf16[96,384]{1,0:T(8,128)(2,1)S(1)}, u32[]{:S(2)}, u32[]{:S(2)}) collective-permute-start(bf16[96,384]{1,0:T(8,128)(2,1)S(1)} %bitcast.48), channel_id=1, source_target_pairs={{0,2},{1,3},{2,0},{3,1},{4,6},{5,7},{6,4},{7,5},{8,10},{9,11},{10,... | collective-permute-start | bytes 221192 | tf_op jit(solution)/shard_map/ppermute | solution.py:433
  207.4 61.8 %collective-permute-start.18 = (bf16[96,384]{1,0:T(8,128)(2,1)S(1)}, bf16[96,384]{1,0:T(8,128)(2,1)S(1)}, u32[]{:S(2)}, u32[]{:S(2)}) collective-permute-start(bf16[96,384]{1,0:T(8,128)(2,1)S(1)} %add_convert_fusion.18), channel_id=1, source_target_pairs={{0,1},{1,0},{2,3},{3,2},{4,5},{5,4},{6,7},{7,6},{8,9},{9,8},{10,11... | collective-permute-start | bytes 221192 | tf_op jit(solution)/shard_map/ppermute | solution.py:433
  211.9 12.1 %collective-permute-start.10 = (bf16[1,304,384]{2,1,0:T(8,128)(2,1)S(1)}, bf16[1,304,384]{2,1,0:T(8,128)(2,1)S(1)}, u32[]{:S(2)}, u32[]{:S(2)}) collective-permute-start(bf16[1,304,384]{2,1,0:T(8,128)(2,1)S(1)} %slice.191), channel_id=1, source_target_pairs={{0,16},{4,20},{8,24},{12,28},{16,0},{20,4},{24,8},{28,12},{1,17},{... | collective-permute-start | bytes 700424 | tf_op jit(solution)/shard_map/ppermute | solution.py:433
  217.7 29.0 %collective-permute-start.26 = (bf16[4,384,384]{2,1,0:T(8,128)(2,1)S(1)}, bf16[4,384,384]{2,1,0:T(8,128)(2,1)S(1)}, u32[]{:S(2)}, u32[]{:S(2)}) collective-permute-start(bf16[4,384,384]{2,1,0:T(8,128)(2,1)S(1)} %slice.220), channel_id=1, source_target_pairs={{0,4},{4,0},{8,12},{12,8},{16,20},{20,16},{24,28},{28,24},{1,5},{5... | collective-permute-start | bytes 3538952 | tf_op jit(solution)/shard_map/ppermute | solution.py:433
  219.3 3.2 %copy-start.16 = (f32[3,256,768]{2,1,0:T(8,128)S(1)}, f32[3,256,768]{2,1,0:T(8,128)}, u32[]{:S(2)}) copy-start(f32[3,256,768]{2,1,0:T(8,128)} %get-tuple-element.64) | copy-start | bytes 7077892
  221.8 45.6 %collective-permute-start.20 = (bf16[4,96,1536]{2,1,0:T(8,128)(2,1)S(1)}, bf16[4,96,1536]{2,1,0:T(8,128)(2,1)S(1)}, u32[]{:S(2)}, u32[]{:S(2)}) collective-permute-start(bf16[4,96,1536]{2,1,0:T(8,128)(2,1)S(1)} %slice.213), channel_id=1, source_target_pairs={{0,4},{4,0},{8,12},{12,8},{16,20},{20,16},{24,28},{28,24},{1,5},{5... | collective-permute-start | bytes 3538952 | tf_op jit(solution)/shard_map/ppermute | solution.py:433
  224.0 8.7 %collective-permute-start.11 = (bf16[304,384]{1,0:T(8,128)(2,1)S(1)}, bf16[304,384]{1,0:T(8,128)(2,1)S(1)}, u32[]{:S(2)}, u32[]{:S(2)}) collective-permute-start(bf16[304,384]{1,0:T(8,128)(2,1)S(1)} %bitcast.47), channel_id=1, source_target_pairs={{0,2},{1,3},{2,0},{3,1},{4,6},{5,7},{6,4},{7,5},{8,10},{9,11},{10,... | collective-permute-start | bytes 700424 | tf_op jit(solution)/shard_map/ppermute | solution.py:433
  224.7 45.4 %collective-permute-start.7 = (bf16[3,128,768]{2,1,0:T(8,128)(2,1)S(1)}, bf16[3,128,768]{2,1,0:T(8,128)(2,1)S(1)}, u32[]{:S(2)}, u32[]{:S(2)}) collective-permute-start(bf16[3,128,768]{2,1,0:T(8,128)(2,1)S(1)} %get-tuple-element.124), channel_id=1, source_target_pairs={{0,2},{1,3},{2,0},{3,1},{4,6},{5,7},{6,4},{7,5},{8,10},{9,11},{10,... | collective-permute-start | bytes 1769480 | tf_op jit(solution)/shard_map/ppermute | solution.py:433
  232.8 38.5 %collective-permute-start.12 = (bf16[304,384]{1,0:T(8,128)(2,1)S(1)}, bf16[304,384]{1,0:T(8,128)(2,1)S(1)}, u32[]{:S(2)}, u32[]{:S(2)}) collective-permute-start(bf16[304,384]{1,0:T(8,128)(2,1)S(1)} %add_convert_fusion.15), channel_id=1, source_target_pairs={{0,1},{1,0},{2,3},{3,2},{4,5},{5,4},{6,7},{7,6},{8,9},{9,8},{10,11... | collective-permute-start | bytes 700424 | tf_op jit(solution)/shard_map/ppermute | solution.py:433
  247.1 24.4 %collective-permute-start.27 = (bf16[2,384,384]{2,1,0:T(8,128)(2,1)S(1)}, bf16[2,384,384]{2,1,0:T(8,128)(2,1)S(1)}, u32[]{:S(2)}, u32[]{:S(2)}) collective-permute-start(bf16[2,384,384]{2,1,0:T(8,128)(2,1)S(1)} %slice.222), channel_id=1, source_target_pairs={{0,8},{4,12},{8,0},{12,4},{16,24},{20,28},{24,16},{28,20},{1,9},{5... | collective-permute-start | bytes 1769480 | tf_op jit(solution)/shard_map/ppermute | solution.py:433
  267.7 17.3 %collective-permute-start.21 = (bf16[2,96,1536]{2,1,0:T(8,128)(2,1)S(1)}, bf16[2,96,1536]{2,1,0:T(8,128)(2,1)S(1)}, u32[]{:S(2)}, u32[]{:S(2)}) collective-permute-start(bf16[2,96,1536]{2,1,0:T(8,128)(2,1)S(1)} %slice.215), channel_id=1, source_target_pairs={{0,8},{4,12},{8,0},{12,4},{16,24},{20,28},{24,16},{28,20},{1,9},{5... | collective-permute-start | bytes 1769480 | tf_op jit(solution)/shard_map/ppermute | solution.py:433
  271.3 14.9 %copy-start.22 = (bf16[304,384]{1,0:T(8,128)(2,1)}, bf16[304,384]{1,0:T(8,128)(2,1)S(1)}, u32[]{:S(2)}) copy-start(bf16[304,384]{1,0:T(8,128)(2,1)S(1)} %collective-permute-done.12) | copy-start | bytes 700420
  271.6 15.5 %collective-permute-start.28 = (bf16[1,384,384]{2,1,0:T(8,128)(2,1)S(1)}, bf16[1,384,384]{2,1,0:T(8,128)(2,1)S(1)}, u32[]{:S(2)}, u32[]{:S(2)}) collective-permute-start(bf16[1,384,384]{2,1,0:T(8,128)(2,1)S(1)} %slice.224), channel_id=1, source_target_pairs={{0,16},{4,20},{8,24},{12,28},{16,0},{20,4},{24,8},{28,12},{1,17},{... | collective-permute-start | bytes 884744 | tf_op jit(solution)/shard_map/ppermute | solution.py:433
  285.2 12.4 %collective-permute-start.22 = (bf16[1,96,1536]{2,1,0:T(8,128)(2,1)S(1)}, bf16[1,96,1536]{2,1,0:T(8,128)(2,1)S(1)}, u32[]{:S(2)}, u32[]{:S(2)}) collective-permute-start(bf16[1,96,1536]{2,1,0:T(8,128)(2,1)S(1)} %slice.217), channel_id=1, source_target_pairs={{0,16},{4,20},{8,24},{12,28},{16,0},{20,4},{24,8},{28,12},{1,17},{... | collective-permute-start | bytes 884744 | tf_op jit(solution)/shard_map/ppermute | solution.py:433
  286.2 12.0 %slice-start = ((bf16[304,384]{1,0:T(8,128)(2,1)}), bf16[16,384]{1,0:T(8,128)(2,1)S(1)}, s32[]{:S(2)}) async-start(bf16[304,384]{1,0:T(8,128)(2,1)} %copy-done.22), calls=%async_computation | async-start | bytes 24576 | tf_op jit(solution)/shard_map/slice | solution.py:580
  287.2 11.6 %collective-permute-start.29 = (bf16[384,384]{1,0:T(8,128)(2,1)S(1)}, bf16[384,384]{1,0:T(8,128)(2,1)S(1)}, u32[]{:S(2)}, u32[]{:S(2)}) collective-permute-start(bf16[384,384]{1,0:T(8,128)(2,1)S(1)} %bitcast.45), channel_id=1, source_target_pairs={{0,2},{1,3},{2,0},{3,1},{4,6},{5,7},{6,4},{7,5},{8,10},{9,11},{10,... | collective-permute-start | bytes 884744 | tf_op jit(solution)/shard_map/ppermute | solution.py:433
  297.6 8.3 %collective-permute-start.23 = (bf16[96,1536]{1,0:T(8,128)(2,1)S(1)}, bf16[96,1536]{1,0:T(8,128)(2,1)S(1)}, u32[]{:S(2)}, u32[]{:S(2)}) collective-permute-start(bf16[96,1536]{1,0:T(8,128)(2,1)S(1)} %bitcast.46), channel_id=1, source_target_pairs={{0,2},{1,3},{2,0},{3,1},{4,6},{5,7},{6,4},{7,5},{8,10},{9,11},{10,... | collective-permute-start | bytes 884744 | tf_op jit(solution)/shard_map/ppermute | solution.py:433
  298.9 7.8 %collective-permute-start.30 = (bf16[384,384]{1,0:T(8,128)(2,1)S(1)}, bf16[384,384]{1,0:T(8,128)(2,1)S(1)}, u32[]{:S(2)}, u32[]{:S(2)}) collective-permute-start(bf16[384,384]{1,0:T(8,128)(2,1)S(1)} %add_convert_fusion.10), channel_id=1, source_target_pairs={{0,1},{1,0},{2,3},{3,2},{4,5},{5,4},{6,7},{7,6},{8,9},{9,8},{10,11... | collective-permute-start | bytes 884744 | tf_op jit(solution)/shard_map/ppermute | solution.py:433
  306.0 2.2 collective-permute-start.24
  306.8 2.6 copy-start.1
  (12 other events, 17.4 us)

commit v2 on v0

v2 whole, which is shorter than its diff:
```python
import functools

import jax
import jax.numpy as jnp
from jax import lax
from jax.experimental import pallas as pl
from jax.experimental.pallas import tpu as pltpu
from jax.sharding import PartitionSpec as P

HD = 64
EPSILON = 1e-12
NEGATIVE = -1e30
LOW = jnp.bfloat16
F32 = jnp.float32
LOG2E = 1.4426950408889634
MIB = 1024 * 1024
SDS = jax.ShapeDtypeStruct


def contract(a, b, left, right):
    return lax.dot_general(a, b, (((left,), (right,)), ((), ())), preferred_element_type=F32)


def call(kernel, where, inputs, after, *, grid, in_specs, out_specs, out_shape, us, name, scratch=(), reuse=()):
    count = len(inputs)
    extra = len(after) + len(reuse)

    def body(w, *refs):
        kernel(w, *refs[:count], *refs[count + extra :])

    return pl.pallas_call(
        body,
        grid_spec=pltpu.PrefetchScalarGridSpec(
            num_scalar_prefetch=1,
            grid=grid,
            in_specs=list(in_specs) + [pl.BlockSpec(memory_space=pl.ANY)] * extra,
            out_specs=list(out_specs),
            scratch_shapes=list(scratch),
        ),
        out_shape=list(out_shape),
        compiler_params=pltpu.CompilerParams(vmem_limit_bytes=60 * MIB),
        cost_estimate=pl.CostEstimate(flops=int(us * 1.1e9), bytes_accessed=0, transcendentals=0),
        input_output_aliases={1 + count + i: i for i in range(len(reuse))},
        name=name,
    )(where, *inputs, *reuse, *after)


def col_sum(v):
    return jnp.sum(v, axis=0, keepdims=True)


def as_column(v, rows):
    return jnp.broadcast_to(v[None, :], (rows, v.shape[0])).T


def attend_kernel(
    where, t0, t1, t2, t3, seg_row, seg_col, wq, wk, wv, bq, bv,
    q_out, k_out, v_out, e_out, inv_out, mix_own, mix_sib,
):
    x = jnp.concatenate([t0[0], t1[0], t2[0], t3[0]], axis=0)
    half = mix_own.shape[2]
    cols = mix_own.shape[1]
    core = where[0]
    own_part = lambda ref: jnp.where(core == 0, ref[:cols].astype(F32), ref[cols:].astype(F32))
    qb = as_column(own_part(bq), 128)[:, :1]
    vb = as_column(own_part(bv), 128)[:, :1]
    q = (contract(wq[...], x, 0, 1) + qb).astype(LOW)
    k = contract(wk[...], x, 0, 1).astype(LOW)
    v = (contract(wv[...], x, 0, 1) + vb).astype(LOW)
    q_out[0] = q
    k_out[0] = k
    v_out[0] = v
    bias = jnp.where(seg_col[0] == seg_row[0], 0.0, NEGATIVE)
    for h in range(q.shape[0] // HD):
        part = slice(h * HD, (h + 1) * HD)
        s = contract(k[part], q[part], 0, 0) + bias
        top = jnp.max(s, axis=0, keepdims=True)
        e = jnp.exp2((s - top) * (LOG2E * HD**-0.5))
        low = e.astype(LOW)
        inv = 1.0 / col_sum(e)
        e_out[0, h] = low
        inv_out[0, h : h + 1] = inv
        mixed = (contract(v[part], low, 1, 0) * inv).astype(LOW)
        mix_own[0, part] = mixed[:, :half]
        mix_sib[0, part] = mixed[:, half:]


def attend(where, toks, seg_row, seg_col, wq, wk, wv, bq, bv, after=()):
    rows, span, width = toks[0].shape
    length = 4 * span
    cols = width // 2
    heads = cols // HD
    row3 = lambda *s: pl.BlockSpec((1,) + s, lambda r, w: (r, 0, 0))
    weight = pl.BlockSpec((width, cols), lambda r, w: (0, w[0]))
    bias = pl.BlockSpec((width,), lambda r, w: (0,))
    return call(
        attend_kernel, where, (*toks, seg_row, seg_col, wq, wk, wv, bq, bv), after,
        grid=(rows,),
        in_specs=[row3(span, width)] * 4
        + [row3(1, length), row3(length, 1), weight, weight, weight, bias, bias],
        out_specs=[row3(cols, length)] * 3
        + [
            pl.BlockSpec((1, heads, length, length), lambda r, w: (r, 0, 0, 0)),
            row3(heads, length), row3(cols, length // 2), row3(cols, length // 2),
        ],
        out_shape=[SDS((rows, cols, length), LOW)] * 3
        + [
            SDS((rows, heads, length, length), LOW), SDS((rows, heads, length), F32),
            SDS((rows, cols, length // 2), LOW), SDS((rows, cols, length // 2), LOW),
        ],
        us=17,
        name="attend",
    )


def norm_parts(v):
    center = v - jnp.mean(v, axis=1, keepdims=True)
    spread = jnp.mean(center * center, axis=1, keepdims=True)
    scale = lax.rsqrt(spread + EPSILON)
    return center * scale, scale


def norm_back(dn, n, scale):
    return scale * (
        dn - jnp.mean(dn, axis=1, keepdims=True) - n * jnp.mean(dn * n, axis=1, keepdims=True)
    )


def fold(v):
    return jnp.sum(v.reshape(v.shape[0] // 8, 8, v.shape[1]), axis=0)


TALL = 128


class Puts:
    def __init__(self, sems):
        self.sems = sems
        self.copies = []

    def __call__(self, src, dst):
        copy = pltpu.make_async_copy(src, dst, self.sems.at[len(self.copies)])
        copy.start()
        self.copies.append(copy)

    def shard(self, where, base, s, src, row, rows, cols, dst):
        if dst.shape[1] == rows:
            at = pl.ds(pl.multiple_of(row, 16), rows)
            self(src.at[at, cols], dst.at[where[base + 2 * s]])
            return
        for k in range(2):
            at = pl.ds(pl.multiple_of(row + k * (rows // 2), 16), rows // 2)
            self(src.at[at, cols], dst.at[where[base + 2 * s + k]])

    def wait(self):
        for copy in self.copies:
            copy.wait()


def place(i, cells, span):
    per = span // TALL
    cell = i // per
    return cell // cells, cell % cells, pl.ds(pl.multiple_of((i % per) * TALL, TALL), TALL)


def forward_kernel(
    where, mix_own, mix_sib, bo, ag, ash, b1, b2, fg, fsh,
    x0_hbm, x1_hbm, c0_hbm, c1_hbm, wo_hbm, w1_hbm, w2_hbm,
    sums, out0, out1, slope_out, low_out, norm_out, scale_out, second_out, douter_out,
    keep0, send0, keep1, send1,
    wo, w1, w2, x, cot, result, act, slope, norm1, scale1, first_low, second, douter, bias1, partial,
    in_sem, out_sem, *, shards,
):
    core = where[0]
    rows, cells, span, width = x.shape
    block = cells * span
    half = width // 2
    hidden = w1.shape[1]
    chunks = 3
    step = hidden // chunks
    lines = rows * block // TALL
    vec = lambda ref: ref[...].astype(F32)[None, :]
    own_half = pl.ds(pl.multiple_of(core * half, half), half)
    sib_half = pl.ds(pl.multiple_of((1 - core) * half, half), half)
    loads = [
        pltpu.make_async_copy(wo_hbm, wo, in_sem.at[0]),
        pltpu.make_async_copy(x0_hbm, x.at[:, 0], in_sem.at[1]),
        pltpu.make_async_copy(x1_hbm, x.at[:, 1], in_sem.at[2]),
        pltpu.make_async_copy(c0_hbm, cot.at[:, 0], in_sem.at[3]),
        pltpu.make_async_copy(c1_hbm, cot.at[:, 1], in_sem.at[4]),
    ]
    for j in range(chunks):
        cols = slice(j * step, (j + 1) * step)
        loads.append(pltpu.make_async_copy(w1_hbm.at[:, cols], w1.at[:, cols], in_sem.at[5 + j]))
    loads.append(pltpu.make_async_copy(w2_hbm, w2, in_sem.at[5 + chunks]))
    for k in (0, 1, 2, 5, 6, 7, 8, 3, 4):
        loads[k].start()
    put = Puts(out_sem)
    bias1[...] = vec(b1)
    partial[...] = jnp.zeros_like(partial)
    loads[0].wait()
    for r in range(rows):
        at = slice(r * block, (r + 1) * block)
        second[at] = contract(mix_own[r], wo[own_half, :], 0, 0) + contract(mix_sib[r], wo[sib_half, :], 0, 0)
    loads[1].wait()
    loads[2].wait()

    def norm_first(i, _):
        at = pl.ds(pl.multiple_of(i * TALL, TALL), TALL)
        r, cell, line = place(i, cells, span)
        n1, s1 = norm_parts(x[r, cell, line].astype(F32) + (second[at] + vec(bo)))
        norm1[at] = n1
        scale1[at] = jnp.broadcast_to(s1, (TALL, 128))
        first = n1 * vec(ag) + vec(ash)
        first_low[at] = first.astype(LOW)
        second[at] = first + vec(b2)
        return 0

    lax.fori_loop(0, lines, norm_first, 0, unroll=lines)
    put(norm1, norm_out)
    put(scale1, scale_out)
    put(first_low, low_out)
    for j in range(chunks):
        cols = slice(j * step, (j + 1) * step)
        loads[5 + j].wait()
        inner = contract(first_low[...], w1[:, cols], 1, 0) + bias1[:, cols]
        big = 0.5 + 0.5 * lax.erf(inner * 0.7071067811865476)
        bell = jnp.exp2(inner * inner * (-0.5 * LOG2E)) * 0.3989422804014327
        act[:, cols] = (inner * big).astype(LOW)
        slope[:, cols] = (big + inner * bell).astype(LOW)
        put(slope.at[:, cols], slope_out.at[:, cols])
    loads[5 + chunks].wait()
    second[...] += contract(act[...], w2[...], 1, 0)
    loads[3].wait()
    loads[4].wait()

    def norm_second(i, _):
        at = pl.ds(pl.multiple_of(i * TALL, TALL), TALL)
        r, cell, line = place(i, cells, span)
        n2, s2 = norm_parts(second[at])
        result[r, cell, line] = (n2 * vec(fg) + vec(fsh)).astype(LOW)
        g = cot[r, cell, line].astype(F32)
        d_second = norm_back(g * vec(fg), n2, s2)
        second[at] = d_second
        d_outer = d_second.astype(LOW)
        douter[at] = d_outer
        partial[:, :width] += fold(d_outer.astype(F32))
        partial[:, width : 2 * width] += fold(g * n2)
        partial[:, 2 * width :] += fold(g)
        return 0

    lax.fori_loop(0, lines, norm_second, 0, unroll=lines)
    put(douter, douter_out)
    put(second, second_out)
    put(result.at[:, 0], out0)
    put(result.at[:, 1], out1)
    sums[...] = col_sum(partial[...])

    size = hidden // shards
    part = size // 4
    every = slice(0, width)
    for s in range(shards):
        for piece in range(8 // shards):
            high = hidden // 8
            at = slice(s * size + piece * high, s * size + (piece + 1) * high)
            w2[at, :] = contract(act[:, at], douter[...], 0, 0).astype(LOW)
        for k, (keep, send) in enumerate(((keep0, send0), (keep1, send1))):
            theirs = s * size + (1 - core) * (2 * part) + k * part
            mine = s * size + core * (2 * part) + k * part
            put.shard(where, 2 + 16 * k, s, w2, theirs, part, every, send)
            put.shard(where, 2 + 16 * k, s, w2, mine, part, every, keep)
    put.wait()


def entries(order, shards):
    if shards == 1:
        return 1
    return 2 * shards if order[-1] == "g" else shards


def forward(where, orders, shards, x0, x1, mix_own, mix_sib, c0, c1, wo, w1, w2, bo, ag, ash, b1, b2, fg, fsh, after=()):
    rows, span, width = x0.shape
    half = 2 * span
    hidden = w1.shape[1]
    tokens = rows * half
    whole = lambda v: pl.BlockSpec(v.shape, lambda i, w: (0,) * len(v.shape))
    anywhere = pl.BlockSpec(memory_space=pl.ANY)
    outs = [SDS((1, 3 * width), F32)]
    outs += [SDS((rows, span, width), LOW)] * 2 + [SDS((tokens, hidden), LOW), SDS((tokens, width), LOW)]
    outs += [SDS((tokens, width), F32), SDS((tokens, 128), F32), SDS((tokens, width), F32)]
    outs += [SDS((tokens, width), LOW)]
    for k in range(2):
        n = entries(orders[k], shards)
        outs += [SDS((n, hidden // 4 // n, width), LOW)] * 2
    small = (mix_own, mix_sib, bo, ag, ash, b1, b2, fg, fsh)
    low = lambda *s: pltpu.VMEM(s, LOW)
    wide = lambda *s: pltpu.VMEM(s, F32)
    return call(
        functools.partial(forward_kernel, shards=shards), where, small + (x0, x1, c0, c1, wo, w1, w2), after,
        grid=(1,),
        in_specs=[whole(v) for v in small] + [anywhere] * 7,
        out_specs=[whole(outs[0])] + [anywhere] * (len(outs) - 1),
        out_shape=outs,
        scratch=[
            low(width, width), low(width, hidden), low(hidden, width),
            low(rows, 2, span, width), low(rows, 2, span, width), low(rows, 2, span, width),
            low(tokens, hidden), low(tokens, hidden), wide(tokens, width), wide(tokens, 128),
            low(tokens, width), wide(tokens, width), low(tokens, width), wide(1, hidden), wide(8, 3 * width),
            pltpu.SemaphoreType.DMA((9,)), pltpu.SemaphoreType.DMA((10 + 8 * shards,)),
        ],
        us=27,
        name="forward",
    )


def inner_kernel(
    where, slope_hbm, low_hbm, douter_hbm, w2_hbm,
    sums, dinner_out, keep0, send0, keep1, send1,
    w2, grad, slope, dinner, first_low, douter, partial, in_sem, out_sem, *, shards,
):
    core = where[0]
    hidden, width = w2.shape
    chunks = 3
    step = hidden // chunks
    load_d = pltpu.make_async_copy(douter_hbm, douter, in_sem.at[0])
    load_d.start()
    load_j = []
    for j in range(chunks):
        cols = slice(j * step, (j + 1) * step)
        load_j.append(pltpu.make_async_copy(w2_hbm.at[cols, :], w2.at[cols, :], in_sem.at[1 + 2 * j]))
        load_j.append(pltpu.make_async_copy(slope_hbm.at[:, cols], slope.at[:, cols], in_sem.at[2 + 2 * j]))
        load_j[-2].start()
        load_j[-1].start()
    load_low = pltpu.make_async_copy(low_hbm, first_low, in_sem.at[7])
    load_low.start()
    put = Puts(out_sem)
    load_d.wait()
    for j in range(chunks):
        cols = slice(j * step, (j + 1) * step)
        load_j[2 * j].wait()
        load_j[2 * j + 1].wait()
        di = (contract(douter[...], w2[cols, :], 1, 1) * slope[:, cols].astype(F32)).astype(LOW)
        dinner[:, cols] = di
        partial[:, cols] = fold(di.astype(F32))
        put(dinner.at[:, cols], dinner_out.at[:, cols])
    sums[...] = col_sum(partial[...])
    load_low.wait()
    size = width // shards
    wide = hidden // 4
    for h in range(2):
        side = jnp.where(core == 0, 1 - h, h)
        for k in range(2):
            at = pl.ds(pl.multiple_of(side * (2 * wide) + k * wide, 128), wide)
            grad[:, at] = contract(first_low[...], dinner[:, at], 0, 0).astype(LOW)
            dst = ((send0, send1), (keep0, keep1))[h][k]
            for s in range(shards):
                put.shard(where, 2 + 16 * (2 + k), s, grad, s * size, size, at, dst)
    put.wait()


def inner_grad(where, orders, shards, slope, low_in, douter, w2, after=()):
    hidden, width = w2.shape
    tokens = douter.shape[0]
    whole = lambda v: pl.BlockSpec(v.shape, lambda i, w: (0,) * len(v.shape))
    anywhere = pl.BlockSpec(memory_space=pl.ANY)
    outs = [SDS((1, hidden), F32), SDS((tokens, hidden), LOW)]
    for k in (2, 3):
        n = entries(orders[k], shards)
        outs += [SDS((n, width // n, hidden // 4), LOW)] * 2
    low = lambda *s: pltpu.VMEM(s, LOW)
    return call(
        functools.partial(inner_kernel, shards=shards), where, (slope, low_in, douter, w2), after,
        grid=(1,),
        in_specs=[anywhere] * 4,
        out_specs=[whole(outs[0])] + [anywhere] * (len(outs) - 1),
        out_shape=outs,
        scratch=[
            low(hidden, width), low(width, hidden), low(tokens, hidden), low(tokens, hidden),
            low(tokens, width), low(tokens, width), pltpu.VMEM((8, hidden), F32),
            pltpu.SemaphoreType.DMA((8,)), pltpu.SemaphoreType.DMA((3 + 8 * shards,)),
        ],
        us=11,
        name="inner_grad",
    )


def branch_kernel(
    where, mix_own, mix_sib, ag, sums_outer, sums_inner, dinner_hbm, norm_hbm, scale_hbm, second_hbm,
    wo_hbm, w1_hbm,
    sums, dbranch_out, dm_own, dm_sib, o_keep, o_send,
    wo, w1, dm, dinner, norm1, scale1, second, dbranch, ograd, partial,
    in_sem, out_sem, *, shards,
):
    core = where[0]
    rows = mix_own.shape[0]
    block = mix_own.shape[2]
    width, hidden = w1.shape
    half = width // 2
    chunks = 3
    step = hidden // chunks
    lines = rows * block // TALL
    vec = lambda ref: ref[...].astype(F32)[None, :]
    own_half = pl.ds(pl.multiple_of(core * half, half), half)
    sib_half = pl.ds(pl.multiple_of((1 - core) * half, half), half)
    load_j = []
    for j in range(chunks):
        cols = slice(j * step, (j + 1) * step)
        load_j.append(pltpu.make_async_copy(dinner_hbm.at[:, cols], dinner.at[:, cols], in_sem.at[2 * j]))
        load_j.append(pltpu.make_async_copy(w1_hbm.at[:, cols], w1.at[:, cols], in_sem.at[1 + 2 * j]))
        load_j[-2].start()
        load_j[-1].start()
    pairs = ((second_hbm, second), (norm_hbm, norm1), (scale_hbm, scale1), (wo_hbm, wo))
    late = [pltpu.make_async_copy(src, dst, in_sem.at[6 + k]) for k, (src, dst) in enumerate(pairs)]
    for copy in late:
        copy.start()
    put = Puts(out_sem)
    partial[...] = jnp.zeros_like(partial)
    total = None
    for j in range(chunks):
        cols = slice(j * step, (j + 1) * step)
        load_j[2 * j].wait()
        load_j[2 * j + 1].wait()
        if j == chunks - 1:
            late[0].wait()
        value = contract(dinner[:, cols], w1[:, cols], 1, 1)
        total = value if total is None else total + value
    second[...] += total
    for copy in late[1:]:
        copy.wait()

    def norm_attn(i, _):
        at = pl.ds(pl.multiple_of(i * TALL, TALL), TALL)
        d_first = second[at]
        n1 = norm1[at]
        d_branch = norm_back(d_first * vec(ag), n1, scale1[at][:, :1]).astype(LOW)
        dbranch[at] = d_branch
        partial[:, :width] += fold(d_branch.astype(F32))
        partial[:, width : 2 * width] += fold(d_first * n1)
        partial[:, 2 * width : 3 * width] += fold(d_first)
        return 0

    lax.fori_loop(0, lines, norm_attn, 0, unroll=lines)
    put(dbranch, dbranch_out)
    for r in range(rows):
        at = slice(r * block, (r + 1) * block)
        dm[0, r] = contract(wo[own_half, :], dbranch[at], 1, 1).astype(LOW)
        dm[1, r] = contract(wo[sib_half, :], dbranch[at], 1, 1).astype(LOW)
    put(dm.at[1], dm_sib)
    put(dm.at[0], dm_own)
    sums[:, : 3 * width] = col_sum(partial[...])
    sums[:, 3 * width : 3 * width + hidden] = sums_inner[...]
    sums[:, 3 * width + hidden :] = sums_outer[...]
    size = width // shards
    for k, mix in enumerate((mix_own, mix_sib)):
        value = contract(mix[0], dbranch[:block], 1, 0)
        for r in range(1, rows):
            value += contract(mix[r], dbranch[r * block : (r + 1) * block], 1, 0)
        ograd[own_half if k == 0 else sib_half, :] = value.astype(LOW)
    for s in range(shards):
        put.shard(where, 2 + 16 * 4, s, ograd, s * size, size, sib_half, o_send)
        put.shard(where, 2 + 16 * 4, s, ograd, s * size, size, own_half, o_keep)
    put.wait()


def branch(
    where, orders, shards, mix_own, mix_sib, ag, sums_outer, sums_inner, dinner, norm, scale, second, wo, w1, after=()
):
    rows, cols, half = mix_own.shape
    width, hidden = w1.shape
    tokens = rows * half
    whole = lambda v: pl.BlockSpec(v.shape, lambda i, w: (0,) * len(v.shape))
    anywhere = pl.BlockSpec(memory_space=pl.ANY)
    outs = [SDS((1, 6 * width + hidden), F32), SDS((tokens, width), LOW)] + [SDS((rows, cols, half), LOW)] * 2
    n = entries(orders[4], shards)
    outs += [SDS((n, width // n, cols), LOW)] * 2
    small = (mix_own, mix_sib, ag, sums_outer, sums_inner)
    big = (dinner, norm, scale, second, wo, w1)
    low = lambda *s: pltpu.VMEM(s, LOW)
    wide = lambda *s: pltpu.VMEM(s, F32)
    return call(
        functools.partial(branch_kernel, shards=shards), where, small + big, after,
        grid=(1,),
        in_specs=[whole(v) for v in small] + [anywhere] * len(big),
        out_specs=[whole(outs[0])] + [anywhere] * (len(outs) - 1),
        out_shape=outs,
        scratch=[
            low(width, width), low(width, hidden), low(2, rows, cols, half), low(tokens, hidden),
            wide(tokens, width), wide(tokens, 128), wide(tokens, width), low(tokens, width),
            low(width, width), wide(8, 3 * width),
            pltpu.SemaphoreType.DMA((10,)), pltpu.SemaphoreType.DMA((3 + 4 * shards,)),
        ],
        us=13,
        name="branch",
    )


def attend_back_kernel(
    where, q_ref, k_ref, v_ref, e_ref, inv_ref, mix_own, mix_sib, dm_own, dm_sib,
    dq_out, dk_out, dv_out,
):
    scale = HD**-0.5
    j = pl.program_id(0)
    heads = q_ref.shape[1] // HD
    for h in range(heads):
        part = slice(h * HD, (h + 1) * HD)
        mixed = jnp.concatenate([mix_own[0, part], mix_sib[0, part]], axis=1)
        dm = jnp.concatenate([dm_own[0, part], dm_sib[0, part]], axis=1)
        d_out = dm.astype(F32) * inv_ref[0, pl.ds(j * heads + h, 1)]
        delta = col_sum(d_out * mixed.astype(F32))
        d_low = d_out.astype(LOW)
        e = e_ref[0, h]
        dp = contract(v_ref[0, part], d_low, 0, 0)
        ds = (e.astype(F32) * (dp - delta)).astype(LOW)
        dq_out[0, part] = (contract(k_ref[0, part], ds, 1, 0) * scale).astype(LOW)
        dk_out[0, part] = (contract(q_ref[0, part], ds, 1, 1) * scale).astype(LOW)
        dv_out[0, part] = contract(d_low, e, 1, 1).astype(LOW)


def attend_back(where, r, q, k, v, e, inv, mix_own, mix_sib, dm_own, dm_sib, reuse=(), after=()):
    rows, cols, length = q.shape
    heads = cols // HD
    step = 2
    tall = step * HD
    at = lambda j, w: (r, j, 0)
    big = pl.BlockSpec((1, tall, length), at)
    small = pl.BlockSpec((1, tall, length // 2), at)
    return call(
        attend_back_kernel, where, (q, k, v, e, inv, mix_own, mix_sib, dm_own, dm_sib), after,
        grid=(heads // step,),
        in_specs=[big] * 3
        + [
            pl.BlockSpec((1, step, length, length), lambda j, w: (r, j, 0, 0)),
            pl.BlockSpec((1, heads, length), lambda j, w: (r, 0, 0)),
        ]
        + [small] * 4,
        out_specs=[big] * 3,
        out_shape=[SDS((rows, cols, length), LOW)] * 3,
        us=6,
        reuse=reuse,
        name="attend_back",
    )


def weight_kernel(where, t0, t1, t2, t3, dq_ref, dk_ref, dv_ref, vectors, gq, gk, gv, aq, ak, av, bias, *, orders, shards):
    i = pl.program_id(0)
    core = where[0]
    width, cols = gk.shape
    size = width // shards
    x = jnp.concatenate([t0[0], t1[0], t2[0], t3[0]], axis=0)
    dq, dk, dv = dq_ref[0], dk_ref[0], dv_ref[0]
    tq, tk, tv = (contract(x, d, 0, 1) for d in (dq, dk, dv))
    ones = jnp.ones((8, x.shape[0]), LOW)
    tb = jnp.concatenate([contract(ones, dq, 1, 1), contract(ones, dv, 1, 1)], axis=1)

    @pl.when(i == 0)
    def _():
        aq[...] = tq
        ak[...] = tk
        av[...] = tv
        bias[...] = tb

    @pl.when(i > 0)
    def _():
        aq[...] += tq
        ak[...] += tk
        av[...] += tv
        bias[...] += tb

    def put(ref, acc, n):
        if shards == 1:
            ref[:width] = acc[...].astype(LOW)
            return
        cut = 2 if len(orders[n]) > 4 else 1
        high = size // cut
        for s in range(shards):
            for k in range(cut):
                start = pl.multiple_of(where[2 + 16 * n + 2 * s + k] * high, 16)
                row = s * size + k * high
                ref[pl.ds(start, high)] = acc[row : row + high].astype(LOW)

    @pl.when(i == pl.num_programs(0) - 1)
    def _():
        put(gq, aq, 5)
        put(gk, ak, 6)
        put(gv, av, 7)
        count = vectors.shape[1] // cols
        lines = [vectors[:, n * cols : (n + 1) * cols] for n in range(count)]
        for v in (bias[:1, :cols], bias[:1, cols:]):
            lines += [jnp.where(core == 0, v, 0.0), jnp.where(core == 1, v, 0.0)]
        lines.append(jnp.zeros((gq.shape[0] - width - len(lines), cols), F32))
        gq[width:] = jnp.concatenate(lines, axis=0).astype(LOW)


def weight_grads(where, orders, shards, toks, dq, dk, dv, vectors, after=()):
    rows, span, width = toks[0].shape
    cols, length = dq.shape[1:]
    extra = 32
    row3 = lambda *s: pl.BlockSpec((1,) + s, lambda r, w: (r, 0, 0))
    whole = lambda *s: pl.BlockSpec(s, lambda r, w: (0,) * len(s))
    return call(
        functools.partial(weight_kernel, orders=orders, shards=shards), where, (*toks, dq, dk, dv, vectors), after,
        grid=(rows,),
        in_specs=[row3(span, width)] * 4 + [row3(cols, length)] * 3 + [whole(*vectors.shape)],
        out_specs=[whole(width + extra, cols), whole(width, cols), whole(width, cols)],
        out_shape=[SDS((width + extra, cols), LOW), SDS((width, cols), LOW), SDS((width, cols), LOW)],
        scratch=[pltpu.VMEM((width, cols), F32)] * 3 + [pltpu.VMEM((8, 2 * cols), F32)],
        us=7,
        name="weight_grads",
    )


def input_kernel(where, dq, dk, dv, wq, wk, wv, own, sib):
    half = own.shape[1]
    back = contract(dq[0], wq[...], 0, 1)
    back = back + contract(dk[0], wk[...], 0, 1) + contract(dv[0], wv[...], 0, 1)
    own[0] = back[:half]
    sib[0] = back[half:].astype(LOW)


def input_part(where, dq, dk, dv, wq, wk, wv, after=()):
    rows, cols, length = dq.shape
    width = wq.shape[0]
    row3 = lambda *s: pl.BlockSpec((1,) + s, lambda r, w: (r, 0, 0))
    weight = pl.BlockSpec((width, cols), lambda r, w: (0, w[0]))
    half = length // 2
    return call(
        input_kernel, where, (dq, dk, dv, wq, wk, wv), after,
        grid=(rows,),
        in_specs=[row3(cols, length)] * 3 + [weight] * 3,
        out_specs=[row3(half, width)] * 2,
        out_shape=[SDS((rows, half, width), F32), SDS((rows, half, width), LOW)],
        us=5,
        name="input_part",
    )


def finish_kernel(where, mine, got, gq, gk, gv, *outs):
    core = where[0]
    b = where[1]
    size, width = gq.shape
    cols = width // 2
    for n, ref in enumerate((gq, gk, gv)):
        a = mine[n * size : (n + 1) * size].astype(F32)
        c = got[n * size : (n + 1) * size].astype(F32)
        ref[:, :cols] = jnp.where(core == 0, a, c)
        ref[:, cols:] = jnp.where(core == 0, c, a)
    total = mine[3 * size :].astype(F32) + got[3 * size :].astype(F32)
    row = 0
    for ref in outs:
        n = ref.shape[0]
        parts = n * (width // size) // cols
        line = jnp.concatenate([total[row + i : row + i + 1] for i in range(parts)], axis=1)
        row += parts
        picked = jnp.zeros((1, n), F32)
        for s in range(width // size):
            picked = jnp.where(b == s, line[:, s * n : (s + 1) * n], picked)
        ref[...] = picked[0]


def finish(where, mine, got, size, width, lengths):
    whole = lambda *s: pl.BlockSpec(s, lambda i, w: (0,) * len(s))
    return call(
        finish_kernel, where, (mine, got), (),
        grid=(1,),
        in_specs=[whole(*mine.shape)] * 2,
        out_specs=[whole(size, width)] * 3 + [whole(n) for n in lengths],
        out_shape=[SDS((size, width), F32)] * 3 + [SDS((n,), F32) for n in lengths],
        us=2,
        name="finish",
    )


def swap(v, axis, mask, size):
    return lax.ppermute(v, axis, [(i, i ^ mask) for i in range(size)])


def add_low(a, b):
    return (a.astype(F32) + b.astype(F32)).astype(LOW)


def fix(v):
    return lax.optimization_barrier(v)


ORDERS = ("1x2y", "y1x2g", "xy12g", "1xy2g", "x12y", "x12y", "1xy2g", "yx12g")
BITS = {"x": 0, "1": 1, "2": 2}


def solution(mesh):
    batch_size = mesh.shape["batch"]
    blk_size = mesh.shape["blk"]
    direct = batch_size == 8
    shards = batch_size if direct else 1

    def blk_swap(v, mask):
        return swap(v, "blk", mask, blk_size)

    def reduce_shards(g, order, y, tail=0):
        for place, step in enumerate(order):
            if step == "g":
                got = blk_swap(g, 2)
                return jnp.where(
                    y == 0, jnp.concatenate([g[0], got[0]], axis=0), jnp.concatenate([got[0], g[0]], axis=0)
                )
            if step == "y" and place == len(order) - 1:
                g = fix(add_low(g, blk_swap(g, 2)))
                return g if tail else g[0]
            n = g.shape[0] - tail
            half = n // 2
            send = g[half:]
            if step == "y":
                got = blk_swap(send, 2)
            else:
                got = swap(send, "batch", 1 << BITS[step], batch_size)
            new = add_low(g[:half], got[:half])
            if tail:
                new = jnp.concatenate([new, add_low(g[n:], got[half:])], axis=0)
            g = fix(new)

    def per_device(
        tokens, segment_ids, query_weight, query_bias, key_weight, value_weight, value_bias,
        output_weight, output_bias, attn_gain, attn_shift, inner_weight, inner_bias,
        outer_weight, outer_bias, final_gain, final_shift, cotangent,
    ):
        count, span, width = tokens.shape
        rows = count // 2
        me = lax.axis_index("blk")
        b = lax.axis_index("batch")
        core = me & 1
        y = (me >> 1) & 1

        index = jnp.arange(16, dtype=jnp.int32)
        moved = {k: ((index >> (1 + n)) ^ (b >> n)) & 1 for k, n in BITS.items()}
        moved["y"] = (index & 1) ^ y
        maps = []
        for order in ORDERS:
            steps = order[:-1]
            maps.append(sum(moved[k] << (len(steps) - 1 - i) for i, k in enumerate(steps)))
        if not direct:
            maps = [jnp.zeros_like(v) for v in maps]
        where = jnp.concatenate([jnp.stack([core, b]).astype(jnp.int32)] + maps)

        def mine(v):
            return lax.dynamic_slice_in_dim(v, y * rows, rows, 0)

        def other(v):
            return lax.dynamic_slice_in_dim(v, (1 - y) * rows, rows, 0)

        def halves(own, got, axis):
            return jnp.where(
                core == 0,
                jnp.concatenate([own, got], axis=axis),
                jnp.concatenate([got, own], axis=axis),
            )

        def return_rows(keep, send):
            got = blk_swap(send, 2)
            return jnp.where(
                y == 0, jnp.concatenate([keep, got], axis=0), jnp.concatenate([got, keep], axis=0)
            )

        t1 = blk_swap(other(tokens), 2)
        t0 = mine(tokens)
        t2 = blk_swap(t0, 1)
        t3 = blk_swap(t1, 1)
        toks = (t0, t1, t2, t3)
        c1 = blk_swap(other(cotangent), 2)
        c0 = mine(cotangent)
        seg = mine(segment_ids).reshape(rows, 4, span)
        seg = jnp.concatenate(
            [lax.dynamic_index_in_dim(seg, me ^ r, 1, keepdims=False) for r in (0, 2, 1, 3)], axis=1
        )
        q, k, v, e, inv, mix_own, mix_out = attend(
            where, toks, seg[:, None, :], seg[:, :, None],
            query_weight, key_weight, value_weight, query_bias, value_bias,
        )
        mix_sib = blk_swap(mix_out, 1)
        (
            sums_outer, out0, out1, slope, first_low, norm, scale, second, douter, ok0, os0, ok1, os1,
        ) = forward(
            where, ORDERS, shards, t0, t1, mix_own, mix_sib, c0, c1, output_weight, inner_weight, outer_weight,
            output_bias, attn_gain, attn_shift, inner_bias, outer_bias, final_gain, final_shift,
        )
        sums_inner, dinner, ik0, is0, ik1, is1 = inner_grad(
            where, ORDERS, shards, slope, first_low, douter, outer_weight
        )

        def over_cores(keep, send):
            return fix(add_low(keep, blk_swap(send, 1)))

        outer = [over_cores(ok0, os0), over_cores(ok1, os1)]
        vectors, dbranch, dm_own, dm_out, o_keep, o_send = branch(
            where, ORDERS, shards, mix_own, mix_sib, attn_gain, sums_outer, sums_inner, dinner, norm, scale,
            second, output_weight, inner_weight, after=tuple(outer),
        )
        dm_sib = blk_swap(dm_out, 1)
        inner = [over_cores(ik0, is0), over_cores(ik1, is1)]
        result = return_rows(out0, out1)
        args = (q, k, v, e, inv, mix_own, mix_out, dm_own, dm_sib)
        grads = attend_back(where, 0, *args, after=tuple(inner))
        o_part = over_cores(o_keep, o_send)
        grads = attend_back(where, 1, *args, reuse=grads, after=(o_part,))
        grads = attend_back(where, 2, *args, reuse=grads)
        gq, gk, gv = weight_grads(where, ORDERS, shards, toks, *grads, vectors)
        in_own, in_out = input_part(where, *grads, query_weight, key_weight, value_weight, after=(gq,))
        in_grad = dbranch.reshape(in_own.shape).astype(F32) + in_own + blk_swap(in_out, 1).astype(F32)
        in_grad = in_grad.astype(LOW)
        input_grad = return_rows(in_grad[:, :span], in_grad[:, span:])

        def join(v, axis):
            v = fix(v)
            return halves(v, blk_swap(v, 1), axis).astype(F32)

        def add_y(g):
            return fix(add_low(g, blk_swap(g, 2)))

        if direct:
            size = width // shards
            tail = gq.shape[0] - gk.shape[0]
            cut = lambda g, n: g.reshape(entries(ORDERS[n], shards), -1, g.shape[1])
            outer = [reduce_shards(g, ORDERS[n], y) for n, g in enumerate(outer)]
            inner = [reduce_shards(g, ORDERS[2 + n], y) for n, g in enumerate(inner)]
            o_part = reduce_shards(o_part, ORDERS[4], y)
            gq = reduce_shards(gq, ORDERS[5], y, tail)
            gk = reduce_shards(cut(gk, 6), ORDERS[6], y)
            gv = reduce_shards(cut(gv, 7), ORDERS[7], y)
            outer_done = join(jnp.concatenate(outer, axis=0), 0)
            inner_done = join(jnp.concatenate(inner, axis=1), 1)
            output_done = join(o_part, 1)
            final = fix(jnp.concatenate([gq[:size], gk, gv, gq[size:]], axis=0))
            lengths = [n // shards for n in (width,) * 3 + (inner_weight.shape[1],) + (width,) * 5]
            query_done, key_done, value_done, *vecs = finish(
                where, final, blk_swap(final, 1), size, width, lengths
            )
        else:

            def whole(v):
                return add_y(lax.psum_scatter(v, "batch", scatter_dimension=0, tiled=True))

            outer_part = jnp.concatenate([outer[0][0], outer[1][0]], axis=0)
            outer_done = whole(halves(outer_part, blk_swap(outer_part, 1), 0)).astype(F32)
            inner_done = join(whole(jnp.concatenate([inner[0][0], inner[1][0]], axis=1)), 1)
            output_done = join(whole(o_part[0]), 1)
            total = lax.psum(gq[width:].astype(F32), ("batch", "blk")).reshape(-1)
            query_done, key_done, value_done = (join(whole(g[:width]), 1) for g in (gq, gk, gv))
            vecs = []
            at = 0
            for n in (width,) * 3 + (inner_weight.shape[1],) + (width,) * 5:
                part = total[at : at + n].reshape(batch_size, n // batch_size)
                vecs.append(lax.dynamic_index_in_dim(part, b, 0, keepdims=False))
                at += n
        g_ob, g_ag, g_as, g_b1, g_b2, g_fg, g_fs, g_qb, g_vb = vecs
        return (
            result, input_grad, query_done, g_qb, key_done, value_done, g_vb, output_done, g_ob,
            g_ag, g_as, inner_done, g_b1, outer_done, g_b2, g_fg, g_fs,
        )

    tok = P("batch", "blk", None)
    mat = P("batch", None)
    vec = P("batch")
    return jax.shard_map(
        per_device,
        mesh=mesh,
        in_specs=(tok, P("batch", None)) + (P(),) * 15 + (tok,),
        out_specs=(
            tok, tok, mat, vec, mat, mat, vec, mat, vec, vec, vec, mat, vec, mat, vec, vec, vec,
        ),
        check_vma=False,
    )
```

time: 1030 us -> 264 us (0.26)
  waiting for transfers between devices: 667 us -> 57.9 us
  matrix products: 146 us -> 0 us
  Pallas kernels: 0 us -> 118 us
  other arithmetic: 82.2 us -> 12 us
  starting transfers between devices: 0.82 us -> 52.7 us
  blocking collectives: 44.5 us -> 0 us
  local copies, waits for them, and re-layouts: 60.7 us -> 16.6 us
  between operations: 16.2 us -> 2.09 us
    reduce_scatter x4 -> x0, waiting for transfers between devices: 367 us -> none  [the longest x1 164 us: per_device(): lax.psum_scatter(outer_weight_part, 'batch', scatter_dimension=0, tiled=T...]
    unnamed x13 -> x0, waiting for transfers between devices: 209 us -> none
    dot_general x24 -> x0, matrix products: 146 us -> none  [the longest x4 27.7 us: back_product(): jnp.einsum('ste,de->std', gradient, matrix, preferred_element_type=jnp.fl...]
    pallas_call x0 -> x10, Pallas kernels: none -> 118 us  [call(): pl.pallas_call(body, grid_spec=pltpu.PrefetchScalarGridSpec(num_scalar_pr...]
    ppermute x0 -> x55, waiting for transfers between devices: none -> 57.9 us  [swap(): return lax.ppermute(v, axis, [(i, i ^ mask) for i in range(size)])]
    ppermute x0 -> x55, starting transfers between devices: none -> 52.7 us  [swap(): return lax.ppermute(v, axis, [(i, i ^ mask) for i in range(size)])]
    convert_element_type x26 -> x44, other arithmetic: 58.6 us -> 9.31 us  [the longest x40 5.9 us: add_low(): return (a.astype(F32) + b.astype(F32)).astype(LOW)]
    psum x1 -> x0, waiting for transfers between devices: 45.7 us -> none  [per_device(): lax.psum(pieces[0].astype(jnp.bfloat16), 'blk').astype(jnp.float32)]
  transfers between devices with their start and end apart: 10 -> 55, of which waited for: 10 -> 23; matrix products, arithmetic and copies ran while one was open for 11% -> 8% of each run, Pallas kernels for 0% -> 35%
where the time goes in v2:
time: 264 us; the launch traced here: 259 us
  Pallas kernels  118 us (45%)
  waiting for transfers between devices  57.9 us (22%)
  starting transfers between devices  52.7 us (20%)
  local copies, waits for them, and re-layouts  16.6 us (6%)
  other arithmetic  12 us (5%)
    pallas_call x10, Pallas kernels, call(): pl.pallas_call(body, grid_spec=pltpu.PrefetchScalarGridSpec(num_scalar_pr...  118 us
    ppermute x55, waiting for transfers between devices, swap(): return lax.ppermute(v, axis, [(i, i ^ mask) for i in range(size)])  57.9 us
    ppermute x55, starting transfers between devices, swap(): return lax.ppermute(v, axis, [(i, i ^ mask) for i in range(size)])  52.7 us
    slice x29, local copies, waits for them, and re-layouts, reduce_shards(): send = g[half:]  6.07 us
    convert_element_type x40, other arithmetic, add_low(): return (a.astype(F32) + b.astype(F32)).astype(LOW)  5.9 us
    unnamed x64, local copies, waits for them, and re-layouts  5.6 us
  transfers between devices with their start and end apart: 55, of which 23 were waited for; matrix products, arithmetic and copies ran while one was open for 8% of the time, Pallas kernels for 35%

profile of v2, /device:TPU:0, one launch (start us, length us, event | category | flops | bytes accessed | tf_op | source)
XLA Modules:
  0.0 259.0 jit_solution(14502377951125940910)
XLA Ops:
  0.7 1.4 constant_dynamic-slice_fusion.6
  2.1 3.0 %collective-permute-start = (bf16[3,128,768]{2,1,0:T(8,128)(2,1)S(1)}, bf16[3,128,768]{2,1,0:T(8,128)(2,1)S(1)}, u32[]{:S(2)}, u32[]{:S(2)}) collective-permute-start(bf16[3,128,768]{2,1,0:T(8,128)(2,1)S(1)} %get-tuple-element.137), channel_id=1, source_target_pairs={{0,2},{1,3},{2,0},{3,1},{4,6},{5,7},{6,4},{7,5},{8,10},{9,11},{10,... | collective-permute-start | bytes 1769480 | tf_op jit(solution)/shard_map/ppermute | solution.py:674
  6.2 13.1 %collective-permute-done.refs_1_.refs_10_ = bf16[3,128,768]{2,1,0:T(8,128)(2,1)S(1)} collective-permute-done((bf16[3,128,768]{2,1,0:T(8,128)(2,1)S(1)}, bf16[3,128,768]{2,1,0:T(8,128)(2,1)S(1)}, u32[]{:S(2)}, u32[]{:S(2)}) %collective-permute-start) | collective-permute-done | bytes 589856 | tf_op jit(solution)/shard_map/ppermute | solution.py:674
  20.1 1.2 copy.42.refs_5_
  23.6 18.0 %attend.1 = (bf16[3,384,512]{2,1,0:T(8,128)(2,1)}, bf16[3,384,512]{2,1,0:T(8,128)(2,1)}, bf16[3,384,512]{2,1,0:T(8,128)(2,1)}, bf16[3,6,512,512]{3,2,1,0:T(8,128...) custom-call(s32[130]{0:T(256)} %concatenate.84.w, ...), custom_call_target="tpu_custom_call" | custom-call | flops 18699999232 | tf_op jit(solution)/shard_map/attend/pallas_call | solution.py:31
  42.0 1.8 collective-permute-done.3.refs_1_
  44.7 27.0 %forward.1 = (f32[1,2304]{1,0:T(1,128)}, bf16[3,128,768]{2,1,0:T(8,128)(2,1)}, bf16[3,128,768]{2,1,0:T(8,128)(2,1)}, bf16[768,3072]{1,0:T(8,128)(2,1)}, bf16[768...) custom-call(s32[130]{0:T(256)} %concatenate.84.w, ...), custom_call_target="tpu_custom_call" | custom-call | flops 29699999744 | tf_op jit(solution)/shard_map/forward/pallas_call | solution.py:31
  71.7 2.1 collective-permute-start.5
  74.3 13.8 %inner_grad.1 = (f32[1,3072]{1,0:T(1,128)}, bf16[768,3072]{1,0:T(8,128)(2,1)}, bf16[16,48,768]{2,1,0:T(8,128)(2,1)}, bf16[16,48,768]{2,1,0:T(8,128)(2,1)}, bf16[...) custom-call(s32[130]{0:T(256)} %concatenate.84.w, bf16[768,3072]{1,0:T(8,128)(2,1)} %get-tuple-element.80.refs_0_, ...), custom_call_target="tpu_custom_call" | custom-call | flops 12099999744 | tf_op jit(solution)/shard_map/inner_grad/pallas_call | solution.py:31
  88.7 1.2 maximum_select_fusion
  91.8 1.6 collective-permute-start.45
  95.6 15.9 %branch.1 = (f32[1,7680]{1,0:T(1,128)}, bf16[768,768]{1,0:T(8,128)(2,1)}, bf16[3,384,256]{2,1,0:T(8,128)(2,1)}, bf16[3,384,256]{2,1,0:T(8,128)(2,1)}, bf16[8,96,...) custom-call(s32[130]{0:T(256)} %concatenate.84.w, bf16[3,384,256]{2,1,0:T(8,128)(2,1)} %get-tuple-element.75.refs_0_.refs_5_, ...), custom_call_target="tpu_custom_call" | custom-call | flops 14300000256 | tf_op jit(solution)/shard_map/branch/pallas_call | solution.py:31
  112.1 1.6 add_convert_fusion.1.refs_9_
  113.8 1.6 collective-permute-start.34
  115.4 1.6 add_convert_fusion.refs_10_
  117.1 1.0 collective-permute-start.39
  119.6 1.5 collective-permute-start.46
  122.0 1.0 collective-permute-start.50
  123.9 6.1 %collective-permute-done.34 = bf16[8,48,768]{2,1,0:T(8,128)(2,1)S(1)} collective-permute-done((bf16[8,48,768]{2,1,0:T(8,128)(2,1)S(1)}, bf16[8,48,768]{2,1,0:T(8,128)(2,1)S(1)}, u32[]{:S(2)}, u32[]{:S(2)}) %collective-permute-start.34) | collective-permute-done | bytes 589856 | tf_op jit(solution)/shard_map/ppermute | solution.py:674
  130.0 1.5 collective-permute-start.29
  133.3 1.1 collective-permute-start.35
  135.4 1.5 collective-permute-start.40
  136.9 7.3 %attend_back.3 = (bf16[3,384,512]{2,1,0:T(8,128)(2,1)}, bf16[3,384,512]{2,1,0:T(8,128)(2,1)}, bf16[3,384,512]{2,1,0:T(8,128)(2,1)}) custom-call(s32[130]{0:T(256)} %concatenate.84.w, bf16[3,384,512]{2,1,0:T(8,128)(2,1)} %get-tuple-element.93.refs_0_, bf16[3,384,512]{2,1,0:T(8,128)(2,1)} %get-tuple-element.94.refs_1_, ...), custom_call_target="tpu_custom_call" | custom-call | flops 6600000000 | tf_op jit(solution)/shard_map/attend_back/pallas_call | solution.py:31
  144.2 7.5 %attend_back.4 = (bf16[3,384,512]{2,1,0:T(8,128)(2,1)}, bf16[3,384,512]{2,1,0:T(8,128)(2,1)}, bf16[3,384,512]{2,1,0:T(8,128)(2,1)}) custom-call(s32[130]{0:T(256)} %concatenate.84.w, bf16[3,384,512]{2,1,0:T(8,128)(2,1)} %get-tuple-element.93.refs_0_, ...), custom_call_target="tpu_custom_call", output_to_operand_aliasing={{0}: (10, {}), {1}: (11, {}), {2}: (12, {})} | custom-call | flops 6600000000 | tf_op jit(solution)/shard_map/attend_back/pallas_call | solution.py:31
  151.7 7.3 %attend_back.5 = (bf16[3,384,512]{2,1,0:T(8,128)(2,1)}, bf16[3,384,512]{2,1,0:T(8,128)(2,1)}, bf16[3,384,512]{2,1,0:T(8,128)(2,1)}) custom-call(s32[130]{0:T(256)} %concatenate.84.w, bf16[3,384,512]{2,1,0:T(8,128)(2,1)} %get-tuple-element.93.refs_0_, ...), custom_call_target="tpu_custom_call", output_to_operand_aliasing={{0}: (10, {}), {1}: (11, {}), {2}: (12, {})} | custom-call | flops 6600000000 | tf_op jit(solution)/shard_map/attend_back/pallas_call | solution.py:31
  159.0 9.5 %weight_grads.1 = (bf16[800,384]{1,0:T(8,128)(2,1)}, bf16[768,384]{1,0:T(8,128)(2,1)}, bf16[768,384]{1,0:T(8,128)(2,1)}) custom-call(s32[130]{0:T(256)} %concatenate.84.w, bf16[3,128,768]{2,1,0:T(8,128)(2,1)} %copy-done.24, bf16[3,128,768]{2,1,0:T(8,128)(2,1)} %copy-done.27, bf16[3,128,768]{2,1,0:T(8,128)(2,1)} %copy-done.28, ...), custom_call_target="tpu_custom_call" | custom-call | flops 7699999744 | tf_op jit(solution)/shard_map/weight_grads/pallas_call | solution.py:31
  168.4 8.3 %input_part.1 = (f32[3,256,768]{2,1,0:T(8,128)}, bf16[3,256,768]{2,1,0:T(8,128)(2,1)}) custom-call(s32[130]{0:T(256)} %concatenate.84.w, bf16[3,384,512]{2,1,0:T(8,128)(2,1)} %get-tuple-element.112.refs_4_.refs_0_, bf16[3,384,512]{2,1,0:T(8,128)(2,1)} %get-tuple-element.113.refs_5_.refs_1_, bf16[3,384,512]{2,1,0:T(8,128)(2,1)} %get-tuple-element.114.refs_6_.refs_2_, ...), custom_call_target="tpu_custom_call" | custom-call | flops 5500000256 | tf_op jit(solution)/shard_map/input_part/pallas_call | solution.py:31
  176.8 1.0 copy-done.22
  178.0 1.0 collective-permute-start.18
  179.8 1.0 collective-permute-start.23
  181.0 2.7 %collective-permute-start.47 = (bf16[1,96,768]{2,1,0:T(8,128)(2,1)S(1)}, bf16[1,96,768]{2,1,0:T(8,128)(2,1)S(1)}, u32[]{:S(2)}, u32[]{:S(2)}) collective-permute-start(bf16[1,96,768]{2,1,0:T(8,128)(2,1)S(1)} %slice.349), channel_id=1, source_target_pairs={{0,16},{4,20},{8,24},{12,28},{16,0},{20,4},{24,8},{28,12},{1,17},{... | collective-permute-start | bytes 442376 | tf_op jit(solution)/shard_map/ppermute | solution.py:674
  183.8 1.0 collective-permute-done.18
  185.6 1.0 collective-permute-done.23
  186.6 1.0 collective-permute-start.30
  187.7 1.0 collective-permute-start.36
  188.9 2.6 collective-permute-done.47
  191.5 1.1 collective-permute-start.41
  192.7 1.6 collective-permute-start.19
  194.4 1.4 collective-permute-start.24
  196.7 1.3 collective-permute-start.48
  198.1 1.4 collective-permute-done.19
  199.9 1.0 collective-permute-done.24
  201.0 1.5 collective-permute-start.31
  202.5 1.5 collective-permute-start.37
  204.2 5.7 %collective-permute-done.52 = bf16[1,48,768]{2,1,0:T(8,128)(2,1)S(1)} collective-permute-done((bf16[1,48,768]{2,1,0:T(8,128)(2,1)S(1)}, bf16[1,48,768]{2,1,0:T(8,128)(2,1)S(1)}, u32[]{:S(2)}, u32[]{:S(2)}) %collective-permute-start.52) | collective-permute-done | bytes 73760 | tf_op jit(solution)/shard_map/ppermute | solution.py:674
  209.8 1.6 collective-permute-done.31
  212.7 2.4 collective-permute-done.42
  216.3 1.4 collective-permute-start.53
  218.1 2.6 collective-permute-start.21
  220.7 2.3 collective-permute-done.21
  223.0 2.6 collective-permute-start.26
  225.6 2.3 collective-permute-done.26
  227.8 1.2 collective-permute-start.32
  230.0 1.2 collective-permute-start.43
  232.3 1.2 collective-permute-start.27
  235.3 1.0 collective-permute-done.27
  236.3 1.2 collective-permute-start.17
  238.2 2.7 %collective-permute-done.17 = bf16[128,384]{1,0:T(8,128)(2,1)S(1)} collective-permute-done((bf16[128,384]{1,0:T(8,128)(2,1)S(1)}, bf16[128,384]{1,0:T(8,128)(2,1)S(1)}, u32[]{:S(2)}, u32[]{:S(2)}) %collective-permute-start.17) | collective-permute-done | bytes 98336 | tf_op jit(solution)/shard_map/ppermute | solution.py:674
  241.8 1.2 collective-permute-start.13
  243.0 1.2 fusion.2
  244.2 1.1 fusion.3
  246.0 3.2 %finish.1 = (f32[96,768]{1,0:T(8,128)}, f32[96,768]{1,0:T(8,128)}, f32[96,768]{1,0:T(8,128)}, f32[96]{0:T(128)}, f32[96]{0:T(128)}, /*index=5*/f32[96]{0:T(128)}...) custom-call(s32[130]{0:T(256)} %concatenate.84.w, ...), custom_call_target="tpu_custom_call" | custom-call | flops 2200000000 | tf_op jit(solution)/shard_map/finish/pallas_call | solution.py:31
  249.2 8.2 %collective-permute-done.13 = bf16[3,128,768]{2,1,0:T(8,128)(2,1)S(1)} collective-permute-done((bf16[3,128,768]{2,1,0:T(8,128)(2,1)S(1)}, bf16[3,128,768]{2,1,0:T(8,128)(2,1)S(1)}, u32[]{:S(2)}, u32[]{:S(2)}) %collective-permute-start.13) | collective-permute-done | bytes 589856 | tf_op jit(solution)/shard_map/ppermute | solution.py:674
  257.4 1.2 maximum_select_fusion.1
  (220 shorter events, 30.1 us)
Async XLA Ops:
  0.7 18.7 %copy-start = (s32[6,512]{1,0:T(8,128)S(1)}, s32[6,512]{1,0:T(8,128)}, u32[]{:S(2)}) copy-start(s32[6,512]{1,0:T(8,128)} %param.19) | copy-start | bytes 36868
  2.1 17.2 %collective-permute-start = (bf16[3,128,768]{2,1,0:T(8,128)(2,1)S(1)}, bf16[3,128,768]{2,1,0:T(8,128)(2,1)S(1)}, u32[]{:S(2)}, u32[]{:S(2)}) collective-permute-start(bf16[3,128,768]{2,1,0:T(8,128)(2,1)S(1)} %get-tuple-element.137), channel_id=1, source_target_pairs={{0,2},{1,3},{2,0},{3,1},{4,6},{5,7},{6,4},{7,5},{8,10},{9,11},{10,... | collective-permute-start | bytes 1769480 | tf_op jit(solution)/shard_map/ppermute | solution.py:674
  5.2 16.8 %collective-permute-start.1 = (bf16[3,128,768]{2,1,0:T(8,128)(2,1)S(1)}, bf16[3,128,768]{2,1,0:T(8,128)(2,1)S(1)}, u32[]{:S(2)}, u32[]{:S(2)}) collective-permute-start(bf16[3,128,768]{2,1,0:T(8,128)(2,1)S(1)} %get-tuple-element.138.refs_0_.refs_9_), channel_id=1, source_target_pairs={{0,1},{1,0},{2,3},{3,2},{4,5},{5,4},{6,7},{7,6},{8,9},{9,8},{10,11... | collective-permute-start | bytes 1769480 | tf_op jit(solution)/shard_map/ppermute | solution.py:674
  6.1 36.0 %collective-permute-start.4 = (bf16[3,128,768]{2,1,0:T(8,128)(2,1)S(1)}, bf16[3,128,768]{2,1,0:T(8,128)(2,1)}, u32[]{:S(2)}, u32[]{:S(2)}) collective-permute-start(bf16[3,128,768]{2,1,0:T(8,128)(2,1)S(1)} %get-tuple-element.135), channel_id=1, source_target_pairs={{0,2},{1,3},{2,0},{3,1},{4,6},{5,7},{6,4},{7,5},{8,10},{9,11},{10,... | collective-permute-start | bytes 1769480 | tf_op jit(solution)/shard_map/ppermute | solution.py:674
  19.3 2.7 %collective-permute-start.2 = (bf16[3,128,768]{2,1,0:T(8,128)(2,1)S(1)}, bf16[3,128,768]{2,1,0:T(8,128)(2,1)S(1)}, u32[]{:S(2)}, u32[]{:S(2)}) collective-permute-start(bf16[3,128,768]{2,1,0:T(8,128)(2,1)S(1)} %collective-permute-done.refs_1_.refs_10_), channel_id=1, source_target_pairs={{0,1},{1,0},{2,3},{3,2},{4,5},{5,4},{6,7},{7,6},{8,9},{9,8},{10,11... | collective-permute-start | bytes 1769480 | tf_op jit(solution)/shard_map/ppermute | solution.py:674
  41.6 2.3 collective-permute-start.3
  71.7 17.1 %collective-permute-start.5 = (bf16[3,128,768]{2,1,0:T(8,128)(2,1)}, bf16[3,128,768]{2,1,0:T(8,128)(2,1)S(1)}, u32[]{:S(2)}, u32[]{:S(2)}) collective-permute-start(bf16[3,128,768]{2,1,0:T(8,128)(2,1)} %get-tuple-element.78), channel_id=1, source_target_pairs={{0,2},{1,3},{2,0},{3,1},{4,6},{5,7},{6,4},{7,5},{8,10},{9,11},{10,... | collective-permute-start | bytes 1769480 | tf_op jit(solution)/shard_map/ppermute | solution.py:674
  73.8 16.1 %collective-permute-start.6 = (bf16[8,96,768]{2,1,0:T(8,128)(2,1)}, bf16[8,96,768]{2,1,0:T(8,128)(2,1)S(1)}, u32[]{:S(2)}, u32[]{:S(2)}) collective-permute-start(bf16[8,96,768]{2,1,0:T(8,128)(2,1)} %get-tuple-element.89), channel_id=1, source_target_pairs={{0,1},{1,0},{2,3},{3,2},{4,5},{5,4},{6,7},{7,6},{8,9},{9,8},{10,11... | collective-permute-start | bytes 3538952 | tf_op jit(solution)/shard_map/ppermute | solution.py:674
  73.9 19.5 %collective-permute-start.7 = (bf16[16,48,768]{2,1,0:T(8,128)(2,1)}, bf16[16,48,768]{2,1,0:T(8,128)(2,1)S(1)}, u32[]{:S(2)}, u32[]{:S(2)}) collective-permute-start(bf16[16,48,768]{2,1,0:T(8,128)(2,1)} %get-tuple-element.91), channel_id=1, source_target_pairs={{0,1},{1,0},{2,3},{3,2},{4,5},{5,4},{6,7},{7,6},{8,9},{9,8},{10,11... | collective-permute-start | bytes 3538952 | tf_op jit(solution)/shard_map/ppermute | solution.py:674
  74.3 14.4 %copy-start.21 = (bf16[3,128,768]{2,1,0:T(8,128)(2,1)S(1)}, bf16[3,128,768]{2,1,0:T(8,128)(2,1)}, u32[]{:S(2)}) copy-start(bf16[3,128,768]{2,1,0:T(8,128)(2,1)} %get-tuple-element.77) | copy-start | bytes 1769476
  88.2 23.5 %collective-permute-start.9 = (bf16[16,48,768]{2,1,0:T(8,128)(2,1)}, bf16[16,48,768]{2,1,0:T(8,128)(2,1)}, u32[]{:S(2)}, u32[]{:S(2)}) collective-permute-start(bf16[16,48,768]{2,1,0:T(8,128)(2,1)} %get-tuple-element.101), channel_id=1, source_target_pairs={{0,1},{1,0},{2,3},{3,2},{4,5},{5,4},{6,7},{7,6},{8,9},{9,8},{10,11... | collective-permute-start | bytes 3538952 | tf_op jit(solution)/shard_map/ppermute | solution.py:674
  88.3 25.5 %collective-permute-start.10 = (bf16[16,48,768]{2,1,0:T(8,128)(2,1)}, bf16[16,48,768]{2,1,0:T(8,128)(2,1)}, u32[]{:S(2)}, u32[]{:S(2)}) collective-permute-start(bf16[16,48,768]{2,1,0:T(8,128)(2,1)} %get-tuple-element.103), channel_id=1, source_target_pairs={{0,1},{1,0},{2,3},{3,2},{4,5},{5,4},{6,7},{7,6},{8,9},{9,8},{10,11... | collective-permute-start | bytes 3538952 | tf_op jit(solution)/shard_map/ppermute | solution.py:674
  91.8 25.2 %collective-permute-start.45 = (bf16[4,96,768]{2,1,0:T(8,128)(2,1)}, bf16[4,96,768]{2,1,0:T(8,128)(2,1)S(1)}, u32[]{:S(2)}, u32[]{:S(2)}) collective-permute-start(bf16[4,96,768]{2,1,0:T(8,128)(2,1)} %slice.345), channel_id=1, source_target_pairs={{0,8},{4,12},{8,0},{12,4},{16,24},{20,28},{24,16},{28,20},{1,9},{5... | collective-permute-start | bytes 1769480 | tf_op jit(solution)/shard_map/ppermute | solution.py:674
  94.7 24.9 %collective-permute-start.49 = (bf16[8,48,768]{2,1,0:T(8,128)(2,1)}, bf16[8,48,768]{2,1,0:T(8,128)(2,1)S(1)}, u32[]{:S(2)}, u32[]{:S(2)}) collective-permute-start(bf16[8,48,768]{2,1,0:T(8,128)(2,1)} %slice.351), channel_id=1, source_target_pairs={{0,2},{1,3},{2,0},{3,1},{4,6},{5,7},{6,4},{7,5},{8,10},{9,11},{10,... | collective-permute-start | bytes 1769480 | tf_op jit(solution)/shard_map/ppermute | solution.py:674
  95.6 16.5 %copy-start.14 = (bf16[16,48,768]{2,1,0:T(8,128)(2,1)S(1)}, bf16[16,48,768]{2,1,0:T(8,128)(2,1)}, u32[]{:S(2)}) copy-start(bf16[16,48,768]{2,1,0:T(8,128)(2,1)} %get-tuple-element.100) | copy-start | bytes 3538948
  111.5 23.8 %collective-permute-start.8 = (bf16[3,384,256]{2,1,0:T(8,128)(2,1)}, bf16[3,384,256]{2,1,0:T(8,128)(2,1)}, u32[]{:S(2)}, u32[]{:S(2)}) collective-permute-start(bf16[3,384,256]{2,1,0:T(8,128)(2,1)} %get-tuple-element.99), channel_id=1, source_target_pairs={{0,1},{1,0},{2,3},{3,2},{4,5},{5,4},{6,7},{7,6},{8,9},{9,8},{10,11... | collective-permute-start | bytes 1769480 | tf_op jit(solution)/shard_map/ppermute | solution.py:674
  111.6 10.3 %collective-permute-start.11 = (bf16[8,96,384]{2,1,0:T(8,128)(2,1)}, bf16[8,96,384]{2,1,0:T(8,128)(2,1)S(1)}, u32[]{:S(2)}, u32[]{:S(2)}) collective-permute-start(bf16[8,96,384]{2,1,0:T(8,128)(2,1)} %get-tuple-element.108), channel_id=1, source_target_pairs={{0,1},{1,0},{2,3},{3,2},{4,5},{5,4},{6,7},{7,6},{8,9},{9,8},{10,11... | collective-permute-start | bytes 1769480 | tf_op jit(solution)/shard_map/ppermute | solution.py:674
  113.7 17.9 %copy-start.2 = (bf16[16,48,768]{2,1,0:T(8,128)(2,1)}, bf16[16,48,768]{2,1,0:T(8,128)(2,1)S(1)}, u32[]{:S(2)}) copy-start(bf16[16,48,768]{2,1,0:T(8,128)(2,1)S(1)} %add_convert_fusion.1.refs_9_) | copy-start | bytes 3538948
  113.8 16.3 %collective-permute-start.34 = (bf16[8,48,768]{2,1,0:T(8,128)(2,1)S(1)}, bf16[8,48,768]{2,1,0:T(8,128)(2,1)S(1)}, u32[]{:S(2)}, u32[]{:S(2)}) collective-permute-start(bf16[8,48,768]{2,1,0:T(8,128)(2,1)S(1)} %slice.329), channel_id=1, source_target_pairs={{0,4},{4,0},{8,12},{12,8},{16,20},{20,16},{24,28},{28,24},{1,5},{5... | collective-permute-start | bytes 1769480 | tf_op jit(solution)/shard_map/ppermute | solution.py:674
  117.0 17.5 %copy-start.3 = (bf16[16,48,768]{2,1,0:T(8,128)(2,1)}, bf16[16,48,768]{2,1,0:T(8,128)(2,1)S(1)}, u32[]{:S(2)}) copy-start(bf16[16,48,768]{2,1,0:T(8,128)(2,1)S(1)} %add_convert_fusion.refs_10_) | copy-start | bytes 3538948
  117.1 16.3 %collective-permute-start.39 = (bf16[8,48,768]{2,1,0:T(8,128)(2,1)S(1)}, bf16[8,48,768]{2,1,0:T(8,128)(2,1)S(1)}, u32[]{:S(2)}, u32[]{:S(2)}) collective-permute-start(bf16[8,48,768]{2,1,0:T(8,128)(2,1)S(1)} %slice.337), channel_id=1, source_target_pairs={{0,8},{4,12},{8,0},{12,4},{16,24},{20,28},{24,16},{28,20},{1,9},{5... | collective-permute-start | bytes 1769480 | tf_op jit(solution)/shard_map/ppermute | solution.py:674
  119.6 58.4 %collective-permute-start.46 = (bf16[2,96,768]{2,1,0:T(8,128)(2,1)}, bf16[2,96,768]{2,1,0:T(8,128)(2,1)S(1)}, u32[]{:S(2)}, u32[]{:S(2)}) collective-permute-start(bf16[2,96,768]{2,1,0:T(8,128)(2,1)} %slice.347), channel_id=1, source_target_pairs={{0,4},{4,0},{8,12},{12,8},{16,20},{20,16},{24,28},{28,24},{1,5},{5... | collective-permute-start | bytes 884744 | tf_op jit(solution)/shard_map/ppermute | solution.py:674
  122.0 57.2 %collective-permute-start.50 = (bf16[4,48,768]{2,1,0:T(8,128)(2,1)}, bf16[4,48,768]{2,1,0:T(8,128)(2,1)S(1)}, u32[]{:S(2)}, u32[]{:S(2)}) collective-permute-start(bf16[4,48,768]{2,1,0:T(8,128)(2,1)} %slice.353), channel_id=1, source_target_pairs={{0,8},{4,12},{8,0},{12,4},{16,24},{20,28},{24,16},{28,20},{1,9},{5... | collective-permute-start | bytes 884744 | tf_op jit(solution)/shard_map/ppermute | solution.py:674
  123.1 8.6 %copy-start.8 = (bf16[8,96,384]{2,1,0:T(8,128)(2,1)}, bf16[8,96,384]{2,1,0:T(8,128)(2,1)S(1)}, u32[]{:S(2)}) copy-start(bf16[8,96,384]{2,1,0:T(8,128)(2,1)S(1)} %add_convert_fusion.8.refs_12_) | copy-start | bytes 1769476
  130.0 49.8 %collective-permute-start.29 = (bf16[4,96,384]{2,1,0:T(8,128)(2,1)}, bf16[4,96,384]{2,1,0:T(8,128)(2,1)S(1)}, u32[]{:S(2)}, u32[]{:S(2)}) collective-permute-start(bf16[4,96,384]{2,1,0:T(8,128)(2,1)} %slice.323), channel_id=1, source_target_pairs={{0,4},{4,0},{8,12},{12,8},{16,20},{20,16},{24,28},{28,24},{1,5},{5... | collective-permute-start | bytes 884744 | tf_op jit(solution)/shard_map/ppermute | solution.py:674
  133.3 47.5 %collective-permute-start.35 = (bf16[4,48,768]{2,1,0:T(8,128)(2,1)}, bf16[4,48,768]{2,1,0:T(8,128)(2,1)S(1)}, u32[]{:S(2)}, u32[]{:S(2)}) collective-permute-start(bf16[4,48,768]{2,1,0:T(8,128)(2,1)} %slice.331), channel_id=1, source_target_pairs={{0,2},{1,3},{2,0},{3,1},{4,6},{5,7},{6,4},{7,5},{8,10},{9,11},{10,... | collective-permute-start | bytes 884744 | tf_op jit(solution)/shard_map/ppermute | solution.py:674
  135.4 45.7 %collective-permute-start.40 = (bf16[4,48,768]{2,1,0:T(8,128)(2,1)}, bf16[4,48,768]{2,1,0:T(8,128)(2,1)S(1)}, u32[]{:S(2)}, u32[]{:S(2)}) collective-permute-start(bf16[4,48,768]{2,1,0:T(8,128)(2,1)} %slice.339), channel_id=1, source_target_pairs={{0,4},{4,0},{8,12},{12,8},{16,20},{20,16},{24,28},{28,24},{1,5},{5... | collective-permute-start | bytes 884744 | tf_op jit(solution)/shard_map/ppermute | solution.py:674
  168.4 8.3 %copy-start.23 = (bf16[768,384]{1,0:T(8,128)(2,1)S(1)}, bf16[768,384]{1,0:T(8,128)(2,1)}, u32[]{:S(2)}) copy-start(bf16[768,384]{1,0:T(8,128)(2,1)} %get-tuple-element.119) | copy-start | bytes 1769476
  178.0 6.8 %collective-permute-start.18 = (bf16[8,48,384]{2,1,0:T(8,128)(2,1)S(1)}, bf16[8,48,384]{2,1,0:T(8,128)(2,1)S(1)}, u32[]{:S(2)}, u32[]{:S(2)}) collective-permute-start(bf16[8,48,384]{2,1,0:T(8,128)(2,1)S(1)} %bitcast.44), channel_id=1, source_target_pairs={{0,8},{4,12},{8,0},{12,4},{16,24},{20,28},{24,16},{28,20},{1,9},{5... | collective-permute-start | bytes 884744 | tf_op jit(solution)/shard_map/ppermute | solution.py:674
  179.1 8.6 %collective-permute-start.14 = (bf16[416,384]{1,0:T(8,128)(2,1)S(1)}, bf16[416,384]{1,0:T(8,128)(2,1)S(1)}, u32[]{:S(2)}, u32[]{:S(2)}) collective-permute-start(bf16[416,384]{1,0:T(8,128)(2,1)S(1)} %slice.224), channel_id=1, source_target_pairs={{0,4},{4,0},{8,12},{12,8},{16,20},{20,16},{24,28},{28,24},{1,5},{5... | collective-permute-start | bytes 958472 | tf_op jit(solution)/shard_map/ppermute | solution.py:674
  179.8 6.8 %collective-permute-start.23 = (bf16[8,48,384]{2,1,0:T(8,128)(2,1)S(1)}, bf16[8,48,384]{2,1,0:T(8,128)(2,1)S(1)}, u32[]{:S(2)}, u32[]{:S(2)}) collective-permute-start(bf16[8,48,384]{2,1,0:T(8,128)(2,1)S(1)} %bitcast.43), channel_id=1, source_target_pairs={{0,2},{1,3},{2,0},{3,1},{4,6},{5,7},{6,4},{7,5},{8,10},{9,11},{10,... | collective-permute-start | bytes 884744 | tf_op jit(solution)/shard_map/ppermute | solution.py:674
  180.8 60.3 %collective-permute-start.12 = (bf16[3,256,768]{2,1,0:T(8,128)(2,1)S(1)}, bf16[3,256,768]{2,1,0:T(8,128)(2,1)S(1)}, u32[]{:S(2)}, u32[]{:S(2)}) collective-permute-start(bf16[3,256,768]{2,1,0:T(8,128)(2,1)S(1)} %copy-done.26), channel_id=1, source_target_pairs={{0,1},{1,0},{2,3},{3,2},{4,5},{5,4},{6,7},{7,6},{8,9},{9,8},{10,11... | collective-permute-start | bytes 3538952 | tf_op jit(solution)/shard_map/ppermute | solution.py:674
  181.0 10.5 %collective-permute-start.47 = (bf16[1,96,768]{2,1,0:T(8,128)(2,1)S(1)}, bf16[1,96,768]{2,1,0:T(8,128)(2,1)S(1)}, u32[]{:S(2)}, u32[]{:S(2)}) collective-permute-start(bf16[1,96,768]{2,1,0:T(8,128)(2,1)S(1)} %slice.349), channel_id=1, source_target_pairs={{0,16},{4,20},{8,24},{12,28},{16,0},{20,4},{24,8},{28,12},{1,17},{... | collective-permute-start | bytes 442376 | tf_op jit(solution)/shard_map/ppermute | solution.py:674
  184.8 7.9 %collective-permute-start.51 = (bf16[2,48,768]{2,1,0:T(8,128)(2,1)S(1)}, bf16[2,48,768]{2,1,0:T(8,128)(2,1)S(1)}, u32[]{:S(2)}, u32[]{:S(2)}) collective-permute-start(bf16[2,48,768]{2,1,0:T(8,128)(2,1)S(1)} %slice.355), channel_id=1, source_target_pairs={{0,4},{4,0},{8,12},{12,8},{16,20},{20,16},{24,28},{28,24},{1,5},{5... | collective-permute-start | bytes 442376 | tf_op jit(solution)/shard_map/ppermute | solution.py:674
  186.6 7.8 %collective-permute-start.30 = (bf16[2,96,384]{2,1,0:T(8,128)(2,1)S(1)}, bf16[2,96,384]{2,1,0:T(8,128)(2,1)S(1)}, u32[]{:S(2)}, u32[]{:S(2)}) collective-permute-start(bf16[2,96,384]{2,1,0:T(8,128)(2,1)S(1)} %slice.325), channel_id=1, source_target_pairs={{0,8},{4,12},{8,0},{12,4},{16,24},{20,28},{24,16},{28,20},{1,9},{5... | collective-permute-start | bytes 442376 | tf_op jit(solution)/shard_map/ppermute | solution.py:674
  187.7 8.1 %collective-permute-start.36 = (bf16[2,48,768]{2,1,0:T(8,128)(2,1)S(1)}, bf16[2,48,768]{2,1,0:T(8,128)(2,1)S(1)}, u32[]{:S(2)}, u32[]{:S(2)}) collective-permute-start(bf16[2,48,768]{2,1,0:T(8,128)(2,1)S(1)} %slice.333), channel_id=1, source_target_pairs={{0,8},{4,12},{8,0},{12,4},{16,24},{20,28},{24,16},{28,20},{1,9},{5... | collective-permute-start | bytes 442376 | tf_op jit(solution)/shard_map/ppermute | solution.py:674
  191.5 5.2 %collective-permute-start.41 = (bf16[2,48,768]{2,1,0:T(8,128)(2,1)S(1)}, bf16[2,48,768]{2,1,0:T(8,128)(2,1)S(1)}, u32[]{:S(2)}, u32[]{:S(2)}) collective-permute-start(bf16[2,48,768]{2,1,0:T(8,128)(2,1)S(1)} %slice.341), channel_id=1, source_target_pairs={{0,2},{1,3},{2,0},{3,1},{4,6},{5,7},{6,4},{7,5},{8,10},{9,11},{10,... | collective-permute-start | bytes 442376 | tf_op jit(solution)/shard_map/ppermute | solution.py:674
  192.7 6.7 %collective-permute-start.19 = (bf16[4,48,384]{2,1,0:T(8,128)(2,1)S(1)}, bf16[4,48,384]{2,1,0:T(8,128)(2,1)S(1)}, u32[]{:S(2)}, u32[]{:S(2)}) collective-permute-start(bf16[4,48,384]{2,1,0:T(8,128)(2,1)S(1)} %slice.310), channel_id=1, source_target_pairs={{0,4},{4,0},{8,12},{12,8},{16,20},{20,16},{24,28},{28,24},{1,5},{5... | collective-permute-start | bytes 442376 | tf_op jit(solution)/shard_map/ppermute | solution.py:674
  194.4 6.6 %collective-permute-start.24 = (bf16[4,48,384]{2,1,0:T(8,128)(2,1)S(1)}, bf16[4,48,384]{2,1,0:T(8,128)(2,1)S(1)}, u32[]{:S(2)}, u32[]{:S(2)}) collective-permute-start(bf16[4,48,384]{2,1,0:T(8,128)(2,1)S(1)} %slice.316), channel_id=1, source_target_pairs={{0,4},{4,0},{8,12},{12,8},{16,20},{20,16},{24,28},{28,24},{1,5},{5... | collective-permute-start | bytes 442376 | tf_op jit(solution)/shard_map/ppermute | solution.py:674
  195.8 6.7 %collective-permute-start.15 = (bf16[224,384]{1,0:T(8,128)(2,1)S(1)}, bf16[224,384]{1,0:T(8,128)(2,1)S(1)}, u32[]{:S(2)}, u32[]{:S(2)}) collective-permute-start(bf16[224,384]{1,0:T(8,128)(2,1)S(1)} %slice.299), channel_id=1, source_target_pairs={{0,8},{4,12},{8,0},{12,4},{16,24},{20,28},{24,16},{28,20},{1,9},{5... | collective-permute-start | bytes 516104 | tf_op jit(solution)/shard_map/ppermute | solution.py:674
  196.7 32.3 %collective-permute-start.48 = (bf16[1,96,768]{2,1,0:T(8,128)(2,1)S(1)}, bf16[1,96,768]{2,1,0:T(8,128)(2,1)S(1)}, u32[]{:S(2)}, u32[]{:S(2)}) collective-permute-start(bf16[1,96,768]{2,1,0:T(8,128)(2,1)S(1)} %add_convert_fusion.17), channel_id=1, source_target_pairs={{0,2},{1,3},{2,0},{3,1},{4,6},{5,7},{6,4},{7,5},{8,10},{9,11},{10,... | collective-permute-start | bytes 442376 | tf_op jit(solution)/shard_map/ppermute | solution.py:674
  199.4 10.4 %collective-permute-start.52 = (bf16[1,48,768]{2,1,0:T(8,128)(2,1)S(1)}, bf16[1,48,768]{2,1,0:T(8,128)(2,1)S(1)}, u32[]{:S(2)}, u32[]{:S(2)}) collective-permute-start(bf16[1,48,768]{2,1,0:T(8,128)(2,1)S(1)} %slice.357), channel_id=1, source_target_pairs={{0,16},{4,20},{8,24},{12,28},{16,0},{20,4},{24,8},{28,12},{1,17},{... | collective-permute-start | bytes 221192 | tf_op jit(solution)/shard_map/ppermute | solution.py:674
  201.0 10.4 %collective-permute-start.31 = (bf16[1,96,384]{2,1,0:T(8,128)(2,1)S(1)}, bf16[1,96,384]{2,1,0:T(8,128)(2,1)S(1)}, u32[]{:S(2)}, u32[]{:S(2)}) collective-permute-start(bf16[1,96,384]{2,1,0:T(8,128)(2,1)S(1)} %slice.327), channel_id=1, source_target_pairs={{0,16},{4,20},{8,24},{12,28},{16,0},{20,4},{24,8},{28,12},{1,17},{... | collective-permute-start | bytes 221192 | tf_op jit(solution)/shard_map/ppermute | solution.py:674
  202.5 9.8 %collective-permute-start.37 = (bf16[1,48,768]{2,1,0:T(8,128)(2,1)S(1)}, bf16[1,48,768]{2,1,0:T(8,128)(2,1)S(1)}, u32[]{:S(2)}, u32[]{:S(2)}) collective-permute-start(bf16[1,48,768]{2,1,0:T(8,128)(2,1)S(1)} %slice.335), channel_id=1, source_target_pairs={{0,16},{4,20},{8,24},{12,28},{16,0},{20,4},{24,8},{28,12},{1,17},{... | collective-permute-start | bytes 221192 | tf_op jit(solution)/shard_map/ppermute | solution.py:674
  209.8 5.3 %collective-permute-start.42 = (bf16[1,48,768]{2,1,0:T(8,128)(2,1)S(1)}, bf16[1,48,768]{2,1,0:T(8,128)(2,1)S(1)}, u32[]{:S(2)}, u32[]{:S(2)}) collective-permute-start(bf16[1,48,768]{2,1,0:T(8,128)(2,1)S(1)} %slice.343), channel_id=1, source_target_pairs={{0,16},{4,20},{8,24},{12,28},{16,0},{20,4},{24,8},{28,12},{1,17},{... | collective-permute-start | bytes 221192 | tf_op jit(solution)/shard_map/ppermute | solution.py:674
  211.4 4.9 %collective-permute-start.20 = (bf16[2,48,384]{2,1,0:T(8,128)(2,1)S(1)}, bf16[2,48,384]{2,1,0:T(8,128)(2,1)S(1)}, u32[]{:S(2)}, u32[]{:S(2)}) collective-permute-start(bf16[2,48,384]{2,1,0:T(8,128)(2,1)S(1)} %slice.312), channel_id=1, source_target_pairs={{0,2},{1,3},{2,0},{3,1},{4,6},{5,7},{6,4},{7,5},{8,10},{9,11},{10,... | collective-permute-start | bytes 221192 | tf_op jit(solution)/shard_map/ppermute | solution.py:674
  212.4 5.8 %collective-permute-start.25 = (bf16[2,48,384]{2,1,0:T(8,128)(2,1)S(1)}, bf16[2,48,384]{2,1,0:T(8,128)(2,1)S(1)}, u32[]{:S(2)}, u32[]{:S(2)}) collective-permute-start(bf16[2,48,384]{2,1,0:T(8,128)(2,1)S(1)} %slice.318), channel_id=1, source_target_pairs={{0,8},{4,12},{8,0},{12,4},{16,24},{20,28},{24,16},{28,20},{1,9},{5... | collective-permute-start | bytes 221192 | tf_op jit(solution)/shard_map/ppermute | solution.py:674
  215.1 14.9 %collective-permute-start.16 = (bf16[128,384]{1,0:T(8,128)(2,1)S(1)}, bf16[128,384]{1,0:T(8,128)(2,1)S(1)}, u32[]{:S(2)}, u32[]{:S(2)}) collective-permute-start(bf16[128,384]{1,0:T(8,128)(2,1)S(1)} %slice.304), channel_id=1, source_target_pairs={{0,16},{4,20},{8,24},{12,28},{16,0},{20,4},{24,8},{28,12},{1,17},{... | collective-permute-start | bytes 294920 | tf_op jit(solution)/shard_map/ppermute | solution.py:674
  216.3 15.0 %collective-permute-start.53 = (bf16[1,48,768]{2,1,0:T(8,128)(2,1)S(1)}, bf16[1,48,768]{2,1,0:T(8,128)(2,1)S(1)}, u32[]{:S(2)}, u32[]{:S(2)}) collective-permute-start(bf16[1,48,768]{2,1,0:T(8,128)(2,1)S(1)} %add_convert_fusion.25), channel_id=1, source_target_pairs={{0,2},{1,3},{2,0},{3,1},{4,6},{5,7},{6,4},{7,5},{8,10},{9,11},{10,... | collective-permute-start | bytes 221192 | tf_op jit(solution)/shard_map/ppermute | solution.py:674
  218.1 4.9 %collective-permute-start.21 = (bf16[1,48,384]{2,1,0:T(8,128)(2,1)S(1)}, bf16[1,48,384]{2,1,0:T(8,128)(2,1)S(1)}, u32[]{:S(2)}, u32[]{:S(2)}) collective-permute-start(bf16[1,48,384]{2,1,0:T(8,128)(2,1)S(1)} %slice.314), channel_id=1, source_target_pairs={{0,16},{4,20},{8,24},{12,28},{16,0},{20,4},{24,8},{28,12},{1,17},{... | collective-permute-start | bytes 110600 | tf_op jit(solution)/shard_map/ppermute | solution.py:674
  223.0 4.9 %collective-permute-start.26 = (bf16[1,48,384]{2,1,0:T(8,128)(2,1)S(1)}, bf16[1,48,384]{2,1,0:T(8,128)(2,1)S(1)}, u32[]{:S(2)}, u32[]{:S(2)}) collective-permute-start(bf16[1,48,384]{2,1,0:T(8,128)(2,1)S(1)} %slice.320), channel_id=1, source_target_pairs={{0,16},{4,20},{8,24},{12,28},{16,0},{20,4},{24,8},{28,12},{1,17},{... | collective-permute-start | bytes 110600 | tf_op jit(solution)/shard_map/ppermute | solution.py:674
  227.8 4.4 %collective-permute-start.32 = (bf16[1,96,384]{2,1,0:T(8,128)(2,1)S(1)}, bf16[1,96,384]{2,1,0:T(8,128)(2,1)S(1)}, u32[]{:S(2)}, u32[]{:S(2)}) collective-permute-start(bf16[1,96,384]{2,1,0:T(8,128)(2,1)S(1)} %add_convert_fusion.29), channel_id=1, source_target_pairs={{0,2},{1,3},{2,0},{3,1},{4,6},{5,7},{6,4},{7,5},{8,10},{9,11},{10,... | collective-permute-start | bytes 221192 | tf_op jit(solution)/shard_map/ppermute | solution.py:674
  229.0 4.5 %collective-permute-start.38 = (bf16[1,48,768]{2,1,0:T(8,128)(2,1)S(1)}, bf16[1,48,768]{2,1,0:T(8,128)(2,1)S(1)}, u32[]{:S(2)}, u32[]{:S(2)}) collective-permute-start(bf16[1,48,768]{2,1,0:T(8,128)(2,1)S(1)} %add_convert_fusion.27), channel_id=1, source_target_pairs={{0,2},{1,3},{2,0},{3,1},{4,6},{5,7},{6,4},{7,5},{8,10},{9,11},{10,... | collective-permute-start | bytes 221192 | tf_op jit(solution)/shard_map/ppermute | solution.py:674
  230.0 4.4 %collective-permute-start.43 = (bf16[1,48,768]{2,1,0:T(8,128)(2,1)S(1)}, bf16[1,48,768]{2,1,0:T(8,128)(2,1)S(1)}, u32[]{:S(2)}, u32[]{:S(2)}) collective-permute-start(bf16[1,48,768]{2,1,0:T(8,128)(2,1)S(1)} %add_convert_fusion.26), channel_id=1, source_target_pairs={{0,2},{1,3},{2,0},{3,1},{4,6},{5,7},{6,4},{7,5},{8,10},{9,11},{10,... | collective-permute-start | bytes 221192 | tf_op jit(solution)/shard_map/ppermute | solution.py:674
  231.3 4.0 %collective-permute-start.22 = (bf16[1,48,384]{2,1,0:T(8,128)(2,1)S(1)}, bf16[1,48,384]{2,1,0:T(8,128)(2,1)S(1)}, u32[]{:S(2)}, u32[]{:S(2)}) collective-permute-start(bf16[1,48,384]{2,1,0:T(8,128)(2,1)S(1)} %add_convert_fusion.34), channel_id=1, source_target_pairs={{0,2},{1,3},{2,0},{3,1},{4,6},{5,7},{6,4},{7,5},{8,10},{9,11},{10,... | collective-permute-start | bytes 110600 | tf_op jit(solution)/shard_map/ppermute | solution.py:674
  232.3 4.0 %collective-permute-start.27 = (bf16[1,48,384]{2,1,0:T(8,128)(2,1)S(1)}, bf16[1,48,384]{2,1,0:T(8,128)(2,1)S(1)}, u32[]{:S(2)}, u32[]{:S(2)}) collective-permute-start(bf16[1,48,384]{2,1,0:T(8,128)(2,1)S(1)} %add_convert_fusion.33), channel_id=1, source_target_pairs={{0,2},{1,3},{2,0},{3,1},{4,6},{5,7},{6,4},{7,5},{8,10},{9,11},{10,... | collective-permute-start | bytes 110600 | tf_op jit(solution)/shard_map/ppermute | solution.py:674
  233.5 7.6 %copy-start.18 = (bf16[768,768]{1,0:T(8,128)(2,1)S(1)}, bf16[768,768]{1,0:T(8,128)(2,1)}, u32[]{:S(2)}) copy-start(bf16[768,768]{1,0:T(8,128)(2,1)} %get-tuple-element.92) | copy-start | bytes 3538948
  233.6 10.6 %collective-permute-start.54 = (bf16[192,768]{1,0:T(8,128)(2,1)S(1)}, bf16[192,768]{1,0:T(8,128)(2,1)S(1)}, u32[]{:S(2)}, u32[]{:S(2)}) collective-permute-start(bf16[192,768]{1,0:T(8,128)(2,1)S(1)} %pad_maximum_fusion.2), channel_id=1, source_target_pairs={{0,1},{1,0},{2,3},{3,2},{4,5},{5,4},{6,7},{7,6},{8,9},{9,8},{10,11... | collective-permute-start | bytes 884744 | tf_op jit(solution)/shard_map/ppermute | solution.py:674
  234.4 3.0 %collective-permute-start.33 = (bf16[96,384]{1,0:T(8,128)(2,1)S(1)}, bf16[96,384]{1,0:T(8,128)(2,1)S(1)}, u32[]{:S(2)}, u32[]{:S(2)}) collective-permute-start(bf16[96,384]{1,0:T(8,128)(2,1)S(1)} %bitcast.41), channel_id=1, source_target_pairs={{0,1},{1,0},{2,3},{3,2},{4,5},{5,4},{6,7},{7,6},{8,9},{9,8},{10,11... | collective-permute-start | bytes 221192 | tf_op jit(solution)/shard_map/ppermute | solution.py:674
  234.5 6.6 %copy-start.12 = (f32[3,256,768]{2,1,0:T(8,128)S(1)}, f32[3,256,768]{2,1,0:T(8,128)}, u32[]{:S(2)}) copy-start(f32[3,256,768]{2,1,0:T(8,128)} %get-tuple-element.117) | copy-start | bytes 7077892
  235.3 7.7 %collective-permute-start.44 = (bf16[96,1536]{1,0:T(8,128)(2,1)S(1)}, bf16[96,1536]{1,0:T(8,128)(2,1)S(1)}, u32[]{:S(2)}, u32[]{:S(2)}) collective-permute-start(bf16[96,1536]{1,0:T(8,128)(2,1)S(1)} %pad_maximum_fusion.1), channel_id=1, source_target_pairs={{0,1},{1,0},{2,3},{3,2},{4,5},{5,4},{6,7},{7,6},{8,9},{9,8},{10,11... | collective-permute-start | bytes 884744 | tf_op jit(solution)/shard_map/ppermute | solution.py:674
  236.3 4.6 %collective-permute-start.17 = (bf16[128,384]{1,0:T(8,128)(2,1)S(1)}, bf16[128,384]{1,0:T(8,128)(2,1)S(1)}, u32[]{:S(2)}, u32[]{:S(2)}) collective-permute-start(bf16[128,384]{1,0:T(8,128)(2,1)S(1)} %pad_maximum_fusion.5), channel_id=1, source_target_pairs={{0,2},{1,3},{2,0},{3,1},{4,6},{5,7},{6,4},{7,5},{8,10},{9,11},{10,... | collective-permute-start | bytes 294920 | tf_op jit(solution)/shard_map/ppermute | solution.py:674
  241.0 4.3 %collective-permute-start.28 = (bf16[320,384]{1,0:T(8,128)(2,1)S(1)}, bf16[320,384]{1,0:T(8,128)(2,1)S(1)}, u32[]{:S(2)}, u32[]{:S(2)}) collective-permute-start(bf16[320,384]{1,0:T(8,128)(2,1)S(1)} %pad_maximum_fusion.3.refs_0_), channel_id=1, source_target_pairs={{0,1},{1,0},{2,3},{3,2},{4,5},{5,4},{6,7},{7,6},{8,9},{9,8},{10,11... | collective-permute-start | bytes 737288 | tf_op jit(solution)/shard_map/ppermute | solution.py:674
  241.8 15.6 %collective-permute-start.13 = (bf16[3,128,768]{2,1,0:T(8,128)(2,1)S(1)}, bf16[3,128,768]{2,1,0:T(8,128)(2,1)S(1)}, u32[]{:S(2)}, u32[]{:S(2)}) collective-permute-start(bf16[3,128,768]{2,1,0:T(8,128)(2,1)S(1)} %get-tuple-element.134), channel_id=1, source_target_pairs={{0,2},{1,3},{2,0},{3,1},{4,6},{5,7},{6,4},{7,5},{8,10},{9,11},{10,... | collective-permute-start | bytes 1769480 | tf_op jit(solution)/shard_map/ppermute | solution.py:674
  (23 other events, 49.6 us)

commit v3 on v2

v3 whole, which is shorter than its diff:
```python
import functools

import jax
import jax.numpy as jnp
from jax import lax
from jax.experimental import pallas as pl
from jax.experimental.pallas import tpu as pltpu
from jax.sharding import PartitionSpec as P

HD = 64
EPSILON = 1e-12
NEGATIVE = -1e30
LOW = jnp.bfloat16
F32 = jnp.float32
LOG2E = 1.4426950408889634
MIB = 1024 * 1024
COST = 5e7
SDS = jax.ShapeDtypeStruct


def contract(a, b, left, right):
    return lax.dot_general(a, b, (((left,), (right,)), ((), ())), preferred_element_type=F32)


def call(kernel, where, inputs, after, thread=None, *, grid, in_specs, out_specs, out_shape, us, name, scratch=(), mib=63):
    plain = thread is None
    thread = thread or ()
    count = len(inputs)
    extra = len(after) + len(thread)
    outs = len(out_shape)
    anywhere = pl.BlockSpec(memory_space=pl.ANY)

    def body(w, *refs):
        at = count + extra
        kernel(w, *refs[:count], *refs[at : at + outs], *refs[at + outs + len(thread) :])

    got = pl.pallas_call(
        body,
        grid_spec=pltpu.PrefetchScalarGridSpec(
            num_scalar_prefetch=1,
            grid=grid,
            in_specs=list(in_specs) + [anywhere] * extra,
            out_specs=list(out_specs) + [anywhere] * len(thread),
            scratch_shapes=list(scratch),
        ),
        out_shape=list(out_shape) + [SDS(v.shape, v.dtype) for v in thread],
        compiler_params=pltpu.CompilerParams(vmem_limit_bytes=mib * MIB),
        cost_estimate=pl.CostEstimate(flops=int(us * COST), bytes_accessed=0, transcendentals=0),
        input_output_aliases={1 + count + i: outs + i for i in range(len(thread))},
        name=name,
    )(where, *inputs, *thread, *after)
    return got if plain else (got[:outs], tuple(got[outs:]))


def gate(where, thread, after):
    return call(
        lambda where: None, where, (), after, thread, grid=(1,), in_specs=[], out_specs=[], out_shape=[], us=0.1,
        name="gate", mib=16,
    )[1]


def col_sum(v):
    return jnp.sum(v, axis=0, keepdims=True)


def as_column(v, rows):
    return jnp.broadcast_to(v[None, :], (rows, v.shape[0])).T


def attend_kernel(
    where, t0, t1, t2, t3, seg_ref, wq, wk, wv, bq, bv,
    x_out, q_out, k_out, v_out, e_out, inv_out, mix_own, mix_sib, bias,
):
    j = lax.rem(pl.program_id(0), 3)
    cols = q_out.shape[1]
    half = mix_own.shape[2]
    heads = e_out.shape[1]

    @pl.when(j == 0)
    def _():
        core = where[0]
        x = jnp.concatenate([t0[0], t1[0], t2[0], t3[0]], axis=0)
        x_out[0] = x
        own_part = lambda ref: jnp.where(core == 0, ref[:cols].astype(F32), ref[cols:].astype(F32))
        qb = as_column(own_part(bq), 128)[:, :1]
        vb = as_column(own_part(bv), 128)[:, :1]
        q_out[0] = (contract(wq[...], x, 0, 1) + qb).astype(LOW)
        k_out[0] = contract(wk[...], x, 0, 1).astype(LOW)
        v_out[0] = (contract(wv[...], x, 0, 1) + vb).astype(LOW)
        me, row = where[2], where[3] + lax.div(pl.program_id(0), 3)
        span = t0.shape[1]
        line = seg_ref[pl.ds(row, 1), :]
        here = [jnp.bitwise_xor(me, r) for r in (0, 2, 1, 3)]
        parts = [line[:, n * span : (n + 1) * span] for n in range(4)]
        pick = lambda q: sum(jnp.where(q == n, part, 0) for n, part in enumerate(parts))
        seg_row = jnp.concatenate([pick(q) for q in here], axis=1).astype(F32)
        seg_col = jnp.broadcast_to(seg_row, (128, seg_row.shape[1])).T[:, :1]
        bias[...] = jnp.where(seg_col == seg_row, 0.0, NEGATIVE)

    for h in range(heads):
        part = pl.ds(pl.multiple_of((j * heads + h) * HD, HD), HD)
        s = contract(k_out[0, part], q_out[0, part], 0, 0) + bias[...]
        top = jnp.max(s, axis=0, keepdims=True)
        e = jnp.exp2((s - top) * (LOG2E * HD**-0.5))
        low = e.astype(LOW)
        inv = 1.0 / col_sum(e)
        e_out[0, h] = low
        inv_out[0, h : h + 1] = inv
        mixed = (contract(v_out[0, part], low, 1, 0) * inv).astype(LOW)
        mix_own[0, h * HD : (h + 1) * HD] = mixed[:, :half]
        mix_sib[0, h * HD : (h + 1) * HD] = mixed[:, half:]


def attend(where, toks, segments, wq, wk, wv, bq, bv, after=()):
    rows, span, width = toks[0].shape
    length = 4 * span
    cols = width // 2
    heads = cols // HD
    step = 2
    tall = step * HD
    row3 = lambda *s: pl.BlockSpec((1,) + s, lambda t, w: (t // 3,) + (0,) * len(s))
    weight = pl.BlockSpec((width, cols), lambda t, w: (0, w[0]), pipeline_mode=pl.Buffered(1))
    bias = pl.BlockSpec((width,), lambda t, w: (0,))
    mix = pl.BlockSpec((1, tall, length // 2), lambda t, w: (t // 3, t % 3, 0))
    return call(
        attend_kernel, where, (*toks, segments, wq, wk, wv, bq, bv), after,
        grid=(3 * rows,),
        in_specs=[row3(span, width)] * 4
        + [pl.BlockSpec(segments.shape, lambda t, w: (0, 0)), weight, weight, weight, bias, bias],
        out_specs=[row3(length, width)]
        + [row3(cols, length)] * 3
        + [
            pl.BlockSpec((1, step, length, length), lambda t, w: (t // 3, t % 3, 0, 0)),
            pl.BlockSpec((1, 8, length), lambda t, w: (t // 3, t % 3, 0)), mix, mix,
        ],
        out_shape=[SDS((rows, length, width), LOW)]
        + [SDS((rows, cols, length), LOW)] * 3
        + [SDS((rows, heads, length, length), LOW), SDS((rows, 24, length), F32)]
        + [SDS((rows, cols, length // 2), LOW)] * 2,
        scratch=[pltpu.VMEM((length, length), F32)],
        us=18,
        name="attend",
    )


def norm_parts(v):
    center = v - jnp.mean(v, axis=1, keepdims=True)
    spread = jnp.mean(center * center, axis=1, keepdims=True)
    scale = lax.rsqrt(spread + EPSILON)
    return center * scale, scale


def norm_back(dn, n, scale):
    return scale * (
        dn - jnp.mean(dn, axis=1, keepdims=True) - n * jnp.mean(dn * n, axis=1, keepdims=True)
    )


def fold(v):
    return jnp.sum(v.reshape(v.shape[0] // 8, 8, v.shape[1]), axis=0)


TALL = 128
HEAD = 4
TAIL = 32


class Puts:
    def __init__(self, sems):
        self.sems = sems
        self.copies = []

    def __call__(self, src, dst):
        copy = pltpu.make_async_copy(src, dst, self.sems.at[len(self.copies)])
        copy.start()
        self.copies.append(copy)

    def shard(self, where, base, s, src, row, rows, cols, dst):
        if dst.shape[1] == rows:
            at = pl.ds(pl.multiple_of(row, 16), rows)
            self(src.at[at, cols], dst.at[where[base + 2 * s]])
            return
        for k in range(2):
            at = pl.ds(pl.multiple_of(row + k * (rows // 2), 16), rows // 2)
            self(src.at[at, cols], dst.at[where[base + 2 * s + k]])

    def wait(self):
        for copy in self.copies:
            copy.wait()


def place(i, block):
    per = block // TALL
    return i // per, pl.ds(pl.multiple_of((i % per) * TALL, TALL), TALL)


def forward_kernel(
    where, mix_own, mix_sib, bo, ag, ash, b1, b2, fg, fsh,
    x_hbm, c0_hbm, c1_hbm, wo_hbm, w1_hbm, w2_hbm,
    sums, out0, out1, dinner_out, norm_out, scale_out, second_out, keep, send, inner_keep, inner_send,
    wo, w1, w2, x, cot, result, act, slope, dinner, norm1, scale1, first_low, second, douter, bias1, partial,
    in_sem, out_sem, *, shards,
):
    core = where[0]
    rows, block, width = x.shape
    span = block // 2
    half = width // 2
    hidden = w1.shape[1]
    chunks = 3
    step = hidden // chunks
    lines = rows * block // TALL
    vec = lambda ref: ref[...].astype(F32)[None, :]
    own_half = pl.ds(pl.multiple_of(core * half, half), half)
    sib_half = pl.ds(pl.multiple_of((1 - core) * half, half), half)
    loads = [
        pltpu.make_async_copy(wo_hbm, wo, in_sem.at[0]),
        pltpu.make_async_copy(x_hbm.at[:, :block], x, in_sem.at[1]),
        pltpu.make_async_copy(c0_hbm, cot.at[:, :span], in_sem.at[2]),
        pltpu.make_async_copy(c1_hbm, cot.at[:, span:], in_sem.at[3]),
    ]
    for j in range(chunks):
        cols = slice(j * step, (j + 1) * step)
        loads.append(pltpu.make_async_copy(w1_hbm.at[:, cols], w1.at[:, cols], in_sem.at[4 + j]))
    loads.append(pltpu.make_async_copy(w2_hbm, w2, in_sem.at[4 + chunks]))
    for k in (0, 1, 4, 5, 6, 7, 2, 3):
        loads[k].start()
    put = Puts(out_sem)
    bias1[...] = vec(b1)
    partial[...] = jnp.zeros_like(partial)
    loads[0].wait()
    for r in range(rows):
        at = slice(r * block, (r + 1) * block)
        second[at] = contract(mix_own[r], wo[own_half, :], 0, 0) + contract(mix_sib[r], wo[sib_half, :], 0, 0)
    loads[1].wait()

    def norm_first(i, _):
        at = pl.ds(pl.multiple_of(i * TALL, TALL), TALL)
        r, line = place(i, block)
        n1, s1 = norm_parts(x[r, line].astype(F32) + (second[at] + vec(bo)))
        norm1[at] = n1
        scale1[at] = jnp.broadcast_to(s1, (TALL, 128))
        first = n1 * vec(ag) + vec(ash)
        first_low[at] = first.astype(LOW)
        second[at] = first + vec(b2)
        return 0

    lax.fori_loop(0, lines, norm_first, 0, unroll=lines)
    put(norm1, norm_out)
    put(scale1, scale_out)
    for j in range(chunks):
        cols = slice(j * step, (j + 1) * step)
        loads[4 + j].wait()
        inner = contract(first_low[...], w1[:, cols], 1, 0) + bias1[:, cols]
        big = 0.5 + 0.5 * lax.erf(inner * 0.7071067811865476)
        bell = jnp.exp2(inner * inner * (-0.5 * LOG2E)) * 0.3989422804014327
        act[:, cols] = (inner * big).astype(LOW)
        slope[:, cols] = (big + inner * bell).astype(LOW)
    loads[4 + chunks].wait()
    second[...] += contract(act[...], w2[...], 1, 0)
    loads[2].wait()
    loads[3].wait()

    def norm_second(i, _):
        at = pl.ds(pl.multiple_of(i * TALL, TALL), TALL)
        r, line = place(i, block)
        n2, s2 = norm_parts(second[at])
        result[r, line] = (n2 * vec(fg) + vec(fsh)).astype(LOW)
        g = cot[r, line].astype(F32)
        d_second = norm_back(g * vec(fg), n2, s2)
        second[at] = d_second
        d_outer = d_second.astype(LOW)
        douter[at] = d_outer
        partial[:, hidden : hidden + width] += fold(d_outer.astype(F32))
        partial[:, hidden + width : hidden + 2 * width] += fold(g * n2)
        partial[:, hidden + 2 * width :] += fold(g)
        return 0

    lax.fori_loop(0, lines, norm_second, 0, unroll=lines)
    put(second, second_out)
    put(result.at[:, :span], out0)
    put(result.at[:, span:], out1)

    for j in range(chunks):
        cols = slice(j * step, (j + 1) * step)
        di = (contract(douter[...], w2[cols, :], 1, 1) * slope[:, cols].astype(F32)).astype(LOW)
        dinner[:, cols] = di
        partial[:, cols] = fold(di.astype(F32))
        put(dinner.at[:, cols], dinner_out.at[:, cols])
    sums[...] = col_sum(partial[...])

    size = hidden // shards
    part = size // 2
    every = slice(0, width)
    for s in range(shards):
        for piece in range(8 // shards):
            high = hidden // 8
            at = slice(s * size + piece * high, s * size + (piece + 1) * high)
            w2[at, :] = contract(act[:, at], douter[...], 0, 0).astype(LOW)
        put.shard(where, HEAD, s, w2, s * size + (1 - core) * part, part, every, send)
        put.shard(where, HEAD, s, w2, s * size + core * part, part, every, keep)
    wide = hidden // 2
    size = width // shards
    for h in range(2):
        side = jnp.where(core == 0, 1 - h, h)
        at = pl.ds(pl.multiple_of(side * wide, 128), wide)
        w1[:, at] = contract(first_low[...], dinner[:, at], 0, 0).astype(LOW)
        dst = (inner_send, inner_keep)[h]
        pieces = dst.shape[0] // shards
        high = size // pieces
        for s in range(shards):
            for k in range(pieces):
                for n in range(2):
                    cols = pl.ds(pl.multiple_of(side * wide + n * width, 128), width)
                    put(
                        w1.at[pl.ds(s * size + k * high, high), cols],
                        dst.at[where[HEAD + 16 + 2 * s + k], pl.ds(n * high, high)],
                    )
    put.wait()


def entries(order, shards):
    if shards == 1:
        return 1
    return 2 * shards if order[-1] == "g" else shards


def forward(where, orders, shards, x, mix_own, mix_sib, c0, c1, wo, w1, w2, bo, ag, ash, b1, b2, fg, fsh, after=()):
    rows, span, width = c0.shape
    half = 2 * span
    hidden = w1.shape[1]
    tokens = rows * half
    whole = lambda v: pl.BlockSpec(v.shape, lambda i, w: (0,) * len(v.shape))
    anywhere = pl.BlockSpec(memory_space=pl.ANY)
    outs = [SDS((1, hidden + 3 * width), F32)]
    outs += [SDS((rows, span, width), LOW)] * 2 + [SDS((tokens, hidden), LOW)]
    outs += [SDS((tokens, width), F32), SDS((tokens, 128), F32), SDS((tokens, width), F32)]
    n = entries(orders[0], shards)
    outs += [SDS((n, hidden // 2 // n, width), LOW)] * 2
    n = entries(orders[1], shards)
    outs += [SDS((n, 2 * width // n, width), LOW)] * 2
    small = (mix_own, mix_sib, bo, ag, ash, b1, b2, fg, fsh)
    low = lambda *s: pltpu.VMEM(s, LOW)
    wide = lambda *s: pltpu.VMEM(s, F32)
    return call(
        functools.partial(forward_kernel, shards=shards), where, small + (x, c0, c1, wo, w1, w2), after,
        grid=(1,),
        in_specs=[whole(v) for v in small] + [anywhere] * 6,
        out_specs=[whole(outs[0])] + [anywhere] * (len(outs) - 1),
        out_shape=outs,
        scratch=[
            low(width, width), low(width, hidden), low(hidden, width),
            low(rows, half, width), low(rows, half, width), low(rows, half, width),
            low(tokens, hidden), low(tokens, hidden), low(tokens, hidden), wide(tokens, width), wide(tokens, 128),
            low(tokens, width), wide(tokens, width), low(tokens, width), wide(1, hidden), wide(8, hidden + 3 * width),
            pltpu.SemaphoreType.DMA((8,)), pltpu.SemaphoreType.DMA((8 + 12 * shards,)),
        ],
        us=27,
        name="forward",
    )


def branch_kernel(
    where, mix_own, mix_sib, ag, sums_in, dinner_hbm, norm_hbm, scale_hbm, second_hbm,
    wo_hbm, w1_hbm,
    sums, dbranch_out, dm_own, dm_sib, o_keep, o_send,
    wo, w1, dm, dinner, norm1, scale1, second, dbranch, ograd, partial,
    in_sem, out_sem, *, shards,
):
    core = where[0]
    rows = mix_own.shape[0]
    block = mix_own.shape[2]
    width, hidden = w1.shape
    half = width // 2
    chunks = 3
    step = hidden // chunks
    lines = rows * block // TALL
    vec = lambda ref: ref[...].astype(F32)[None, :]
    own_half = pl.ds(pl.multiple_of(core * half, half), half)
    sib_half = pl.ds(pl.multiple_of((1 - core) * half, half), half)
    load_j = []
    for j in range(chunks):
        cols = slice(j * step, (j + 1) * step)
        load_j.append(pltpu.make_async_copy(dinner_hbm.at[:, cols], dinner.at[:, cols], in_sem.at[2 * j]))
        load_j.append(pltpu.make_async_copy(w1_hbm.at[:, cols], w1.at[:, cols], in_sem.at[1 + 2 * j]))
        load_j[-2].start()
        load_j[-1].start()
    pairs = ((second_hbm, second), (norm_hbm, norm1), (scale_hbm, scale1), (wo_hbm, wo))
    late = [pltpu.make_async_copy(src, dst, in_sem.at[6 + k]) for k, (src, dst) in enumerate(pairs)]
    for copy in late:
        copy.start()
    put = Puts(out_sem)
    partial[...] = jnp.zeros_like(partial)
    total = None
    for j in range(chunks):
        cols = slice(j * step, (j + 1) * step)
        load_j[2 * j].wait()
        load_j[2 * j + 1].wait()
        if j == chunks - 1:
            late[0].wait()
        value = contract(dinner[:, cols], w1[:, cols], 1, 1)
        total = value if total is None else total + value
    second[...] += total
    for copy in late[1:]:
        copy.wait()

    def norm_attn(i, _):
        at = pl.ds(pl.multiple_of(i * TALL, TALL), TALL)
        d_first = second[at]
        n1 = norm1[at]
        d_branch = norm_back(d_first * vec(ag), n1, scale1[at][:, :1]).astype(LOW)
        dbranch[at] = d_branch
        partial[:, :width] += fold(d_branch.astype(F32))
        partial[:, width : 2 * width] += fold(d_first * n1)
        partial[:, 2 * width : 3 * width] += fold(d_first)
        return 0

    lax.fori_loop(0, lines, norm_attn, 0, unroll=lines)
    put(dbranch, dbranch_out)
    for r in range(rows):
        at = slice(r * block, (r + 1) * block)
        dm[0, r] = contract(wo[own_half, :], dbranch[at], 1, 1).astype(LOW)
        dm[1, r] = contract(wo[sib_half, :], dbranch[at], 1, 1).astype(LOW)
    put(dm.at[1], dm_sib)
    put(dm.at[0], dm_own)
    sums[:, : 3 * width] = col_sum(partial[...])
    sums[:, 3 * width :] = sums_in[...]
    size = width // shards
    for k, mix in enumerate((mix_own, mix_sib)):
        value = contract(mix[0], dbranch[:block], 1, 0)
        for r in range(1, rows):
            value += contract(mix[r], dbranch[r * block : (r + 1) * block], 1, 0)
        ograd[own_half if k == 0 else sib_half, :] = value.astype(LOW)
    for s in range(shards):
        put.shard(where, HEAD + 16 * 2, s, ograd, s * size, size, sib_half, o_send)
        put.shard(where, HEAD + 16 * 2, s, ograd, s * size, size, own_half, o_keep)
    put.wait()


def branch(
    where, orders, shards, mix_own, mix_sib, ag, sums, dinner, norm, scale, second, wo, w1, after=(), thread=()
):
    rows, cols, half = mix_own.shape
    width, hidden = w1.shape
    tokens = rows * half
    whole = lambda v: pl.BlockSpec(v.shape, lambda i, w: (0,) * len(v.shape))
    anywhere = pl.BlockSpec(memory_space=pl.ANY)
    outs = [SDS((1, 6 * width + hidden), F32), SDS((tokens, width), LOW)] + [SDS((rows, cols, half), LOW)] * 2
    n = entries(orders[2], shards)
    outs += [SDS((n, width // n, cols), LOW)] * 2
    small = (mix_own, mix_sib, ag, sums)
    big = (dinner, norm, scale, second, wo, w1)
    low = lambda *s: pltpu.VMEM(s, LOW)
    wide = lambda *s: pltpu.VMEM(s, F32)
    return call(
        functools.partial(branch_kernel, shards=shards), where, small + big, after, thread,
        grid=(1,),
        in_specs=[whole(v) for v in small] + [anywhere] * len(big),
        out_specs=[whole(outs[0])] + [anywhere] * (len(outs) - 1),
        out_shape=outs,
        scratch=[
            low(width, width), low(width, hidden), low(2, rows, cols, half), low(tokens, hidden),
            wide(tokens, width), wide(tokens, 128), wide(tokens, width), low(tokens, width),
            low(width, width), wide(8, 3 * width),
            pltpu.SemaphoreType.DMA((10,)), pltpu.SemaphoreType.DMA((3 + 4 * shards,)),
        ],
        us=13,
        name="branch",
    )


def spread(where, dst, src, order, n, shards, lanes):
    width = src.shape[0]
    size = width // shards
    if shards == 1:
        dst[:width, lanes] = src[...].astype(LOW)
        return
    cut = 2 if order[-1] == "g" else 1
    high = size // cut
    for s in range(shards):
        for k in range(cut):
            start = pl.multiple_of(where[HEAD + 16 * n + 2 * s + k] * high, 16)
            row = s * size + k * high
            dst[pl.ds(start, high), lanes] = src[row : row + high].astype(LOW)


def pair_back(step_refs, grads, acc, bias, first):
    x_ref, q_ref, k_ref, v_ref, e_ref, inv_ref, mix_own, mix_sib, dm_own, dm_sib = step_refs
    scale = HD**-0.5
    tall = q_ref.shape[1]
    for h in range(tall // HD):
        part = slice(h * HD, (h + 1) * HD)
        mixed = jnp.concatenate([mix_own[0, part], mix_sib[0, part]], axis=1)
        dm = jnp.concatenate([dm_own[0, part], dm_sib[0, part]], axis=1)
        d_out = dm.astype(F32) * inv_ref[0, h : h + 1]
        delta = col_sum(d_out * mixed.astype(F32))
        d_low = d_out.astype(LOW)
        e = e_ref[0, h]
        dp = contract(v_ref[0, part], d_low, 0, 0)
        ds = (e.astype(F32) * (dp - delta)).astype(LOW)
        at = lambda n: slice(n * tall + h * HD, n * tall + (h + 1) * HD)
        grads[at(0)] = (contract(k_ref[0, part], ds, 1, 0) * scale).astype(LOW)
        grads[at(1)] = (contract(q_ref[0, part], ds, 1, 1) * scale).astype(LOW)
        grads[at(2)] = contract(d_low, e, 1, 1).astype(LOW)
    value = contract(x_ref[0], grads[...], 0, 1)
    ones = jnp.ones((8, x_ref.shape[1]), LOW)
    sums = contract(ones, grads[...], 1, 1)
    acc[...] = jnp.where(first, value, acc[...] + value)
    bias[...] = jnp.where(first, sums, bias[...] + sums)


def send_off(packed, keep, send, sems):
    put = Puts(sems)
    half = keep.shape[0]
    put(packed.at[half:], send)
    put(packed.at[:half], keep)
    put.wait()


def pair_kernel(where, *refs, orders, shards, with_o):
    step_refs, refs = refs[:10], refs[10:]
    if with_o:
        o_keep, o_got, *refs = refs
    d_out, bias, keep, send, acc, packed, sems = refs
    r = pl.program_id(0)
    pair_back(step_refs, d_out.at[0], acc, bias, r == 0)

    @pl.when(r == pl.num_programs(0) - 1)
    def _():
        cols = acc.shape[1]
        spread(where, packed, acc, orders[2], 2, shards, slice(0, cols))
        if with_o:
            packed[:, cols:] = (o_keep[...].astype(F32) + o_got[...].astype(F32)).astype(LOW)
        send_off(packed, keep, send, sems)


def last_pair_kernel(
    where, *refs, orders, shards,
):
    step_refs, refs = refs[:10], refs[10:]
    d0, d1, bias0, bias1, dbranch, wq, wk, wv, vectors, *refs = refs
    in_own, in_out, keep, send, grads, dq, dk, dv, acc, bias, packed, sems = refs
    r = pl.program_id(0)
    pair_back(step_refs, grads, acc, bias, r == 0)
    tall = grads.shape[0] // 3
    for n, d in enumerate((dq, dk, dv)):
        part = slice(n * tall, (n + 1) * tall)
        d[:tall] = d0[0, part]
        d[tall : 2 * tall] = d1[0, part]
        d[2 * tall :] = grads[part]
    back = contract(dq[...], wq[...], 0, 1)
    back = back + contract(dk[...], wk[...], 0, 1) + contract(dv[...], wv[...], 0, 1)
    half = back.shape[0] // 2
    in_own[0] = (back[:half] + dbranch[0].astype(F32)).astype(LOW)
    in_out[0] = back[half:].astype(LOW)

    @pl.when(r == pl.num_programs(0) - 1)
    def _():
        core = where[0]
        width, cols = acc.shape
        spread(where, packed, acc, orders[3], 3, shards, slice(0, cols))
        lines = [vectors[:, n * cols : (n + 1) * cols] for n in range(vectors.shape[1] // cols)]
        zero = jnp.zeros((1, cols), F32)
        for n in (2, 0):
            part = slice(n * tall, (n + 1) * tall)
            line = jnp.concatenate([bias0[:1, part], bias1[:1, part], bias[:1, part]], axis=1)
            lines += [jnp.where(core == c, line, zero) for c in range(2)]
        lines.append(jnp.zeros((TAIL - len(lines), cols), F32))
        packed[width:] = jnp.concatenate(lines, axis=0).astype(LOW)
        send_off(packed, keep, send, sems)


def pair_specs(p, x, attention):
    rows, cols, length = attention[0].shape
    width = x.shape[2]
    heads = cols // HD
    step = 2
    tall = step * HD
    row3 = lambda *s: pl.BlockSpec((1,) + s, lambda r, w: (r,) + (0,) * len(s))
    big = pl.BlockSpec((1, tall, length), lambda r, w: (r, p, 0))
    small = pl.BlockSpec((1, tall, length // 2), lambda r, w: (r, p, 0))
    inv = pl.BlockSpec((1, 8, length), lambda r, w: (r, p, 0))
    specs = [row3(length, width)] + [big] * 3
    specs += [pl.BlockSpec((1, step, length, length), lambda r, w: (r, p, 0, 0)), inv]
    return specs + [small] * 4, row3


def pair_grads(where, orders, shards, p, x, attention, o=(), after=(), thread=()):
    rows, cols, length = attention[0].shape
    width = x.shape[2]
    specs, row3 = pair_specs(p, x, attention)
    whole = lambda v: pl.BlockSpec(v.shape, lambda r, w: (0,) * len(v.shape))
    anywhere = pl.BlockSpec(memory_space=pl.ANY)
    total = cols + sum(v.shape[1] for v in o[:1])
    outs = [SDS((rows, cols, length), LOW), SDS((8, cols), F32)] + [SDS((width // 2, total), LOW)] * 2
    return call(
        functools.partial(pair_kernel, orders=orders, shards=shards, with_o=bool(o)), where,
        (x, *attention, *o), after, thread,
        grid=(rows,),
        in_specs=specs + [whole(v) for v in o],
        out_specs=[row3(cols, length), whole(outs[1]), anywhere, anywhere],
        out_shape=outs,
        scratch=[pltpu.VMEM((width, cols), F32), pltpu.VMEM((width, total), LOW), pltpu.SemaphoreType.DMA((2,))],
        us=8,
        name="pair_grads",
    )


def last_pair_grads(where, orders, shards, x, attention, pairs, dbranch, weights, vectors, after=(), thread=()):
    rows, cols, length = attention[0].shape
    width = x.shape[2]
    specs, row3 = pair_specs(2, x, attention)
    whole = lambda v: pl.BlockSpec(v.shape, lambda r, w: (0,) * len(v.shape))
    weight = pl.BlockSpec((width, cols), lambda r, w: (0, w[0]), pipeline_mode=pl.Buffered(1))
    anywhere = pl.BlockSpec(memory_space=pl.ANY)
    low = lambda *s: pltpu.VMEM(s, LOW)
    half = width // 2
    (d0, bias0), (d1, bias1) = pairs
    return call(
        functools.partial(last_pair_kernel, orders=orders, shards=shards), where,
        (x, *attention, d0, d1, bias0, bias1, dbranch, *weights, vectors), after, thread,
        grid=(rows,),
        in_specs=specs
        + [row3(cols, length)] * 2
        + [whole(bias0), whole(bias1), row3(length // 2, width), weight, weight, weight, whole(vectors)],
        out_specs=[row3(length // 2, width)] * 2 + [anywhere] * 2,
        out_shape=[SDS((rows, length // 2, width), LOW)] * 2
        + [SDS((half, cols), LOW), SDS((half + TAIL, cols), LOW)],
        scratch=[low(cols, length)] * 4
        + [pltpu.VMEM((width, cols), F32), pltpu.VMEM((8, cols), F32), low(width + TAIL, cols)]
        + [pltpu.SemaphoreType.DMA((2,))],
        us=10,
        name="last_pair_grads",
    )


def round_kernel(where, *refs, groups):
    add = lambda a, b: (a.astype(F32) + b.astype(F32)).astype(LOW)
    ins = sum(2 * n + tail for n, tail, _ in groups)
    outs = list(refs[ins:])
    refs = list(refs[:ins])
    for n, tail, split in groups:
        keeps, gots = refs[:n], refs[n : 2 * n]
        sent = refs[2 * n] if tail else None
        refs = refs[2 * n + tail :]
        out_keep = outs.pop(0)
        out_send = outs.pop(0) if split or tail else None
        at = 0
        for keep, got in zip(keeps, gots):
            rows, cols = keep.shape
            half = out_keep.shape[0]
            lanes = slice(at, at + cols)
            at += cols
            out_keep[:, lanes] = add(keep[:half], got[:half])
            if split:
                out_send[: rows - half, lanes] = add(keep[half:], got[half:rows])
            elif tail:
                out_send[:rows, lanes] = out_keep[...]
        if tail:
            end = lambda ref: ref[ref.shape[0] - TAIL :]
            out_send[out_send.shape[0] - TAIL :] = add(end(sent), end(gots[0]))


def next_round(where, groups, after=(), thread=()):
    whole = lambda v: pl.BlockSpec(v.shape, lambda i, w: (0,) * len(v.shape))
    ins, outs, form, counts = [], [], [], []
    for keeps, gots, sent, split in groups:
        tail = sent is not None
        ins += [*keeps, *gots] + ([sent] if tail else [])
        rows = keeps[0].shape[0]
        cols = sum(v.shape[1] for v in keeps)
        half = rows // 2 if split else rows
        new = [SDS((half, cols), LOW)]
        if split or tail:
            new.append(SDS((half + (TAIL if tail else 0), cols), LOW))
        outs += new
        counts.append(len(new))
        form.append((len(keeps), int(tail), split))
    got, thread = call(
        functools.partial(round_kernel, groups=tuple(form)), where, ins, after, thread,
        grid=(1,),
        in_specs=[whole(v) for v in ins],
        out_specs=[whole(v) for v in outs],
        out_shape=outs,
        us=1,
        name="next_round",
        mib=16,
    )
    results = []
    for n in counts:
        results.append(tuple(got[:n]))
        got = got[n:]
    return results, thread


def finish_kernel(where, ab_mine, c_mine, ab_got, c_got, gq, gk, gv, go, *outs):
    core = where[0]
    b = where[1]
    size, width = gq.shape
    cols = width // 2
    tall = cols // 3

    def both(ref, at, mine, got):
        mine, got = mine.astype(F32), got.astype(F32)
        n = mine.shape[1]
        ref[:, at : at + n] = jnp.where(core == 0, mine, got)
        ref[:, cols + at : cols + at + n] = jnp.where(core == 0, got, mine)

    for n, ref in enumerate((gq, gk, gv)):
        for p in range(3):
            mine, got = (c_mine, c_got) if p == 2 else (ab_mine, ab_got)
            at = n * tall + (width if p == 1 else 0)
            both(ref, p * tall, mine[:size, at : at + tall], got[:size, at : at + tall])
    both(go, 0, ab_mine[:, cols:width], ab_got[:, cols:width])
    total = c_mine[size:].astype(F32) + c_got[size:].astype(F32)
    row = 0
    for ref in outs:
        n = ref.shape[0]
        parts = n * (width // size) // cols
        line = jnp.concatenate([total[row + i : row + i + 1] for i in range(parts)], axis=1)
        row += parts
        picked = jnp.zeros((1, n), F32)
        for s in range(width // size):
            picked = jnp.where(b == s, line[:, s * n : (s + 1) * n], picked)
        ref[...] = picked[0]


def finish(where, mine, got, lengths):
    whole = lambda *s: pl.BlockSpec(s, lambda i, w: (0,) * len(s))
    size = mine[0].shape[0]
    width = 2 * mine[1].shape[1]
    return call(
        finish_kernel, where, (*mine, *got), (),
        grid=(1,),
        in_specs=[whole(*v.shape) for v in (*mine, *got)],
        out_specs=[whole(size, width)] * 4 + [whole(n) for n in lengths],
        out_shape=[SDS((size, width), F32)] * 4 + [SDS((n,), F32) for n in lengths],
        us=2,
        name="finish",
        mib=16,
    )


def swap(v, axis, mask, size):
    return lax.ppermute(v, axis, [(i, i ^ mask) for i in range(size)])


def add_low(a, b):
    return (a.astype(F32) + b.astype(F32)).astype(LOW)


def fix(v):
    return lax.optimization_barrier(v)


ORDERS = ("x1y2g", "1xy2g", "y1x2g", "x12y")
BITS = {"x": 0, "1": 1, "2": 2}


def solution(mesh):
    batch_size = mesh.shape["batch"]
    blk_size = mesh.shape["blk"]
    direct = batch_size == 8
    shards = batch_size if direct else 1

    def blk_swap(v, mask):
        return swap(v, "blk", mask, blk_size)

    def hop(v, step):
        if step in BITS:
            return swap(v, "batch", 1 << BITS[step], batch_size)
        return blk_swap(v, 2)

    def split_sum(keep, got):
        half = keep.shape[0] // 2
        return fix(add_low(keep[half:], got[half:])), fix(add_low(keep[:half], got[:half]))

    def per_device(
        tokens, segment_ids, query_weight, query_bias, key_weight, value_weight, value_bias,
        output_weight, output_bias, attn_gain, attn_shift, inner_weight, inner_bias,
        outer_weight, outer_bias, final_gain, final_shift, cotangent,
    ):
        count, span, width = tokens.shape
        rows = count // 2
        me = lax.axis_index("blk")
        b = lax.axis_index("batch")
        core = me & 1
        y = (me >> 1) & 1

        index = jnp.arange(16, dtype=jnp.int32)
        moved = {k: ((index >> (1 + n)) ^ (b >> n)) & 1 for k, n in BITS.items()}
        moved["y"] = (index & 1) ^ y
        maps = []
        for order in ORDERS:
            steps = order[:-1]
            maps.append(sum(moved[k] << (len(steps) - 1 - i) for i, k in enumerate(steps)))
        if not direct:
            maps = [jnp.zeros_like(v) for v in maps]
        where = jnp.concatenate([jnp.stack([core, b, me, y * rows]).astype(jnp.int32)] + maps)

        def mine(v):
            return lax.dynamic_slice_in_dim(v, y * rows, rows, 0)

        def other(v):
            return lax.dynamic_slice_in_dim(v, (1 - y) * rows, rows, 0)

        def halves(own, got, axis):
            return jnp.where(
                core == 0,
                jnp.concatenate([own, got], axis=axis),
                jnp.concatenate([got, own], axis=axis),
            )

        def join_rows(keep, got):
            return jnp.where(
                y == 0, jnp.concatenate([keep, got], axis=0), jnp.concatenate([got, keep], axis=0)
            )

        t1 = blk_swap(other(tokens), 2)
        t0 = mine(tokens)
        t2 = blk_swap(t0, 1)
        t3 = blk_swap(t1, 1)
        x, q, k, v, e, inv, mix_own, mix_out = attend(
            where, (t0, t1, t2, t3), segment_ids,
            query_weight, key_weight, value_weight, query_bias, value_bias,
        )
        c1 = blk_swap(other(cotangent), 2)
        c0 = mine(cotangent)
        mix_sib = blk_swap(mix_out, 1)
        flat = lambda g: g.reshape(-1, g.shape[-1])
        (
            sums, out0, out1, dinner, norm, scale, second, outer_keep, outer_send, inner_keep, inner_send,
        ) = forward(
            where, ORDERS, shards, x, mix_own, mix_sib, c0, c1, output_weight, inner_weight, outer_weight,
            output_bias, attn_gain, attn_shift, inner_bias, outer_bias, final_gain, final_shift,
        )
        outer_keep = flat(outer_keep)
        got = blk_swap(flat(outer_send), 1)
        out_got = blk_swap(out1, 2)
        outer = split_sum(outer_keep, got)
        (inner_send,) = gate(where, (flat(inner_send),), outer)
        inner = split_sum(flat(inner_keep), blk_swap(inner_send, 1))

        def hops():
            if not direct:
                return (), ()
            steps = (ORDERS[0][stage], ORDERS[1][stage])
            return (hop(outer[0], steps[0]), hop(inner[0], steps[1])), (outer[1], inner[1])

        stage = 0
        got, keeps = hops()
        (vectors, dbranch, dm_own, dm_out, o_keep, o_send), through = branch(
            where, ORDERS, shards, mix_own, mix_sib, attn_gain, sums, dinner, norm, scale,
            second, output_weight, inner_weight, after=(outer[0], inner[0]), thread=(out0,) + keeps,
        )
        out0, keeps = through[0], through[1:]
        result = join_rows(out0, out_got)
        dm_sib = blk_swap(dm_out, 1)
        o_got = blk_swap(flat(o_send), 1)
        dbranch = dbranch.reshape(rows, 2 * span, width)
        attention = (q, k, v, e, inv, mix_own, mix_out, dm_own, dm_sib)
        (d0, bias0, a_keep, a_send), keeps = pair_grads(
            where, ORDERS, shards, 0, x, attention, (flat(o_keep), o_got), after=(out_got,), thread=keeps
        )
        if direct:
            outer, inner = (split_sum(keep, g) for keep, g in zip(keeps, got))
        stage = 1
        got, keeps = hops()
        if direct:
            got += (hop(a_send, ORDERS[2][0]),)
            keeps += (a_keep,)
        (d1, bias1, b_keep, b_send), keeps = pair_grads(
            where, ORDERS, shards, 1, x, attention, after=(outer[0], inner[0]), thread=keeps
        )
        if direct:
            got += (hop(b_send, ORDERS[2][0]),)
            keeps += (b_keep,)
        (in_own, in_out, c_keep, c_send), keeps = last_pair_grads(
            where, ORDERS, shards, x, attention, ((d0, bias0), (d1, bias1)), dbranch,
            (query_weight, key_weight, value_weight), vectors, thread=keeps,
        )
        in_sum = fix(add_low(in_own, blk_swap(in_out, 1)))

        def join(v, axis):
            v = fix(v)
            return halves(v, blk_swap(v, 1), axis).astype(F32)

        def add_y(g):
            return fix(add_low(g, blk_swap(g, 2)))

        if direct:

            cells = lambda v: v.reshape(4, -1, width)
            pairs = [add_low(cells(keep), cells(g)) for keep, g in zip(keeps[:2], got[:2])]
            both = lambda a, b: fix(jnp.concatenate([p[a:b] for p in pairs], axis=1).reshape(-1, width))
            ffn, ffn_send = both(0, 2), both(2, 4)
            ((ab, ab_send),), (c_send, ffn_send) = next_round(
                where, [(keeps[2:], got[2:], None, True)], after=(ffn,), thread=(c_send, ffn_send)
            )
            c_got, ffn_got, ab_got = hop(c_send, "x"), hop(ffn_send, "y"), hop(ab_send, "1")
            ffn_send, ffn = split_sum(ffn, ffn_got)
            ((c, c_send), (ab, ab_send)), (ffn_send, in_sum) = next_round(
                where, [((c_keep,), (c_got,), c_send, True), ((ab,), (ab_got,), None, True)],
                after=(ffn,), thread=(ffn_send, in_sum),
            )
            in_got = blk_swap(in_sum[:, span:], 2)
            c_got, ffn_got, ab_got = hop(c_send, "1"), hop(ffn_send, "2"), hop(ab_send, "x")
            ((c, c_send), (ab, ab_send)), _ = next_round(
                where, [((c,), (c_got,), c_send, True), ((ab,), (ab_got,), None, True)], after=(in_got,)
            )
            input_grad = join_rows(in_sum[:, :span], in_got)
            ffn = fix(add_low(ffn, ffn_got))
            c_got, ab_got = hop(c_send, "2"), hop(ab_send, "2")
            ((_, c), (ab,)), (ffn,) = next_round(
                where, [((c,), (c_got,), c_send, False), ((ab,), (ab_got,), None, False)], thread=(ffn,)
            )
            c_got, ab_got, ffn_got = hop(c, "y"), hop(ab, "y"), hop(ffn, "y")
            c = fix(add_low(c, c_got))
            ab = fix(jnp.concatenate([jnp.where(y == 0, ab, ab_got), jnp.where(y == 0, ab_got, ab)], axis=0))
            pair = jnp.stack([ffn, ffn_got])
            ffn = fix(jnp.where(y == 0, pair, pair[::-1]))
            ffn_got = blk_swap(ffn, 1)
            high = ffn.shape[1] // 2
            part = lambda v: v[:, :high].reshape(-1, width)
            outer_done = halves(part(ffn), part(ffn_got), 0).astype(F32)

            def columns(v):
                v = v[:, high:].reshape(2, 2, -1, width)
                return jnp.concatenate([v[:, 0], v[:, 1]], axis=2).reshape(-1, 2 * width)

            inner_done = halves(columns(ffn), columns(ffn_got), 1).astype(F32)
            lengths = [n // shards for n in (width,) * 3 + (inner_weight.shape[1],) + (width,) * 5]
            query_done, key_done, value_done, output_done, *vecs = finish(
                where, (ab, c), tuple(blk_swap(g, 1) for g in (ab, c)), lengths
            )
        else:
            input_grad = join_rows(in_sum[:, :span], blk_swap(in_sum[:, span:], 2))

            def whole(v):
                return add_y(lax.psum_scatter(v, "batch", scatter_dimension=0, tiled=True))

            join_halves = lambda pair: jnp.concatenate([pair[1], pair[0]], axis=0)
            outer_part = join_halves(outer)
            outer_done = whole(halves(outer_part, blk_swap(outer_part, 1), 0)).astype(F32)
            inner_part = join_halves(inner)
            inner_part = jnp.concatenate([inner_part[:width], inner_part[width:]], axis=1)
            inner_done = join(whole(inner_part), 1)
            cols = width // 2
            tall = cols // 3
            whole_a = jnp.concatenate([a_keep, a_send], axis=0)
            groups = (whole_a, jnp.concatenate([b_keep, b_send], axis=0))
            groups += (jnp.concatenate([c_keep, c_send[: c_keep.shape[0]]], axis=0),)
            query_done, key_done, value_done = (
                join(whole(jnp.concatenate([g[:, n * tall : (n + 1) * tall] for g in groups], axis=1)), 1)
                for n in range(3)
            )
            output_done = join(whole(whole_a[:, cols:]), 1)
            total = lax.psum(c_send[c_keep.shape[0] :].astype(F32), ("batch", "blk")).reshape(-1)
            vecs = []
            at = 0
            for n in (width,) * 3 + (inner_weight.shape[1],) + (width,) * 5:
                part = total[at : at + n].reshape(batch_size, n // batch_size)
                vecs.append(lax.dynamic_index_in_dim(part, b, 0, keepdims=False))
                at += n
        g_ob, g_ag, g_as, g_b1, g_b2, g_fg, g_fs, g_vb, g_qb = vecs
        return (
            result, input_grad, query_done, g_qb, key_done, value_done, g_vb, output_done, g_ob,
            g_ag, g_as, inner_done, g_b1, outer_done, g_b2, g_fg, g_fs,
        )

    tok = P("batch", "blk", None)
    mat = P("batch", None)
    vec = P("batch")
    return jax.shard_map(
        per_device,
        mesh=mesh,
        in_specs=(tok, P("batch", None)) + (P(),) * 15 + (tok,),
        out_specs=(
            tok, tok, mat, vec, mat, mat, vec, mat, vec, vec, vec, mat, vec, mat, vec, vec, vec,
        ),
        check_vma=False,
    )
```

time: 264 us -> 237 us (0.90)
  starting transfers between devices: 52.7 us -> 30.8 us
  local copies, waits for them, and re-layouts: 16.6 us -> 8.7 us
  other arithmetic: 12 us -> 19.4 us
  Pallas kernels: 118 us -> 113 us
    ppermute x55 -> x32, starting transfers between devices: 52.7 us -> 30.8 us  [swap(): return lax.ppermute(v, axis, [(i, i ^ mask) for i in range(size)])]
    convert_element_type x40 -> x10, other arithmetic: 5.9 us -> 13.1 us  [add_low(): return (a.astype(F32) + b.astype(F32)).astype(LOW)]
    pallas_call x10 -> x12, Pallas kernels: 118 us -> 113 us  [call(): pl.pallas_call(body, grid_spec=pltpu.PrefetchScalarGridSpec(num_scalar_pr...]
    unnamed x64 -> x42, local copies, waits for them, and re-layouts: 5.6 us -> 2.2 us
    slice x32 -> x9, local copies, waits for them, and re-layouts: 6.16 us -> 3.22 us  [the longest x2 1.93 us: split_sum(): keep[half:]]
    ppermute x55 -> x32, waiting for transfers between devices: 57.9 us -> 60.3 us  [swap(): return lax.ppermute(v, axis, [(i, i ^ mask) for i in range(size)])]
  transfers between devices with their start and end apart: 55 -> 32, of which waited for: 23 -> 14; matrix products, arithmetic and copies ran while one was open for 8% -> 8% of each run, Pallas kernels for 35% -> 32%
where the time goes in v3:
time: 237 us; the launch traced here: 234 us
  Pallas kernels  113 us (48%)
  waiting for transfers between devices  60.3 us (25%)
  starting transfers between devices  30.8 us (13%)
  other arithmetic  19.4 us (8%)
  local copies, waits for them, and re-layouts  8.7 us (4%)
    pallas_call x12, Pallas kernels, call(): pl.pallas_call(body, grid_spec=pltpu.PrefetchScalarGridSpec(num_scalar_pr...  113 us
    ppermute x32, waiting for transfers between devices, swap(): return lax.ppermute(v, axis, [(i, i ^ mask) for i in range(size)])  60.3 us
    ppermute x32, starting transfers between devices, swap(): return lax.ppermute(v, axis, [(i, i ^ mask) for i in range(size)])  30.8 us
    convert_element_type x10, other arithmetic, add_low(): return (a.astype(F32) + b.astype(F32)).astype(LOW)  13.1 us
  transfers between devices with their start and end apart: 32, of which 14 were waited for; matrix products, arithmetic and copies ran while one was open for 8% of the time, Pallas kernels for 32%

profile of v3, /device:TPU:0, one launch (start us, length us, event | category | flops | bytes accessed | tf_op | source)
XLA Modules:
  0.0 233.9 jit_solution(2158518553720886452)
XLA Ops:
  0.7 1.4 constant_dynamic-slice_fusion.2
  2.1 3.0 %collective-permute-start = (bf16[3,128,768]{2,1,0:T(8,128)(2,1)S(1)}, bf16[3,128,768]{2,1,0:T(8,128)(2,1)S(1)}, u32[]{:S(2)}, u32[]{:S(2)}) collective-permute-start(bf16[3,128,768]{2,1,0:T(8,128)(2,1)S(1)} %get-tuple-element.193), channel_id=1, source_target_pairs={{0,2},{1,3},{2,0},{3,1},{4,6},{5,7},{6,4},{7,5},{8,10},{9,11},{10,... | collective-permute-start | bytes 1769480 | tf_op jit(solution)/shard_map/ppermute | solution.py:744
  5.1 13.3 %collective-permute-done.refs_1_ = bf16[3,128,768]{2,1,0:T(8,128)(2,1)S(1)} collective-permute-done((bf16[3,128,768]{2,1,0:T(8,128)(2,1)S(1)}, bf16[3,128,768]{2,1,0:T(8,128)(2,1)S(1)}, u32[]{:S(2)}, u32[]{:S(2)}) %collective-permute-start) | collective-permute-done | bytes 589856 | tf_op jit(solution)/shard_map/ppermute | solution.py:744
  18.5 1.3 constant_dynamic-slice_fusion
  19.7 1.8 collective-permute-start.4
  21.5 0.6 concatenate.50.w
  22.1 0.8 copy-done.19
  23.0 19.8 %attend.1 = (bf16[3,512,768]{2,1,0:T(8,128)(2,1)}, bf16[3,384,512]{2,1,0:T(8,128)(2,1)}, bf16[3,384,512]{2,1,0:T(8,128)(2,1)}, bf16[3,384,512]{2,1,0:T(8,128)(2,...) custom-call(s32[68]{0:T(128)} %concatenate.50.w, ...), custom_call_target="tpu_custom_call" | custom-call | flops 900000000 | tf_op jit(solution)/shard_map/attend/pallas_call | solution.py:37
  42.9 2.1 collective-permute-done.3.refs_1_
  45.0 0.8 copy-done.11
  45.8 35.6 %forward.1 = (f32[1,5376]{1,0:T(1,128)}, bf16[3,128,768]{2,1,0:T(8,128)(2,1)}, bf16[3,128,768]{2,1,0:T(8,128)(2,1)}, bf16[768,3072]{1,0:T(8,128)(2,1)}, f32[768,...) custom-call(s32[68]{0:T(128)} %concatenate.50.w, ...), custom_call_target="tpu_custom_call" | custom-call | flops 1350000000 | tf_op jit(solution)/shard_map/forward/pallas_call | solution.py:37
  81.6 1.8 fusion.8
  83.4 2.8 %collective-permute-done.5 = bf16[1536,768]{1,0:T(8,128)(2,1)S(1)} collective-permute-done((bf16[1536,768]{1,0:T(8,128)(2,1)}, bf16[1536,768]{1,0:T(8,128)(2,1)S(1)}, u32[]{:S(2)}, u32[]{:S(2)}) %collective-permute-start.5) | collective-permute-done | bytes 2359328 | tf_op jit(solution)/shard_map/ppermute | solution.py:744
  86.2 2.2 fusion.1
  88.4 0.5 gate.1
  89.0 0.5 copy-done
  89.5 1.5 collective-permute-start.10
  91.2 0.6 collective-permute-start.7
  91.8 2.1 collective-permute-done.6
  93.9 2.2 fusion
  96.1 1.6 collective-permute-start.11
  97.7 15.8 %branch.1 = (f32[1,7680]{1,0:T(1,128)}, bf16[768,768]{1,0:T(8,128)(2,1)}, bf16[3,384,256]{2,1,0:T(8,128)(2,1)}, bf16[3,384,256]{2,1,0:T(8,128)(2,1)}, bf16[16,48...) custom-call(s32[68]{0:T(128)} %concatenate.50.w, ...), custom_call_target="tpu_custom_call", output_to_operand_aliasing={{6}: (11, {}), {7}: (12, {}), {8}: (13, {})} | custom-call | flops 650000000 | tf_op jit(solution)/shard_map/branch/pallas_call | solution.py:37
  113.6 0.5 collective-permute-start.9
  114.1 1.8 collective-permute-done.8.refs_9_
  115.8 0.9 collective-permute-done.9.refs_11_
  116.7 10.9 %pair_grads.2 = (bf16[3,384,512]{2,1,0:T(8,128)(2,1)}, f32[8,384]{1,0:T(8,128)}, bf16[384,768]{1,0:T(8,128)(2,1)}, bf16[384,768]{1,0:T(8,128)(2,1)}, bf16[768,768]{1,0:T(8,128)(2,1)}, /*index=5*/bf16[768,768]{1,0:T(8,128)(2,1)}) custom-call(s32[68]{0:T(128)} %concatenate.50.w, ...), custom_call_target="tpu_custom_call", output_to_operand_aliasing={{4}: (13, {}), {5}: (14, {})} | custom-call | flops 400000000 | tf_op jit(solution)/shard_map/pair_grads/pallas_call | solution.py:37
  127.7 3.0 %add_convert_fusion.4 = (bf16[384,768]{1,0:T(8,128)(2,1)}, bf16[384,768]{1,0:T(8,128)(2,1)}) fusion(bf16[768,768]{1,0:T(8,128)(2,1)} %collective-permute-done.10, bf16[768,768]{1,0:T(8,128)(2,1)} %get-tuple-element.123), kind=kLoop, calls=%fused_computation.14 | loop fusion | flops 2359296 | bytes 3538944 | tf_op jit(solution)/shard_map/convert_element_type | solution.py:748
  131.4 2.6 %add_convert_fusion.3 = (bf16[384,768]{1,0:T(8,128)(2,1)}, bf16[384,768]{1,0:T(8,128)(2,1)}) fusion(bf16[768,768]{1,0:T(8,128)(2,1)} %collective-permute-done.11, bf16[768,768]{1,0:T(8,128)(2,1)S(1)} %copy-done.8), kind=kLoop, calls=%fused_computation.13 | loop fusion | flops 2359296 | bytes 3538944 | tf_op jit(solution)/shard_map/convert_element_type | solution.py:748
  134.0 1.7 collective-permute-start.15
  135.7 10.2 %pair_grads.3 = (bf16[3,384,512]{2,1,0:T(8,128)(2,1)}, f32[8,384]{1,0:T(8,128)}, bf16[384,384]{1,0:T(8,128)(2,1)}, bf16[384,384]{1,0:T(8,128)(2,1)}, bf16[384,76...) custom-call(s32[68]{0:T(128)} %concatenate.50.w, ...), custom_call_target="tpu_custom_call", output_to_operand_aliasing={{4}: (11, {}), {5}: (12, {}), {6}: (13, {})} | custom-call | flops 400000000 | tf_op jit(solution)/shard_map/pair_grads/pallas_call | solution.py:37
  146.0 15.2 %last_pair_grads.1 = (bf16[3,256,768]{2,1,0:T(8,128)(2,1)}, bf16[3,256,768]{2,1,0:T(8,128)(2,1)}, bf16[384,384]{1,0:T(8,128)(2,1)}, bf16[416,384]{1,0:T(8,128)(2...) custom-call(s32[68]{0:T(128)} %concatenate.50.w, ...), custom_call_target="tpu_custom_call", output_to_operand_aliasing={{4}: (20, {}), {5}: (21, {}), {6}: (22, {}), {7}: (23, {})} | custom-call | flops 500000000 | tf_op jit(solution)/shard_map/last_pair_grads/pallas_call | solution.py:37
  161.2 1.6 collective-permute-start.13
  162.8 1.4 add_convert_fusion.2
  164.3 1.2 add_convert_fusion.1
  165.7 4.9 %collective-permute-done.13.refs_3_ = bf16[384,384]{1,0:T(8,128)(2,1)S(1)} collective-permute-done((bf16[384,384]{1,0:T(8,128)(2,1)S(1)}, bf16[384,384]{1,0:T(8,128)(2,1)S(1)}, u32[]{:S(2)}, u32[]{:S(2)}) %collective-permute-start.13) | collective-permute-done | bytes 294944 | tf_op jit(solution)/shard_map/ppermute | solution.py:744
  170.7 0.7 next_round.4
  171.4 1.6 collective-permute-start.18
  173.0 1.6 collective-permute-start.17
  174.6 0.5 collective-permute-start.16
  175.5 10.9 %collective-permute-done.18 = bf16[384,768]{1,0:T(8,128)(2,1)S(1)} collective-permute-done((bf16[384,768]{1,0:T(8,128)(2,1)S(1)}, bf16[384,768]{1,0:T(8,128)(2,1)S(1)}, u32[]{:S(2)}, u32[]{:S(2)}) %collective-permute-start.18) | collective-permute-done | bytes 589856 | tf_op jit(solution)/shard_map/ppermute | solution.py:744
  186.6 0.7 next_round.5
  187.3 1.1 fusion.9
  188.4 1.5 collective-permute-start.20
  189.9 2.6 %collective-permute-start.25 = (bf16[192,768]{1,0:T(8,128)(2,1)S(1)}, bf16[192,768]{1,0:T(8,128)(2,1)S(1)}, u32[]{:S(2)}, u32[]{:S(2)}) collective-permute-start(bf16[192,768]{1,0:T(8,128)(2,1)S(1)} %get-tuple-element.158), channel_id=1, source_target_pairs={{0,16},{4,20},{8,24},{12,28},{16,0},{20,4},{24,8},{28,12},{1,17},{... | collective-permute-start | bytes 884744 | tf_op jit(solution)/shard_map/ppermute | solution.py:744
  192.5 0.5 collective-permute-start.22
  193.1 1.6 collective-permute-start.21
  194.6 2.5 %maximum_select_fusion = bf16[6,128,768]{2,1,0:T(8,128)(2,1)} fusion(bf16[3,128,768]{2,1,0:T(8,128)(2,1)} %collective-permute-done.7.refs_14_, bf16[3,128,768]{2,1,0:T(8,128)(2,1)S(1)} %copy-done.12, pred[]{:T(512)S(6)} %eq.4), kind=kLoop, calls=%fused_computation.9 | loop fusion | flops 1769472 | bytes 2359297 | tf_op jit(solution)/shard_map/jit(_where)/select_n | solution.py:814
  197.1 4.0 %collective-permute-done.21.refs_1_ = bf16[224,384]{1,0:T(8,128)(2,1)S(1)} collective-permute-done((bf16[224,384]{1,0:T(8,128)(2,1)S(1)}, bf16[224,384]{1,0:T(8,128)(2,1)S(1)}, u32[]{:S(2)}, u32[]{:S(2)}) %collective-permute-start.21) | collective-permute-done | bytes 172064 | tf_op jit(solution)/shard_map/ppermute | solution.py:744
  201.1 1.5 collective-permute-done.20.refs_5_
  202.6 0.6 next_round.6
  203.3 2.7 %collective-permute-start.24 = (bf16[48,1152]{1,0:T(8,128)(2,1)S(1)}, bf16[48,1152]{1,0:T(8,128)(2,1)S(1)}, u32[]{:S(2)}, u32[]{:S(2)}) collective-permute-start(bf16[48,1152]{1,0:T(8,128)(2,1)S(1)} %get-tuple-element.157), channel_id=1, source_target_pairs={{0,16},{4,20},{8,24},{12,28},{16,0},{20,4},{24,8},{28,12},{1,17},{... | collective-permute-start | bytes 331784 | tf_op jit(solution)/shard_map/ppermute | solution.py:744
  206.3 7.3 %collective-permute-done.23.refs_1_ = bf16[128,384]{1,0:T(8,128)(2,1)S(1)} collective-permute-done((bf16[128,384]{1,0:T(8,128)(2,1)S(1)}, bf16[128,384]{1,0:T(8,128)(2,1)S(1)}, u32[]{:S(2)}, u32[]{:S(2)}) %collective-permute-start.23) | collective-permute-done | bytes 98336 | tf_op jit(solution)/shard_map/ppermute | solution.py:744
  213.6 1.2 next_round.7
  214.8 1.5 collective-permute-start.27
  216.3 1.2 maximum_select_fusion.1
  217.5 0.5 collective-permute-start.30
  218.0 1.5 collective-permute-start.26
  219.5 1.0 collective-permute-done.27
  220.7 6.0 %collective-permute-done.26 = bf16[48,1152]{1,0:T(8,128)(2,1)S(1)} collective-permute-done((bf16[48,1152]{1,0:T(8,128)(2,1)S(1)}, bf16[48,1152]{1,0:T(8,128)(2,1)S(1)}, u32[]{:S(2)}, u32[]{:S(2)}) %collective-permute-start.26) | collective-permute-done | bytes 110624 | tf_op jit(solution)/shard_map/ppermute | solution.py:744
  226.9 0.6 collective-permute-start.28
  227.6 1.6 collective-permute-done.28.refs_2_
  229.2 2.1 finish.1
  231.4 1.1 fusion.5
  232.5 1.2 fusion.4
  (88 shorter events, 3.2 us)
Async XLA Ops:
  0.7 17.8 %copy-start.17 = (bf16[6,128,768]{2,1,0:T(8,128)(2,1)S(1)}, bf16[6,128,768]{2,1,0:T(8,128)(2,1)}, u32[]{:S(2)}) copy-start(bf16[6,128,768]{2,1,0:T(8,128)(2,1)} %param.35) | copy-start | bytes 3538948
  2.1 17.6 %copy-start.15 = (bf16[3,128,768]{2,1,0:T(8,128)(2,1)}, bf16[3,128,768]{2,1,0:T(8,128)(2,1)S(1)}, u32[]{:S(2)}) copy-start(bf16[3,128,768]{2,1,0:T(8,128)(2,1)S(1)} %get-tuple-element.194.refs_0_) | copy-start | bytes 1769476
  2.1 16.4 %collective-permute-start = (bf16[3,128,768]{2,1,0:T(8,128)(2,1)S(1)}, bf16[3,128,768]{2,1,0:T(8,128)(2,1)S(1)}, u32[]{:S(2)}, u32[]{:S(2)}) collective-permute-start(bf16[3,128,768]{2,1,0:T(8,128)(2,1)S(1)} %get-tuple-element.193), channel_id=1, source_target_pairs={{0,2},{1,3},{2,0},{3,1},{4,6},{5,7},{6,4},{7,5},{8,10},{9,11},{10,... | collective-permute-start | bytes 1769480 | tf_op jit(solution)/shard_map/ppermute | solution.py:744
  5.1 17.0 %collective-permute-start.1 = (bf16[3,128,768]{2,1,0:T(8,128)(2,1)S(1)}, bf16[3,128,768]{2,1,0:T(8,128)(2,1)S(1)}, u32[]{:S(2)}, u32[]{:S(2)}) collective-permute-start(bf16[3,128,768]{2,1,0:T(8,128)(2,1)S(1)} %get-tuple-element.194.refs_0_), channel_id=1, source_target_pairs={{0,1},{1,0},{2,3},{3,2},{4,5},{5,4},{6,7},{7,6},{8,9},{9,8},{10,11... | collective-permute-start | bytes 1769480 | tf_op jit(solution)/shard_map/ppermute | solution.py:744
  18.5 1.3 copy-start.18
  18.5 4.5 %collective-permute-start.2 = (bf16[3,128,768]{2,1,0:T(8,128)(2,1)S(1)}, bf16[3,128,768]{2,1,0:T(8,128)(2,1)}, u32[]{:S(2)}, u32[]{:S(2)}) collective-permute-start(bf16[3,128,768]{2,1,0:T(8,128)(2,1)S(1)} %collective-permute-done.refs_1_), channel_id=1, source_target_pairs={{0,1},{1,0},{2,3},{3,2},{4,5},{5,4},{6,7},{7,6},{8,9},{9,8},{10,11... | collective-permute-start | bytes 1769480 | tf_op jit(solution)/shard_map/ppermute | solution.py:744
  19.7 23.1 %collective-permute-start.4 = (bf16[3,128,768]{2,1,0:T(8,128)(2,1)}, bf16[3,128,768]{2,1,0:T(8,128)(2,1)}, u32[]{:S(2)}, u32[]{:S(2)}) collective-permute-start(bf16[3,128,768]{2,1,0:T(8,128)(2,1)} %get-tuple-element.191), channel_id=1, source_target_pairs={{0,2},{1,3},{2,0},{3,1},{4,6},{5,7},{6,4},{7,5},{8,10},{9,11},{10,... | collective-permute-start | bytes 1769480 | tf_op jit(solution)/shard_map/ppermute | solution.py:744
  22.1 0.8 copy-start.19
  42.7 2.3 collective-permute-start.3
  45.0 0.8 copy-start.11
  81.4 4.8 %collective-permute-start.5 = (bf16[1536,768]{1,0:T(8,128)(2,1)}, bf16[1536,768]{1,0:T(8,128)(2,1)S(1)}, u32[]{:S(2)}, u32[]{:S(2)}) collective-permute-start(bf16[1536,768]{1,0:T(8,128)(2,1)} %bitcast.57), channel_id=1, source_target_pairs={{0,1},{1,0},{2,3},{3,2},{4,5},{5,4},{6,7},{7,6},{8,9},{9,8},{10,11... | collective-permute-start | bytes 7077896 | tf_op jit(solution)/shard_map/ppermute | solution.py:744
  86.2 2.2 copy-start.2
  86.2 2.2 copy-start.6
  88.4 1.0 copy-start
  88.4 2.7 %copy-start.13 = (bf16[16,96,768]{2,1,0:T(8,128)(2,1)S(1)}, bf16[16,96,768]{2,1,0:T(8,128)(2,1)}, u32[]{:S(2)}) copy-start(bf16[16,96,768]{2,1,0:T(8,128)(2,1)} %get-tuple-element.107) | copy-start | bytes 7077892
  89.4 4.5 %collective-permute-start.6 = (bf16[1536,768]{1,0:T(8,128)(2,1)S(1)}, bf16[1536,768]{1,0:T(8,128)(2,1)S(1)}, u32[]{:S(2)}, u32[]{:S(2)}) collective-permute-start(bf16[1536,768]{1,0:T(8,128)(2,1)S(1)} %gate.1), channel_id=1, source_target_pairs={{0,1},{1,0},{2,3},{3,2},{4,5},{5,4},{6,7},{7,6},{8,9},{9,8},{10,11... | collective-permute-start | bytes 7077896 | tf_op jit(solution)/shard_map/ppermute | solution.py:744
  89.5 38.1 %collective-permute-start.10 = (bf16[768,768]{1,0:T(8,128)(2,1)}, bf16[768,768]{1,0:T(8,128)(2,1)}, u32[]{:S(2)}, u32[]{:S(2)}) collective-permute-start(bf16[768,768]{1,0:T(8,128)(2,1)} %get-tuple-element.183.refs_1_.refs_13_), channel_id=1, source_target_pairs={{0,4},{4,0},{8,12},{12,8},{16,20},{20,16},{24,28},{28,24},{1,5},{5... | collective-permute-start | bytes 3538952 | tf_op jit(solution)/shard_map/ppermute | solution.py:744
  91.2 22.8 %collective-permute-start.7 = (bf16[3,128,768]{2,1,0:T(8,128)(2,1)}, bf16[3,128,768]{2,1,0:T(8,128)(2,1)}, u32[]{:S(2)}, u32[]{:S(2)}) collective-permute-start(bf16[3,128,768]{2,1,0:T(8,128)(2,1)} %get-tuple-element.110), channel_id=1, source_target_pairs={{0,2},{1,3},{2,0},{3,1},{4,6},{5,7},{6,4},{7,5},{8,10},{9,11},{10,... | collective-permute-start | bytes 1769480 | tf_op jit(solution)/shard_map/ppermute | solution.py:744
  96.1 35.3 %collective-permute-start.11 = (bf16[768,768]{1,0:T(8,128)(2,1)}, bf16[768,768]{1,0:T(8,128)(2,1)}, u32[]{:S(2)}, u32[]{:S(2)}) collective-permute-start(bf16[768,768]{1,0:T(8,128)(2,1)} %get-tuple-element.179.refs_14_), channel_id=1, source_target_pairs={{0,8},{4,12},{8,0},{12,4},{16,24},{20,28},{24,16},{28,20},{1,9},{5... | collective-permute-start | bytes 3538952 | tf_op jit(solution)/shard_map/ppermute | solution.py:744
  113.5 2.3 %collective-permute-start.8 = (bf16[3,384,256]{2,1,0:T(8,128)(2,1)}, bf16[3,384,256]{2,1,0:T(8,128)(2,1)S(1)}, u32[]{:S(2)}, u32[]{:S(2)}) collective-permute-start(bf16[3,384,256]{2,1,0:T(8,128)(2,1)} %get-tuple-element.117), channel_id=1, source_target_pairs={{0,1},{1,0},{2,3},{3,2},{4,5},{5,4},{6,7},{7,6},{8,9},{9,8},{10,11... | collective-permute-start | bytes 1769480 | tf_op jit(solution)/shard_map/ppermute | solution.py:744
  113.6 3.2 %collective-permute-start.9 = (bf16[768,384]{1,0:T(8,128)(2,1)}, bf16[768,384]{1,0:T(8,128)(2,1)}, u32[]{:S(2)}, u32[]{:S(2)}) collective-permute-start(bf16[768,384]{1,0:T(8,128)(2,1)} %bitcast.58), channel_id=1, source_target_pairs={{0,1},{1,0},{2,3},{3,2},{4,5},{5,4},{6,7},{7,6},{8,9},{9,8},{10,11... | collective-permute-start | bytes 1769480 | tf_op jit(solution)/shard_map/ppermute | solution.py:744
  115.8 0.9 copy-start.10
  127.7 3.7 %copy-start.8 = (bf16[768,768]{1,0:T(8,128)(2,1)S(1)}, bf16[768,768]{1,0:T(8,128)(2,1)}, u32[]{:S(2)}) copy-start(bf16[768,768]{1,0:T(8,128)(2,1)} %get-tuple-element.124) | copy-start | bytes 3538948
  130.7 32.1 %collective-permute-start.14 = (bf16[384,768]{1,0:T(8,128)(2,1)}, bf16[384,768]{1,0:T(8,128)(2,1)}, u32[]{:S(2)}, u32[]{:S(2)}) collective-permute-start(bf16[384,768]{1,0:T(8,128)(2,1)} %get-tuple-element.177.refs_13_), channel_id=1, source_target_pairs={{0,8},{4,12},{8,0},{12,4},{16,24},{20,28},{24,16},{28,20},{1,9},{5... | collective-permute-start | bytes 1769480 | tf_op jit(solution)/shard_map/ppermute | solution.py:744
  131.2 34.6 %collective-permute-start.12 = (bf16[384,768]{1,0:T(8,128)(2,1)}, bf16[384,768]{1,0:T(8,128)(2,1)S(1)}, u32[]{:S(2)}, u32[]{:S(2)}) collective-permute-start(bf16[384,768]{1,0:T(8,128)(2,1)} %get-tuple-element.138), channel_id=1, source_target_pairs={{0,2},{1,3},{2,0},{3,1},{4,6},{5,7},{6,4},{7,5},{8,10},{9,11},{10,... | collective-permute-start | bytes 1769480 | tf_op jit(solution)/shard_map/ppermute | solution.py:744
  134.0 30.4 %collective-permute-start.15 = (bf16[384,768]{1,0:T(8,128)(2,1)}, bf16[384,768]{1,0:T(8,128)(2,1)}, u32[]{:S(2)}, u32[]{:S(2)}) collective-permute-start(bf16[384,768]{1,0:T(8,128)(2,1)} %get-tuple-element.175.refs_14_), channel_id=1, source_target_pairs={{0,4},{4,0},{8,12},{12,8},{16,20},{20,16},{24,28},{28,24},{1,5},{5... | collective-permute-start | bytes 1769480 | tf_op jit(solution)/shard_map/ppermute | solution.py:744
  145.9 15.3 %copy-start.20 = (bf16[384,384]{1,0:T(8,128)(2,1)S(1)}, bf16[384,384]{1,0:T(8,128)(2,1)}, u32[]{:S(2)}) copy-start(bf16[384,384]{1,0:T(8,128)(2,1)} %get-tuple-element.139) | copy-start | bytes 884740
  161.2 14.0 %collective-permute-start.19 = (bf16[3,256,768]{2,1,0:T(8,128)(2,1)}, bf16[3,256,768]{2,1,0:T(8,128)(2,1)S(1)}, u32[]{:S(2)}, u32[]{:S(2)}) collective-permute-start(bf16[3,256,768]{2,1,0:T(8,128)(2,1)} %get-tuple-element.148), channel_id=1, source_target_pairs={{0,1},{1,0},{2,3},{3,2},{4,5},{5,4},{6,7},{7,6},{8,9},{9,8},{10,11... | collective-permute-start | bytes 3538952 | tf_op jit(solution)/shard_map/ppermute | solution.py:744
  161.2 9.4 %collective-permute-start.13 = (bf16[384,384]{1,0:T(8,128)(2,1)S(1)}, bf16[384,384]{1,0:T(8,128)(2,1)S(1)}, u32[]{:S(2)}, u32[]{:S(2)}) collective-permute-start(bf16[384,384]{1,0:T(8,128)(2,1)S(1)} %copy-done.20), channel_id=1, source_target_pairs={{0,2},{1,3},{2,0},{3,1},{4,6},{5,7},{6,4},{7,5},{8,10},{9,11},{10,... | collective-permute-start | bytes 884744 | tf_op jit(solution)/shard_map/ppermute | solution.py:744
  162.8 1.5 copy-start.9
  165.6 5.1 %copy-start.1 = (bf16[384,768]{1,0:T(8,128)(2,1)S(1)}, bf16[384,768]{1,0:T(8,128)(2,1)}, u32[]{:S(2)}) copy-start(bf16[384,768]{1,0:T(8,128)(2,1)} %get-tuple-element.136.refs_0_) | copy-start | bytes 1769476
  165.6 5.1 %copy-start.3 = (bf16[416,384]{1,0:T(8,128)(2,1)S(1)}, bf16[416,384]{1,0:T(8,128)(2,1)}, u32[]{:S(2)}) copy-start(bf16[416,384]{1,0:T(8,128)(2,1)} %get-tuple-element.140.refs_4_) | copy-start | bytes 958468
  165.6 5.0 %copy-start.4 = (bf16[384,384]{1,0:T(8,128)(2,1)S(1)}, bf16[384,384]{1,0:T(8,128)(2,1)}, u32[]{:S(2)}) copy-start(bf16[384,384]{1,0:T(8,128)(2,1)} %get-tuple-element.137.refs_1_) | copy-start | bytes 884740
  165.6 5.0 %copy-start.7 = (s32[68]{0:T(128)S(1)}, s32[68]{0:T(128)}, u32[]{:S(2)}) copy-start(s32[68]{0:T(128)} %concatenate.50.w) | copy-start | bytes 820
  170.7 4.5 %copy-start.16 = (bf16[3,256,768]{2,1,0:T(8,128)(2,1)S(1)}, bf16[3,256,768]{2,1,0:T(8,128)(2,1)}, u32[]{:S(2)}) copy-start(bf16[3,256,768]{2,1,0:T(8,128)(2,1)} %get-tuple-element.147) | copy-start | bytes 3538948
  171.4 14.9 %collective-permute-start.18 = (bf16[384,768]{1,0:T(8,128)(2,1)S(1)}, bf16[384,768]{1,0:T(8,128)(2,1)S(1)}, u32[]{:S(2)}, u32[]{:S(2)}) collective-permute-start(bf16[384,768]{1,0:T(8,128)(2,1)S(1)} %get-tuple-element.146), channel_id=1, source_target_pairs={{0,2},{1,3},{2,0},{3,1},{4,6},{5,7},{6,4},{7,5},{8,10},{9,11},{10,... | collective-permute-start | bytes 1769480 | tf_op jit(solution)/shard_map/ppermute | solution.py:744
  173.0 13.5 %collective-permute-start.17 = (bf16[192,1152]{1,0:T(8,128)(2,1)S(1)}, bf16[192,1152]{1,0:T(8,128)(2,1)S(1)}, u32[]{:S(2)}, u32[]{:S(2)}) collective-permute-start(bf16[192,1152]{1,0:T(8,128)(2,1)S(1)} %get-tuple-element.145), channel_id=1, source_target_pairs={{0,8},{4,12},{8,0},{12,4},{16,24},{20,28},{24,16},{28,20},{1,9},{5... | collective-permute-start | bytes 1327112 | tf_op jit(solution)/shard_map/ppermute | solution.py:744
  174.6 11.9 %collective-permute-start.16 = (bf16[416,384]{1,0:T(8,128)(2,1)S(1)}, bf16[416,384]{1,0:T(8,128)(2,1)S(1)}, u32[]{:S(2)}, u32[]{:S(2)}) collective-permute-start(bf16[416,384]{1,0:T(8,128)(2,1)S(1)} %get-tuple-element.143.refs_2_), channel_id=1, source_target_pairs={{0,4},{4,0},{8,12},{12,8},{16,20},{20,16},{24,28},{28,24},{1,5},{5... | collective-permute-start | bytes 958472 | tf_op jit(solution)/shard_map/ppermute | solution.py:744
  175.5 11.1 %copy-start.5 = (bf16[384,384]{1,0:T(8,128)(2,1)S(1)}, bf16[384,384]{1,0:T(8,128)(2,1)}, u32[]{:S(2)}) copy-start(bf16[384,384]{1,0:T(8,128)(2,1)} %get-tuple-element.135.refs_0_) | copy-start | bytes 884740
  187.3 7.3 %copy-start.12 = (bf16[3,128,768]{2,1,0:T(8,128)(2,1)S(1)}, bf16[3,128,768]{2,1,0:T(8,128)(2,1)}, u32[]{:S(2)}) copy-start(bf16[3,128,768]{2,1,0:T(8,128)(2,1)} %get-tuple-element.109) | copy-start | bytes 1769476
  188.4 14.2 %collective-permute-start.20 = (bf16[3,128,768]{2,1,0:T(8,128)(2,1)}, bf16[3,128,768]{2,1,0:T(8,128)(2,1)S(1)}, u32[]{:S(2)}, u32[]{:S(2)}) collective-permute-start(bf16[3,128,768]{2,1,0:T(8,128)(2,1)} %get-tuple-element.188), channel_id=1, source_target_pairs={{0,2},{1,3},{2,0},{3,1},{4,6},{5,7},{6,4},{7,5},{8,10},{9,11},{10,... | collective-permute-start | bytes 1769480 | tf_op jit(solution)/shard_map/ppermute | solution.py:744
  189.9 16.3 %collective-permute-start.25 = (bf16[192,768]{1,0:T(8,128)(2,1)S(1)}, bf16[192,768]{1,0:T(8,128)(2,1)S(1)}, u32[]{:S(2)}, u32[]{:S(2)}) collective-permute-start(bf16[192,768]{1,0:T(8,128)(2,1)S(1)} %get-tuple-element.158), channel_id=1, source_target_pairs={{0,16},{4,20},{8,24},{12,28},{16,0},{20,4},{24,8},{28,12},{1,17},{... | collective-permute-start | bytes 884744 | tf_op jit(solution)/shard_map/ppermute | solution.py:744
  192.5 8.6 %collective-permute-start.22 = (bf16[96,1152]{1,0:T(8,128)(2,1)S(1)}, bf16[96,1152]{1,0:T(8,128)(2,1)S(1)}, u32[]{:S(2)}, u32[]{:S(2)}) collective-permute-start(bf16[96,1152]{1,0:T(8,128)(2,1)S(1)} %get-tuple-element.153), channel_id=1, source_target_pairs={{0,4},{4,0},{8,12},{12,8},{16,20},{20,16},{24,28},{28,24},{1,5},{5... | collective-permute-start | bytes 663560 | tf_op jit(solution)/shard_map/ppermute | solution.py:744
  193.1 8.1 %collective-permute-start.21 = (bf16[224,384]{1,0:T(8,128)(2,1)S(1)}, bf16[224,384]{1,0:T(8,128)(2,1)S(1)}, u32[]{:S(2)}, u32[]{:S(2)}) collective-permute-start(bf16[224,384]{1,0:T(8,128)(2,1)S(1)} %get-tuple-element.151.refs_2_), channel_id=1, source_target_pairs={{0,8},{4,12},{8,0},{12,4},{16,24},{20,28},{24,16},{28,20},{1,9},{5... | collective-permute-start | bytes 516104 | tf_op jit(solution)/shard_map/ppermute | solution.py:744
  203.3 13.1 %copy-start.14 = (bf16[3,128,768]{2,1,0:T(8,128)(2,1)S(1)}, bf16[3,128,768]{2,1,0:T(8,128)(2,1)}, u32[]{:S(2)}) copy-start(bf16[3,128,768]{2,1,0:T(8,128)(2,1)} %get-tuple-element.187) | copy-start | bytes 1769476
  203.3 10.3 %collective-permute-start.24 = (bf16[48,1152]{1,0:T(8,128)(2,1)S(1)}, bf16[48,1152]{1,0:T(8,128)(2,1)S(1)}, u32[]{:S(2)}, u32[]{:S(2)}) collective-permute-start(bf16[48,1152]{1,0:T(8,128)(2,1)S(1)} %get-tuple-element.157), channel_id=1, source_target_pairs={{0,16},{4,20},{8,24},{12,28},{16,0},{20,4},{24,8},{28,12},{1,17},{... | collective-permute-start | bytes 331784 | tf_op jit(solution)/shard_map/ppermute | solution.py:744
  205.9 7.7 %collective-permute-start.23 = (bf16[128,384]{1,0:T(8,128)(2,1)S(1)}, bf16[128,384]{1,0:T(8,128)(2,1)S(1)}, u32[]{:S(2)}, u32[]{:S(2)}) collective-permute-start(bf16[128,384]{1,0:T(8,128)(2,1)S(1)} %get-tuple-element.155.refs_2_), channel_id=1, source_target_pairs={{0,16},{4,20},{8,24},{12,28},{16,0},{20,4},{24,8},{28,12},{1,17},{... | collective-permute-start | bytes 294920 | tf_op jit(solution)/shard_map/ppermute | solution.py:744
  214.8 5.7 %collective-permute-start.27 = (bf16[128,384]{1,0:T(8,128)(2,1)S(1)}, bf16[128,384]{1,0:T(8,128)(2,1)S(1)}, u32[]{:S(2)}, u32[]{:S(2)}) collective-permute-start(bf16[128,384]{1,0:T(8,128)(2,1)S(1)} %get-tuple-element.160), channel_id=1, source_target_pairs={{0,2},{1,3},{2,0},{3,1},{4,6},{5,7},{6,4},{7,5},{8,10},{9,11},{10,... | collective-permute-start | bytes 294920 | tf_op jit(solution)/shard_map/ppermute | solution.py:744
  217.5 9.1 %collective-permute-start.30 = (bf16[192,768]{1,0:T(8,128)(2,1)S(1)}, bf16[192,768]{1,0:T(8,128)(2,1)S(1)}, u32[]{:S(2)}, u32[]{:S(2)}) collective-permute-start(bf16[192,768]{1,0:T(8,128)(2,1)S(1)} %get-tuple-element.170), channel_id=1, source_target_pairs={{0,2},{1,3},{2,0},{3,1},{4,6},{5,7},{6,4},{7,5},{8,10},{9,11},{10,... | collective-permute-start | bytes 884744 | tf_op jit(solution)/shard_map/ppermute | solution.py:744
  218.0 8.6 %collective-permute-start.26 = (bf16[48,1152]{1,0:T(8,128)(2,1)S(1)}, bf16[48,1152]{1,0:T(8,128)(2,1)S(1)}, u32[]{:S(2)}, u32[]{:S(2)}) collective-permute-start(bf16[48,1152]{1,0:T(8,128)(2,1)S(1)} %get-tuple-element.159), channel_id=1, source_target_pairs={{0,2},{1,3},{2,0},{3,1},{4,6},{5,7},{6,4},{7,5},{8,10},{9,11},{10,... | collective-permute-start | bytes 331784 | tf_op jit(solution)/shard_map/ppermute | solution.py:744
  220.6 7.0 %collective-permute-start.29 = (bf16[128,384]{1,0:T(8,128)(2,1)S(1)}, bf16[128,384]{1,0:T(8,128)(2,1)S(1)}, u32[]{:S(2)}, u32[]{:S(2)}) collective-permute-start(bf16[128,384]{1,0:T(8,128)(2,1)S(1)} %add_convert_fusion.10.refs_1_), channel_id=1, source_target_pairs={{0,1},{1,0},{2,3},{3,2},{4,5},{5,4},{6,7},{7,6},{8,9},{9,8},{10,11... | collective-permute-start | bytes 294920 | tf_op jit(solution)/shard_map/ppermute | solution.py:744
  226.8 4.5 %collective-permute-start.31 = (bf16[2,192,768]{2,1,0:T(8,128)(2,1)S(1)}, bf16[2,192,768]{2,1,0:T(8,128)(2,1)S(1)}, u32[]{:S(2)}, u32[]{:S(2)}) collective-permute-start(bf16[2,192,768]{2,1,0:T(8,128)(2,1)S(1)} %reverse_select_fusion), channel_id=1, source_target_pairs={{0,1},{1,0},{2,3},{3,2},{4,5},{5,4},{6,7},{7,6},{8,9},{9,8},{10,11... | collective-permute-start | bytes 1769480 | tf_op jit(solution)/shard_map/ppermute | solution.py:744
  226.9 2.3 collective-permute-start.28

commit v4 on v3

--- a/solution.py
+++ b/solution.py
@@ -71,13 +71,12 @@
     where, t0, t1, t2, t3, seg_ref, wq, wk, wv, bq, bv,
     x_out, q_out, k_out, v_out, e_out, inv_out, mix_own, mix_sib, bias,
 ):
-    j = lax.rem(pl.program_id(0), 3)
+    j = 0
     cols = q_out.shape[1]
     half = mix_own.shape[2]
     heads = e_out.shape[1]
 
-    @pl.when(j == 0)
-    def _():
+    if True:
         core = where[0]
         x = jnp.concatenate([t0[0], t1[0], t2[0], t3[0]], axis=0)
         x_out[0] = x
@@ -87,7 +86,7 @@
         q_out[0] = (contract(wq[...], x, 0, 1) + qb).astype(LOW)
         k_out[0] = contract(wk[...], x, 0, 1).astype(LOW)
         v_out[0] = (contract(wv[...], x, 0, 1) + vb).astype(LOW)
-        me, row = where[2], where[3] + lax.div(pl.program_id(0), 3)
+        me, row = where[2], where[3] + pl.program_id(0)
         span = t0.shape[1]
         line = seg_ref[pl.ds(row, 1), :]
         here = [jnp.bitwise_xor(me, r) for r in (0, 2, 1, 3)]
@@ -98,14 +97,14 @@
         bias[...] = jnp.where(seg_col == seg_row, 0.0, NEGATIVE)
 
     for h in range(heads):
-        part = pl.ds(pl.multiple_of((j * heads + h) * HD, HD), HD)
+        part = slice(h * HD, (h + 1) * HD)
         s = contract(k_out[0, part], q_out[0, part], 0, 0) + bias[...]
         top = jnp.max(s, axis=0, keepdims=True)
         e = jnp.exp2((s - top) * (LOG2E * HD**-0.5))
         low = e.astype(LOW)
         inv = 1.0 / col_sum(e)
         e_out[0, h] = low
-        inv_out[0, h : h + 1] = inv
+        inv_out[0, 8 * (h // 2) + h % 2 : 8 * (h // 2) + h % 2 + 1] = inv
         mixed = (contract(v_out[0, part], low, 1, 0) * inv).astype(LOW)
         mix_own[0, h * HD : (h + 1) * HD] = mixed[:, :half]
         mix_sib[0, h * HD : (h + 1) * HD] = mixed[:, half:]
@@ -116,22 +115,22 @@
     length = 4 * span
     cols = width // 2
     heads = cols // HD
-    step = 2
+    step = heads
     tall = step * HD
-    row3 = lambda *s: pl.BlockSpec((1,) + s, lambda t, w: (t // 3,) + (0,) * len(s))
+    row3 = lambda *s: pl.BlockSpec((1,) + s, lambda t, w: (t,) + (0,) * len(s))
     weight = pl.BlockSpec((width, cols), lambda t, w: (0, w[0]), pipeline_mode=pl.Buffered(1))
     bias = pl.BlockSpec((width,), lambda t, w: (0,))
-    mix = pl.BlockSpec((1, tall, length // 2), lambda t, w: (t // 3, t % 3, 0))
+    mix = pl.BlockSpec((1, tall, length // 2), lambda t, w: (t, 0, 0))
     return call(
         attend_kernel, where, (*toks, segments, wq, wk, wv, bq, bv), after,
-        grid=(3 * rows,),
+        grid=(rows,),
         in_specs=[row3(span, width)] * 4
         + [pl.BlockSpec(segments.shape, lambda t, w: (0, 0)), weight, weight, weight, bias, bias],
         out_specs=[row3(length, width)]
         + [row3(cols, length)] * 3
         + [
-            pl.BlockSpec((1, step, length, length), lambda t, w: (t // 3, t % 3, 0, 0)),
-            pl.BlockSpec((1, 8, length), lambda t, w: (t // 3, t % 3, 0)), mix, mix,
+            pl.BlockSpec((1, step, length, length), lambda t, w: (t, 0, 0, 0)),
+            pl.BlockSpec((1, 24, length), lambda t, w: (t, 0, 0)), mix, mix,
         ],
         out_shape=[SDS((rows, length, width), LOW)]
         + [SDS((rows, cols, length), LOW)] * 3
@@ -162,7 +161,7 @@
 
 TALL = 128
 HEAD = 4
-TAIL = 32
+TAIL = 16
 
 
 class Puts:
@@ -256,7 +255,9 @@
         act[:, cols] = (inner * big).astype(LOW)
         slope[:, cols] = (big + inner * bell).astype(LOW)
     loads[4 + chunks].wait()
-    second[...] += contract(act[...], w2[...], 1, 0)
+    for r in range(rows):
+        at = slice(r * block, (r + 1) * block)
+        second[at] += contract(act[at], w2[...], 1, 0)
     loads[2].wait()
     loads[3].wait()
 
@@ -533,61 +534,92 @@
         send_off(packed, keep, send, sems)
 
 
-def last_pair_kernel(
-    where, *refs, orders, shards,
-):
+def join_copies(where, own, got, room, whole, sems):
+    rows = own.shape[0]
+    mine = pl.ds(where[3], rows)
+    theirs = pl.ds(rows - where[3], rows)
+    loads = [pltpu.make_async_copy(v, room.at[n], sems.at[n]) for n, v in enumerate((own, got))]
+    stores = [pltpu.make_async_copy(room.at[n], whole.at[at], sems.at[2 + n]) for n, at in enumerate((mine, theirs))]
+    return loads, stores
+
+
+def begin(copies, others=()):
+    for copy in others:
+        copy.wait()
+    for copy in copies:
+        copy.start()
+
+
+def last_pairs_kernel(where, *refs, orders, shards):
     step_refs, refs = refs[:10], refs[10:]
-    d0, d1, bias0, bias1, dbranch, wq, wk, wv, vectors, *refs = refs
-    in_own, in_out, keep, send, grads, dq, dk, dv, acc, bias, packed, sems = refs
-    r = pl.program_id(0)
-    pair_back(step_refs, grads, acc, bias, r == 0)
-    tall = grads.shape[0] // 3
-    for n, d in enumerate((dq, dk, dv)):
-        part = slice(n * tall, (n + 1) * tall)
-        d[:tall] = d0[0, part]
-        d[tall : 2 * tall] = d1[0, part]
-        d[2 * tall :] = grads[part]
-    back = contract(dq[...], wq[...], 0, 1)
-    back = back + contract(dk[...], wk[...], 0, 1) + contract(dv[...], wv[...], 0, 1)
-    half = back.shape[0] // 2
-    in_own[0] = (back[:half] + dbranch[0].astype(F32)).astype(LOW)
-    in_out[0] = back[half:].astype(LOW)
-
-    @pl.when(r == pl.num_programs(0) - 1)
+    d0, bias0, dbranch, wq, wk, wv, vectors, out_own, out_got, *refs = refs
+    in_own, in_out, keep, send, result, grads, dq, dk, dv, acc, bias, packed, sems, room, join_sems = refs
+    loads, stores = join_copies(where, out_own, out_got, room, result, join_sems)
+    t = pl.program_id(0)
+    r = t // 2
+    width = acc.shape[1]
+    cols = grads.shape[1]
+    tall = cols // 3
+
+    pl.when(t == 0)(lambda: begin(loads))
+    pl.when(t == 1)(lambda: begin(stores, loads))
+    for p in range(2):
+
+        @pl.when(lax.rem(t, 2) == p)
+        def _():
+            lanes = slice(p * cols, (p + 1) * cols)
+            pair_back(step_refs, grads.at[p], acc.at[p], bias.at[:, lanes], r == 0)
+
+    @pl.when(lax.rem(t, 2) == 1)
+    def _():
+        for n, d in enumerate((dq, dk, dv)):
+            part = slice(n * tall, (n + 1) * tall)
+            d[:tall] = d0[0, part]
+            d[tall : 2 * tall] = grads[0, part]
+            d[2 * tall :] = grads[1, part]
+        back = contract(dq[...], wq[...], 0, 1)
+        back = back + contract(dk[...], wk[...], 0, 1) + contract(dv[...], wv[...], 0, 1)
+        half = back.shape[0] // 2
+        in_own[0] = (back[:half] + dbranch[0].astype(F32)).astype(LOW)
+        in_out[0] = back[half:].astype(LOW)
+
+    @pl.when(t == pl.num_programs(0) - 1)
     def _():
         core = where[0]
-        width, cols = acc.shape
-        spread(where, packed, acc, orders[3], 3, shards, slice(0, cols))
-        lines = [vectors[:, n * cols : (n + 1) * cols] for n in range(vectors.shape[1] // cols)]
+        width = acc.shape[1]
+        for p in range(2):
+            spread(where, packed, acc.at[p], orders[3], 3, shards, slice(p * cols, (p + 1) * cols))
+        wide = 2 * cols
+        lines = [vectors[:, n * wide : (n + 1) * wide] for n in range(vectors.shape[1] // wide)]
         zero = jnp.zeros((1, cols), F32)
         for n in (2, 0):
-            part = slice(n * tall, (n + 1) * tall)
-            line = jnp.concatenate([bias0[:1, part], bias1[:1, part], bias[:1, part]], axis=1)
-            lines += [jnp.where(core == c, line, zero) for c in range(2)]
-        lines.append(jnp.zeros((TAIL - len(lines), cols), F32))
-        packed[width:] = jnp.concatenate(lines, axis=0).astype(LOW)
+            at = lambda p: slice(p * cols + n * tall, p * cols + (n + 1) * tall)
+            line = jnp.concatenate([bias0[:1, n * tall : (n + 1) * tall], bias[:1, at(0)], bias[:1, at(1)]], axis=1)
+            lines.append(jnp.concatenate([jnp.where(core == c, line, zero) for c in range(2)], axis=1))
+        lines.append(jnp.zeros((TAIL - len(lines), wide), F32))
+        packed[packed.shape[0] - TAIL :] = jnp.concatenate(lines, axis=0).astype(LOW)
         send_off(packed, keep, send, sems)
-
-
-def pair_specs(p, x, attention):
+        begin((), stores)
+
+
+def pair_specs(row, pair, x, attention):
     rows, cols, length = attention[0].shape
     width = x.shape[2]
-    heads = cols // HD
     step = 2
     tall = step * HD
-    row3 = lambda *s: pl.BlockSpec((1,) + s, lambda r, w: (r,) + (0,) * len(s))
-    big = pl.BlockSpec((1, tall, length), lambda r, w: (r, p, 0))
-    small = pl.BlockSpec((1, tall, length // 2), lambda r, w: (r, p, 0))
-    inv = pl.BlockSpec((1, 8, length), lambda r, w: (r, p, 0))
+    row3 = lambda *s: pl.BlockSpec((1,) + s, lambda t, w: (row(t),) + (0,) * len(s))
+    big = pl.BlockSpec((1, tall, length), lambda t, w: (row(t), pair(t), 0))
+    small = pl.BlockSpec((1, tall, length // 2), lambda t, w: (row(t), pair(t), 0))
+    inv = pl.BlockSpec((1, 8, length), lambda t, w: (row(t), pair(t), 0))
     specs = [row3(length, width)] + [big] * 3
-    specs += [pl.BlockSpec((1, step, length, length), lambda r, w: (r, p, 0, 0)), inv]
+    specs += [pl.BlockSpec((1, step, length, length), lambda t, w: (row(t), pair(t), 0, 0)), inv]
     return specs + [small] * 4, row3
 
 
-def pair_grads(where, orders, shards, p, x, attention, o=(), after=(), thread=()):
+def pair_grads(where, orders, shards, x, attention, o=(), after=(), thread=()):
     rows, cols, length = attention[0].shape
     width = x.shape[2]
-    specs, row3 = pair_specs(p, x, attention)
+    specs, row3 = pair_specs(lambda t: t, lambda t: 0, x, attention)
     whole = lambda v: pl.BlockSpec(v.shape, lambda r, w: (0,) * len(v.shape))
     anywhere = pl.BlockSpec(memory_space=pl.ANY)
     total = cols + sum(v.shape[1] for v in o[:1])
@@ -605,30 +637,34 @@
     )
 
 
-def last_pair_grads(where, orders, shards, x, attention, pairs, dbranch, weights, vectors, after=(), thread=()):
+def last_pair_grads(
+    where, orders, shards, x, attention, first, dbranch, weights, vectors, out_own, out_got, after=(), thread=()
+):
     rows, cols, length = attention[0].shape
     width = x.shape[2]
-    specs, row3 = pair_specs(2, x, attention)
-    whole = lambda v: pl.BlockSpec(v.shape, lambda r, w: (0,) * len(v.shape))
-    weight = pl.BlockSpec((width, cols), lambda r, w: (0, w[0]), pipeline_mode=pl.Buffered(1))
+    specs, row3 = pair_specs(lambda t: t // 2, lambda t: 1 + t % 2, x, attention)
+    whole = lambda v: pl.BlockSpec(v.shape, lambda t, w: (0,) * len(v.shape))
+    weight = pl.BlockSpec((width, cols), lambda t, w: (0, w[0]), pipeline_mode=pl.Buffered(1))
     anywhere = pl.BlockSpec(memory_space=pl.ANY)
     low = lambda *s: pltpu.VMEM(s, LOW)
     half = width // 2
-    (d0, bias0), (d1, bias1) = pairs
+    d0, bias0 = first
     return call(
-        functools.partial(last_pair_kernel, orders=orders, shards=shards), where,
-        (x, *attention, d0, d1, bias0, bias1, dbranch, *weights, vectors), after, thread,
-        grid=(rows,),
+        functools.partial(last_pairs_kernel, orders=orders, shards=shards), where,
+        (x, *attention, d0, bias0, dbranch, *weights, vectors, out_own, out_got), after, thread,
+        grid=(2 * rows,),
         in_specs=specs
-        + [row3(cols, length)] * 2
-        + [whole(bias0), whole(bias1), row3(length // 2, width), weight, weight, weight, whole(vectors)],
-        out_specs=[row3(length // 2, width)] * 2 + [anywhere] * 2,
+        + [row3(cols, length), whole(bias0), row3(length // 2, width), weight, weight, weight, whole(vectors)]
+        + [anywhere] * 2,
+        out_specs=[row3(length // 2, width)] * 2 + [anywhere] * 3,
         out_shape=[SDS((rows, length // 2, width), LOW)] * 2
-        + [SDS((half, cols), LOW), SDS((half + TAIL, cols), LOW)],
-        scratch=[low(cols, length)] * 4
-        + [pltpu.VMEM((width, cols), F32), pltpu.VMEM((8, cols), F32), low(width + TAIL, cols)]
-        + [pltpu.SemaphoreType.DMA((2,))],
-        us=10,
+        + [SDS((half, 2 * cols), LOW), SDS((half + TAIL, 2 * cols), LOW)]
+        + [SDS((2 * rows,) + out_own.shape[1:], LOW)],
+        scratch=[low(2, cols, length)]
+        + [low(cols, length)] * 3
+        + [pltpu.VMEM((2, width, cols), F32), pltpu.VMEM((8, 2 * cols), F32), low(width + TAIL, 2 * cols)]
+        + [pltpu.SemaphoreType.DMA((2,)), low(2, *out_own.shape), pltpu.SemaphoreType.DMA((4,))],
+        us=20,
         name="last_pair_grads",
     )
 
@@ -692,7 +728,11 @@
     return results, thread
 
 
-def finish_kernel(where, ab_mine, c_mine, ab_got, c_got, gq, gk, gv, go, *outs):
+def finish_kernel(where, a_mine, c_mine, a_got, c_got, in_own, in_got, joined, gq, gk, gv, go, *outs):
+    *outs, room, sems = outs
+    loads, stores = join_copies(where, in_own.at[:, : joined.shape[1]], in_got, room, joined, sems)
+    begin(loads)
+    begin(stores, loads)
     core = where[0]
     b = where[1]
     size, width = gq.shape
@@ -707,33 +747,39 @@
 
     for n, ref in enumerate((gq, gk, gv)):
         for p in range(3):
-            mine, got = (c_mine, c_got) if p == 2 else (ab_mine, ab_got)
-            at = n * tall + (width if p == 1 else 0)
+            mine, got = (a_mine, a_got) if p == 0 else (c_mine, c_got)
+            at = n * tall + (cols if p == 2 else 0)
             both(ref, p * tall, mine[:size, at : at + tall], got[:size, at : at + tall])
-    both(go, 0, ab_mine[:, cols:width], ab_got[:, cols:width])
+    both(go, 0, a_mine[:, cols:], a_got[:, cols:])
     total = c_mine[size:].astype(F32) + c_got[size:].astype(F32)
     row = 0
     for ref in outs:
         n = ref.shape[0]
-        parts = n * (width // size) // cols
+        parts = n * (width // size) // width
         line = jnp.concatenate([total[row + i : row + i + 1] for i in range(parts)], axis=1)
         row += parts
         picked = jnp.zeros((1, n), F32)
         for s in range(width // size):
             picked = jnp.where(b == s, line[:, s * n : (s + 1) * n], picked)
         ref[...] = picked[0]
-
-
-def finish(where, mine, got, lengths):
+    begin((), stores)
+
+
+def finish(where, mine, got, in_own, in_got, lengths, after=()):
     whole = lambda *s: pl.BlockSpec(s, lambda i, w: (0,) * len(s))
+    anywhere = pl.BlockSpec(memory_space=pl.ANY)
     size = mine[0].shape[0]
-    width = 2 * mine[1].shape[1]
+    width = mine[1].shape[1]
+    rows = in_got.shape[0]
     return call(
-        finish_kernel, where, (*mine, *got), (),
+        finish_kernel, where, (*mine, *got, in_own, in_got), after,
         grid=(1,),
-        in_specs=[whole(*v.shape) for v in (*mine, *got)],
-        out_specs=[whole(size, width)] * 4 + [whole(n) for n in lengths],
-        out_shape=[SDS((size, width), F32)] * 4 + [SDS((n,), F32) for n in lengths],
+        in_specs=[whole(*v.shape) for v in (*mine, *got)] + [anywhere] * 2,
+        out_specs=[anywhere] + [whole(size, width)] * 4 + [whole(n) for n in lengths],
+        out_shape=[SDS((2 * rows,) + in_got.shape[1:], LOW)]
+        + [SDS((size, width), F32)] * 4
+        + [SDS((n,), F32) for n in lengths],
+        scratch=[pltpu.VMEM((2,) + in_got.shape, LOW), pltpu.SemaphoreType.DMA((4,))],
         us=2,
         name="finish",
         mib=16,
@@ -837,7 +883,7 @@
         got = blk_swap(flat(outer_send), 1)
         out_got = blk_swap(out1, 2)
         outer = split_sum(outer_keep, got)
-        (inner_send,) = gate(where, (flat(inner_send),), outer)
+        (inner_send,) = gate(where, (flat(inner_send),), (got,))
         inner = split_sum(flat(inner_keep), blk_swap(inner_send, 1))
 
         def hops():
@@ -853,13 +899,12 @@
             second, output_weight, inner_weight, after=(outer[0], inner[0]), thread=(out0,) + keeps,
         )
         out0, keeps = through[0], through[1:]
-        result = join_rows(out0, out_got)
         dm_sib = blk_swap(dm_out, 1)
         o_got = blk_swap(flat(o_send), 1)
         dbranch = dbranch.reshape(rows, 2 * span, width)
         attention = (q, k, v, e, inv, mix_own, mix_out, dm_own, dm_sib)
         (d0, bias0, a_keep, a_send), keeps = pair_grads(
-            where, ORDERS, shards, 0, x, attention, (flat(o_keep), o_got), after=(out_got,), thread=keeps
+            where, ORDERS, shards, x, attention, (flat(o_keep), o_got), after=(out_got,), thread=keeps
         )
         if direct:
             outer, inner = (split_sum(keep, g) for keep, g in zip(keeps, got))
@@ -868,15 +913,9 @@
         if direct:
             got += (hop(a_send, ORDERS[2][0]),)
             keeps += (a_keep,)
-        (d1, bias1, b_keep, b_send), keeps = pair_grads(
-            where, ORDERS, shards, 1, x, attention, after=(outer[0], inner[0]), thread=keeps
-        )
-        if direct:
-            got += (hop(b_send, ORDERS[2][0]),)
-            keeps += (b_keep,)
-        (in_own, in_out, c_keep, c_send), keeps = last_pair_grads(
-            where, ORDERS, shards, x, attention, ((d0, bias0), (d1, bias1)), dbranch,
-            (query_weight, key_weight, value_weight), vectors, thread=keeps,
+        (in_own, in_out, c_keep, c_send, result), keeps = last_pair_grads(
+            where, ORDERS, shards, x, attention, (d0, bias0), dbranch,
+            (query_weight, key_weight, value_weight), vectors, out0, out_got, after=(outer[0], inner[0]), thread=keeps,
         )
         in_sum = fix(add_low(in_own, blk_swap(in_out, 1)))
 
@@ -904,16 +943,16 @@
             )
             in_got = blk_swap(in_sum[:, span:], 2)
             c_got, ffn_got, ab_got = hop(c_send, "1"), hop(ffn_send, "2"), hop(ab_send, "x")
-            ((c, c_send), (ab, ab_send)), _ = next_round(
-                where, [((c,), (c_got,), c_send, True), ((ab,), (ab_got,), None, True)], after=(in_got,)
+            ((c, c_send), (ab, ab_send), (ffn,)), _ = next_round(
+                where,
+                [((c,), (c_got,), c_send, True), ((ab,), (ab_got,), None, True), ((ffn,), (ffn_got,), None, False)],
+                after=(in_got,),
             )
-            input_grad = join_rows(in_sum[:, :span], in_got)
-            ffn = fix(add_low(ffn, ffn_got))
-            c_got, ab_got = hop(c_send, "2"), hop(ab_send, "2")
-            ((_, c), (ab,)), (ffn,) = next_round(
-                where, [((c,), (c_got,), c_send, False), ((ab,), (ab_got,), None, False)], thread=(ffn,)
+            c_got, ab_got, ffn_got = hop(c_send, "2"), hop(ab_send, "2"), hop(ffn, "y")
+            ((_, c), (ab,)), _ = next_round(
+                where, [((c,), (c_got,), c_send, False), ((ab,), (ab_got,), None, False)], after=(ffn_got,)
             )
-            c_got, ab_got, ffn_got = hop(c, "y"), hop(ab, "y"), hop(ffn, "y")
+            c_got, ab_got = hop(c, "y"), hop(ab, "y")
             c = fix(add_low(c, c_got))
             ab = fix(jnp.concatenate([jnp.where(y == 0, ab, ab_got), jnp.where(y == 0, ab_got, ab)], axis=0))
             pair = jnp.stack([ffn, ffn_got])
@@ -929,8 +968,9 @@
 
             inner_done = halves(columns(ffn), columns(ffn_got), 1).astype(F32)
             lengths = [n // shards for n in (width,) * 3 + (inner_weight.shape[1],) + (width,) * 5]
-            query_done, key_done, value_done, output_done, *vecs = finish(
-                where, (ab, c), tuple(blk_swap(g, 1) for g in (ab, c)), lengths
+            input_grad, query_done, key_done, value_done, output_done, *vecs = finish(
+                where, (ab, c), tuple(blk_swap(g, 1) for g in (ab, c)), in_sum, in_got, lengths,
+                after=(outer_done, inner_done),
             )
         else:
             input_grad = join_rows(in_sum[:, :span], blk_swap(in_sum[:, span:], 2))
@@ -947,8 +987,8 @@
             cols = width // 2
             tall = cols // 3
             whole_a = jnp.concatenate([a_keep, a_send], axis=0)
-            groups = (whole_a, jnp.concatenate([b_keep, b_send], axis=0))
-            groups += (jnp.concatenate([c_keep, c_send[: c_keep.shape[0]]], axis=0),)
+            whole_c = jnp.concatenate([c_keep, c_send[: c_keep.shape[0]]], axis=0)
+            groups = (whole_a, whole_c[:, :cols], whole_c[:, cols:])
             query_done, key_done, value_done = (
                 join(whole(jnp.concatenate([g[:, n * tall : (n + 1) * tall] for g in groups], axis=1)), 1)
                 for n in range(3)

time: 237 us -> 222 us (0.937)
  Pallas kernels: 113 us -> 107 us
  other arithmetic: 19.4 us -> 13.8 us
    pallas_call x12 -> x11, Pallas kernels: 113 us -> 107 us  [call(): pl.pallas_call(body, grid_spec=pltpu.PrefetchScalarGridSpec(num_scalar_pr...]
    select_n x2 -> x0, other arithmetic: 3.67 us -> none  [join_rows(): jnp.where(y == 0, jnp.concatenate([keep, got], axis=0), jnp.concatenate([...]
    ppermute x32 -> x31, starting transfers between devices: 30.8 us -> 28.9 us  [swap(): return lax.ppermute(v, axis, [(i, i ^ mask) for i in range(size)])]
    ppermute x32 -> x31, waiting for transfers between devices: 60.3 us -> 58.8 us  [swap(): return lax.ppermute(v, axis, [(i, i ^ mask) for i in range(size)])]
    convert_element_type x10 -> x9, other arithmetic: 13.1 us -> 13.2 us  [add_low(): return (a.astype(F32) + b.astype(F32)).astype(LOW)]
  transfers between devices with their start and end apart: 32 -> 31, of which waited for: 14 -> 15; matrix products, arithmetic and copies ran while one was open for 8% -> 7% of each run, Pallas kernels for 32% -> 31%
where the time goes in v4:
time: 222 us; the launch traced here: 218 us
  Pallas kernels  107 us (48%)
  waiting for transfers between devices  58.8 us (26%)
  starting transfers between devices  28.9 us (13%)
  other arithmetic  13.8 us (6%)
  local copies, waits for them, and re-layouts  7.54 us (3%)
    pallas_call x11, Pallas kernels, call(): pl.pallas_call(body, grid_spec=pltpu.PrefetchScalarGridSpec(num_scalar_pr...  107 us
    ppermute x31, waiting for transfers between devices, swap(): return lax.ppermute(v, axis, [(i, i ^ mask) for i in range(size)])  58.8 us
    ppermute x31, starting transfers between devices, swap(): return lax.ppermute(v, axis, [(i, i ^ mask) for i in range(size)])  28.9 us
    convert_element_type x9, other arithmetic, add_low(): return (a.astype(F32) + b.astype(F32)).astype(LOW)  13.2 us
  transfers between devices with their start and end apart: 31, of which 15 were waited for; matrix products, arithmetic and copies ran while one was open for 7% of the time, Pallas kernels for 31%

profile of v4, /device:TPU:0, one launch (start us, length us, event | category | flops | bytes accessed | tf_op | source)
XLA Modules:
  0.0 217.9 jit_solution(8128052440535289782)
XLA Ops:
  0.7 1.4 constant_dynamic-slice_fusion.2
  2.1 3.0 %collective-permute-start = (bf16[3,128,768]{2,1,0:T(8,128)(2,1)S(1)}, bf16[3,128,768]{2,1,0:T(8,128)(2,1)S(1)}, u32[]{:S(2)}, u32[]{:S(2)}) collective-permute-start(bf16[3,128,768]{2,1,0:T(8,128)(2,1)S(1)} %get-tuple-element.179), channel_id=1, source_target_pairs={{0,2},{1,3},{2,0},{3,1},{4,6},{5,7},{6,4},{7,5},{8,10},{9,11},{10,... | collective-permute-start | bytes 1769480 | tf_op jit(solution)/shard_map/ppermute | solution.py:790
  5.1 13.3 %collective-permute-done.refs_1_ = bf16[3,128,768]{2,1,0:T(8,128)(2,1)S(1)} collective-permute-done((bf16[3,128,768]{2,1,0:T(8,128)(2,1)S(1)}, bf16[3,128,768]{2,1,0:T(8,128)(2,1)S(1)}, u32[]{:S(2)}, u32[]{:S(2)}) %collective-permute-start) | collective-permute-done | bytes 589856 | tf_op jit(solution)/shard_map/ppermute | solution.py:790
  18.5 1.2 constant_dynamic-slice_fusion
  19.7 1.7 collective-permute-start.4
  21.5 0.6 concatenate.38.w
  22.1 0.8 copy-done.17
  22.9 18.1 %attend.1 = (bf16[3,512,768]{2,1,0:T(8,128)(2,1)}, bf16[3,384,512]{2,1,0:T(8,128)(2,1)}, bf16[3,384,512]{2,1,0:T(8,128)(2,1)}, bf16[3,384,512]{2,1,0:T(8,128)(2,...) custom-call(s32[68]{0:T(128)} %concatenate.38.w, ...), custom_call_target="tpu_custom_call" | custom-call | flops 900000000 | tf_op jit(solution)/shard_map/attend/pallas_call | solution.py:37
  41.0 0.2 collective-permute-start.3
  41.3 2.1 collective-permute-done.3.refs_1_
  43.3 0.8 copy-done.10
  44.1 33.9 %forward.1 = (f32[1,5376]{1,0:T(1,128)}, bf16[3,128,768]{2,1,0:T(8,128)(2,1)}, bf16[3,128,768]{2,1,0:T(8,128)(2,1)}, bf16[768,3072]{1,0:T(8,128)(2,1)}, f32[768,...) custom-call(s32[68]{0:T(128)} %concatenate.38.w, ...), custom_call_target="tpu_custom_call" | custom-call | flops 1350000000 | tf_op jit(solution)/shard_map/forward/pallas_call | solution.py:37
  78.0 0.2 collective-permute-start.5
  78.2 4.6 %collective-permute-done.5.refs_1_ = bf16[1536,768]{1,0:T(8,128)(2,1)S(1)} collective-permute-done((bf16[1536,768]{1,0:T(8,128)(2,1)}, bf16[1536,768]{1,0:T(8,128)(2,1)S(1)}, u32[]{:S(2)}, u32[]{:S(2)}) %collective-permute-start.5) | collective-permute-done | bytes 2359328 | tf_op jit(solution)/shard_map/ppermute | solution.py:790
  82.8 0.5 gate.1
  83.4 0.2 collective-permute-start.6
  83.6 0.9 copy-done.12
  84.7 2.4 %fusion.1 = (bf16[768,768]{1,0:T(8,128)(2,1)}, bf16[768,768]{1,0:T(8,128)(2,1)}) fusion(bf16[1536,768]{1,0:T(8,128)(2,1)S(1)} %collective-permute-done.5.refs_1_, bf16[8,96,768]{2,1,0:T(8,128)(2,1)S(1)} %get-tuple-element.173, bf16[8,96,768]{2,1,0:T(8,128)(2,1)S(1)} %get-tuple-element.174), kind=kLoop, calls=%fused_computation.3 | loop fusion | flops 4718592 | bytes 7077888 | tf_op jit(solution)/shard_map/convert_element_type | solution.py:794
  87.0 1.5 collective-permute-start.10
  88.7 0.6 collective-permute-start.9
  89.3 2.1 fusion
  91.4 1.6 collective-permute-start.11
  93.0 15.7 %branch.1 = (f32[1,7680]{1,0:T(1,128)}, bf16[768,768]{1,0:T(8,128)(2,1)}, bf16[3,384,256]{2,1,0:T(8,128)(2,1)}, bf16[3,384,256]{2,1,0:T(8,128)(2,1)}, bf16[16,48...) custom-call(s32[68]{0:T(128)} %concatenate.38.w, ...), custom_call_target="tpu_custom_call", output_to_operand_aliasing={{6}: (11, {}), {7}: (12, {}), {8}: (13, {})} | custom-call | flops 650000000 | tf_op jit(solution)/shard_map/branch/pallas_call | solution.py:37
  108.8 0.5 collective-permute-start.8
  109.3 1.8 collective-permute-done.7.refs_9_
  111.1 0.8 collective-permute-done.8.refs_11_
  112.0 10.9 %pair_grads.1 = (bf16[3,384,512]{2,1,0:T(8,128)(2,1)}, f32[8,384]{1,0:T(8,128)}, bf16[384,768]{1,0:T(8,128)(2,1)}, bf16[384,768]{1,0:T(8,128)(2,1)}, bf16[768,768]{1,0:T(8,128)(2,1)}, /*index=5*/bf16[768,768]{1,0:T(8,128)(2,1)}) custom-call(s32[68]{0:T(128)} %concatenate.38.w, ...), custom_call_target="tpu_custom_call", output_to_operand_aliasing={{4}: (13, {}), {5}: (14, {})} | custom-call | flops 400000000 | tf_op jit(solution)/shard_map/pair_grads/pallas_call | solution.py:37
  122.9 3.0 %add_convert_fusion.4 = (bf16[384,768]{1,0:T(8,128)(2,1)}, bf16[384,768]{1,0:T(8,128)(2,1)}) fusion(bf16[768,768]{1,0:T(8,128)(2,1)} %collective-permute-done.10, bf16[768,768]{1,0:T(8,128)(2,1)} %get-tuple-element.120), kind=kLoop, calls=%fused_computation.12 | loop fusion | flops 2359296 | bytes 3538944 | tf_op jit(solution)/shard_map/convert_element_type | solution.py:794
  125.9 0.5 collective-permute-start.13
  126.4 1.5 collective-permute-start.12
  127.9 2.6 %add_convert_fusion.3 = (bf16[384,768]{1,0:T(8,128)(2,1)}, bf16[384,768]{1,0:T(8,128)(2,1)}) fusion(bf16[768,768]{1,0:T(8,128)(2,1)} %collective-permute-done.11, bf16[768,768]{1,0:T(8,128)(2,1)S(1)} %copy-done.7), kind=kLoop, calls=%fused_computation.11 | loop fusion | flops 2359296 | bytes 3538944 | tf_op jit(solution)/shard_map/convert_element_type | solution.py:794
  130.5 0.5 collective-permute-start.14
  131.0 21.8 %last_pair_grads.1 = (bf16[3,256,768]{2,1,0:T(8,128)(2,1)}, bf16[3,256,768]{2,1,0:T(8,128)(2,1)}, bf16[384,768]{1,0:T(8,128)(2,1)}, bf16[400,768]{1,0:T(8,128)(2...) custom-call(s32[68]{0:T(128)} %concatenate.38.w, ...), custom_call_target="tpu_custom_call", output_to_operand_aliasing={{5}: (20, {}), {6}: (21, {}), {7}: (22, {})} | custom-call | flops 1000000000 | tf_op jit(solution)/shard_map/last_pair_grads/pallas_call | solution.py:37
  152.9 1.4 add_convert_fusion.2
  154.4 1.2 add_convert_fusion.1
  155.8 0.9 copy-done.2
  156.9 0.7 next_round.4
  157.6 0.5 collective-permute-start.17
  158.1 1.6 collective-permute-start.15
  159.7 1.6 collective-permute-start.16
  161.3 0.3 add_convert_fusion.refs_6_
  161.6 11.8 %collective-permute-done.17 = bf16[384,768]{1,0:T(8,128)(2,1)S(1)} collective-permute-done((bf16[384,768]{1,0:T(8,128)(2,1)S(1)}, bf16[384,768]{1,0:T(8,128)(2,1)S(1)}, u32[]{:S(2)}, u32[]{:S(2)}) %collective-permute-start.17) | collective-permute-done | bytes 589856 | tf_op jit(solution)/shard_map/ppermute | solution.py:790
  173.6 0.5 collective-permute-done.15.refs_1_
  174.0 0.7 next_round.5
  174.8 1.7 collective-permute-start.22
  176.5 1.6 collective-permute-start.19
  178.1 2.6 %collective-permute-start.21 = (bf16[192,768]{1,0:T(8,128)(2,1)S(1)}, bf16[192,768]{1,0:T(8,128)(2,1)S(1)}, u32[]{:S(2)}, u32[]{:S(2)}) collective-permute-start(bf16[192,768]{1,0:T(8,128)(2,1)S(1)} %get-tuple-element.140), channel_id=1, source_target_pairs={{0,16},{4,20},{8,24},{12,28},{16,0},{20,4},{24,8},{28,12},{1,17},{... | collective-permute-start | bytes 884744 | tf_op jit(solution)/shard_map/ppermute | solution.py:790
  180.7 1.5 collective-permute-start.20
  182.2 3.6 %collective-permute-done.20.refs_4_ = bf16[96,768]{1,0:T(8,128)(2,1)S(1)} collective-permute-done((bf16[96,768]{1,0:T(8,128)(2,1)S(1)}, bf16[96,768]{1,0:T(8,128)(2,1)S(1)}, u32[]{:S(2)}, u32[]{:S(2)}) %collective-permute-start.20) | collective-permute-done | bytes 147488 | tf_op jit(solution)/shard_map/ppermute | solution.py:790
  185.9 4.7 %collective-permute-done.21.refs_6_ = bf16[192,768]{1,0:T(8,128)(2,1)S(1)} collective-permute-done((bf16[192,768]{1,0:T(8,128)(2,1)S(1)}, bf16[192,768]{1,0:T(8,128)(2,1)S(1)}, u32[]{:S(2)}, u32[]{:S(2)}) %collective-permute-start.21) | collective-permute-done | bytes 294944 | tf_op jit(solution)/shard_map/ppermute | solution.py:790
  190.5 0.8 collective-permute-done.19.refs_1_
  191.4 0.7 next_round.6
  192.1 0.5 collective-permute-start.25
  192.6 2.7 %collective-permute-start.23 = (bf16[112,768]{1,0:T(8,128)(2,1)S(1)}, bf16[112,768]{1,0:T(8,128)(2,1)S(1)}, u32[]{:S(2)}, u32[]{:S(2)}) collective-permute-start(bf16[112,768]{1,0:T(8,128)(2,1)S(1)} %get-tuple-element.143.refs_2_), channel_id=1, source_target_pairs={{0,16},{4,20},{8,24},{12,28},{16,0},{20,4},{24,8},{28,12},{1,17},{... | collective-permute-start | bytes 516104 | tf_op jit(solution)/shard_map/ppermute | solution.py:790
  195.3 0.2 collective-permute-start.24
  195.5 3.8 %collective-permute-done.25.refs_5_ = bf16[192,768]{1,0:T(8,128)(2,1)S(1)} collective-permute-done((bf16[192,768]{1,0:T(8,128)(2,1)S(1)}, bf16[192,768]{1,0:T(8,128)(2,1)S(1)}, u32[]{:S(2)}, u32[]{:S(2)}) %collective-permute-start.25) | collective-permute-done | bytes 294944 | tf_op jit(solution)/shard_map/ppermute | solution.py:790
  199.6 5.2 %collective-permute-done.24.refs_4_ = bf16[48,768]{1,0:T(8,128)(2,1)S(1)} collective-permute-done((bf16[48,768]{1,0:T(8,128)(2,1)S(1)}, bf16[48,768]{1,0:T(8,128)(2,1)S(1)}, u32[]{:S(2)}, u32[]{:S(2)}) %collective-permute-start.24) | collective-permute-done | bytes 73760 | tf_op jit(solution)/shard_map/ppermute | solution.py:790
  204.8 1.3 next_round.7
  206.1 1.5 collective-permute-start.26
  207.6 0.5 collective-permute-start.27
  208.1 2.6 %collective-permute-done.26 = bf16[48,768]{1,0:T(8,128)(2,1)S(1)} collective-permute-done((bf16[48,768]{1,0:T(8,128)(2,1)S(1)}, bf16[48,768]{1,0:T(8,128)(2,1)S(1)}, u32[]{:S(2)}, u32[]{:S(2)}) %collective-permute-start.26) | collective-permute-done | bytes 73760 | tf_op jit(solution)/shard_map/ppermute | solution.py:790
  210.9 2.1 collective-permute-done.27
  213.5 1.0 collective-permute-done.29.refs_3_
  214.5 2.9 %finish.1 = (bf16[6,128,768]{2,1,0:T(8,128)(2,1)}, f32[96,768]{1,0:T(8,128)}, f32[96,768]{1,0:T(8,128)}, f32[96,768]{1,0:T(8,128)}, f32[96,768]{1,0:T(8,128)}, /...) custom-call(s32[68]{0:T(128)S(1)} %copy-done.6, ...), custom_call_target="tpu_custom_call" | custom-call | flops 100000000 | tf_op jit(solution)/shard_map/finish/pallas_call | solution.py:37
  (76 shorter events, 2.0 us)
Async XLA Ops:
  0.7 17.8 %copy-start.15 = (bf16[6,128,768]{2,1,0:T(8,128)(2,1)S(1)}, bf16[6,128,768]{2,1,0:T(8,128)(2,1)}, u32[]{:S(2)}) copy-start(bf16[6,128,768]{2,1,0:T(8,128)(2,1)} %param.35) | copy-start | bytes 3538948
  2.1 17.6 %copy-start.13 = (bf16[3,128,768]{2,1,0:T(8,128)(2,1)}, bf16[3,128,768]{2,1,0:T(8,128)(2,1)S(1)}, u32[]{:S(2)}) copy-start(bf16[3,128,768]{2,1,0:T(8,128)(2,1)S(1)} %get-tuple-element.180.refs_0_) | copy-start | bytes 1769476
  2.1 16.4 %collective-permute-start = (bf16[3,128,768]{2,1,0:T(8,128)(2,1)S(1)}, bf16[3,128,768]{2,1,0:T(8,128)(2,1)S(1)}, u32[]{:S(2)}, u32[]{:S(2)}) collective-permute-start(bf16[3,128,768]{2,1,0:T(8,128)(2,1)S(1)} %get-tuple-element.179), channel_id=1, source_target_pairs={{0,2},{1,3},{2,0},{3,1},{4,6},{5,7},{6,4},{7,5},{8,10},{9,11},{10,... | collective-permute-start | bytes 1769480 | tf_op jit(solution)/shard_map/ppermute | solution.py:790
  5.1 16.9 %collective-permute-start.1 = (bf16[3,128,768]{2,1,0:T(8,128)(2,1)S(1)}, bf16[3,128,768]{2,1,0:T(8,128)(2,1)S(1)}, u32[]{:S(2)}, u32[]{:S(2)}) collective-permute-start(bf16[3,128,768]{2,1,0:T(8,128)(2,1)S(1)} %get-tuple-element.180.refs_0_), channel_id=1, source_target_pairs={{0,1},{1,0},{2,3},{3,2},{4,5},{5,4},{6,7},{7,6},{8,9},{9,8},{10,11... | collective-permute-start | bytes 1769480 | tf_op jit(solution)/shard_map/ppermute | solution.py:790
  18.5 1.2 copy-start.16
  18.5 4.4 %collective-permute-start.2 = (bf16[3,128,768]{2,1,0:T(8,128)(2,1)S(1)}, bf16[3,128,768]{2,1,0:T(8,128)(2,1)}, u32[]{:S(2)}, u32[]{:S(2)}) collective-permute-start(bf16[3,128,768]{2,1,0:T(8,128)(2,1)S(1)} %collective-permute-done.refs_1_), channel_id=1, source_target_pairs={{0,1},{1,0},{2,3},{3,2},{4,5},{5,4},{6,7},{7,6},{8,9},{9,8},{10,11... | collective-permute-start | bytes 1769480 | tf_op jit(solution)/shard_map/ppermute | solution.py:790
  19.7 21.6 %collective-permute-start.4 = (bf16[3,128,768]{2,1,0:T(8,128)(2,1)}, bf16[3,128,768]{2,1,0:T(8,128)(2,1)}, u32[]{:S(2)}, u32[]{:S(2)}) collective-permute-start(bf16[3,128,768]{2,1,0:T(8,128)(2,1)} %get-tuple-element.177), channel_id=1, source_target_pairs={{0,2},{1,3},{2,0},{3,1},{4,6},{5,7},{6,4},{7,5},{8,10},{9,11},{10,... | collective-permute-start | bytes 1769480 | tf_op jit(solution)/shard_map/ppermute | solution.py:790
  22.1 0.8 copy-start.17
  41.0 2.3 %collective-permute-start.3 = (bf16[3,384,256]{2,1,0:T(8,128)(2,1)}, bf16[3,384,256]{2,1,0:T(8,128)(2,1)S(1)}, u32[]{:S(2)}, u32[]{:S(2)}) collective-permute-start(bf16[3,384,256]{2,1,0:T(8,128)(2,1)} %get-tuple-element.97.refs_7_), channel_id=1, source_target_pairs={{0,1},{1,0},{2,3},{3,2},{4,5},{5,4},{6,7},{7,6},{8,9},{9,8},{10,11... | collective-permute-start | bytes 1769480 | tf_op jit(solution)/shard_map/ppermute | solution.py:790
  43.3 0.8 copy-start.10
  44.1 38.7 %copy-start.5 = (s32[68]{0:T(128)S(1)}, s32[68]{0:T(128)}, u32[]{:S(2)}) copy-start(s32[68]{0:T(128)} %concatenate.38.w) | copy-start | bytes 820
  78.0 4.8 %collective-permute-start.5 = (bf16[1536,768]{1,0:T(8,128)(2,1)}, bf16[1536,768]{1,0:T(8,128)(2,1)S(1)}, u32[]{:S(2)}, u32[]{:S(2)}) collective-permute-start(bf16[1536,768]{1,0:T(8,128)(2,1)} %bitcast.64), channel_id=1, source_target_pairs={{0,1},{1,0},{2,3},{3,2},{4,5},{5,4},{6,7},{7,6},{8,9},{9,8},{10,11... | collective-permute-start | bytes 7077896 | tf_op jit(solution)/shard_map/ppermute | solution.py:790
  82.8 1.7 copy-start.12
  83.4 5.9 %collective-permute-start.6 = (bf16[1536,768]{1,0:T(8,128)(2,1)}, bf16[1536,768]{1,0:T(8,128)(2,1)S(1)}, u32[]{:S(2)}, u32[]{:S(2)}) collective-permute-start(bf16[1536,768]{1,0:T(8,128)(2,1)} %gate.1), channel_id=1, source_target_pairs={{0,1},{1,0},{2,3},{3,2},{4,5},{5,4},{6,7},{7,6},{8,9},{9,8},{10,11... | collective-permute-start | bytes 7077896 | tf_op jit(solution)/shard_map/ppermute | solution.py:790
  84.7 3.9 %copy-start.11 = (bf16[16,96,768]{2,1,0:T(8,128)(2,1)S(1)}, bf16[16,96,768]{2,1,0:T(8,128)(2,1)}, u32[]{:S(2)}) copy-start(bf16[16,96,768]{2,1,0:T(8,128)(2,1)} %get-tuple-element.106) | copy-start | bytes 7077892
  87.0 35.9 %collective-permute-start.10 = (bf16[768,768]{1,0:T(8,128)(2,1)}, bf16[768,768]{1,0:T(8,128)(2,1)}, u32[]{:S(2)}, u32[]{:S(2)}) collective-permute-start(bf16[768,768]{1,0:T(8,128)(2,1)} %get-tuple-element.171.refs_13_), channel_id=1, source_target_pairs={{0,4},{4,0},{8,12},{12,8},{16,20},{20,16},{24,28},{28,24},{1,5},{5... | collective-permute-start | bytes 3538952 | tf_op jit(solution)/shard_map/ppermute | solution.py:790
  88.7 20.6 %collective-permute-start.9 = (bf16[3,128,768]{2,1,0:T(8,128)(2,1)}, bf16[3,128,768]{2,1,0:T(8,128)(2,1)S(1)}, u32[]{:S(2)}, u32[]{:S(2)}) collective-permute-start(bf16[3,128,768]{2,1,0:T(8,128)(2,1)} %get-tuple-element.114), channel_id=1, source_target_pairs={{0,2},{1,3},{2,0},{3,1},{4,6},{5,7},{6,4},{7,5},{8,10},{9,11},{10,... | collective-permute-start | bytes 1769480 | tf_op jit(solution)/shard_map/ppermute | solution.py:790
  91.4 36.5 %collective-permute-start.11 = (bf16[768,768]{1,0:T(8,128)(2,1)}, bf16[768,768]{1,0:T(8,128)(2,1)}, u32[]{:S(2)}, u32[]{:S(2)}) collective-permute-start(bf16[768,768]{1,0:T(8,128)(2,1)} %get-tuple-element.167.refs_14_), channel_id=1, source_target_pairs={{0,8},{4,12},{8,0},{12,4},{16,24},{20,28},{24,16},{28,20},{1,9},{5... | collective-permute-start | bytes 3538952 | tf_op jit(solution)/shard_map/ppermute | solution.py:790
  108.7 2.4 %collective-permute-start.7 = (bf16[3,384,256]{2,1,0:T(8,128)(2,1)}, bf16[3,384,256]{2,1,0:T(8,128)(2,1)}, u32[]{:S(2)}, u32[]{:S(2)}) collective-permute-start(bf16[3,384,256]{2,1,0:T(8,128)(2,1)} %get-tuple-element.109), channel_id=1, source_target_pairs={{0,1},{1,0},{2,3},{3,2},{4,5},{5,4},{6,7},{7,6},{8,9},{9,8},{10,11... | collective-permute-start | bytes 1769480 | tf_op jit(solution)/shard_map/ppermute | solution.py:790
  108.8 3.2 %collective-permute-start.8 = (bf16[768,384]{1,0:T(8,128)(2,1)}, bf16[768,384]{1,0:T(8,128)(2,1)}, u32[]{:S(2)}, u32[]{:S(2)}) collective-permute-start(bf16[768,384]{1,0:T(8,128)(2,1)} %bitcast.65), channel_id=1, source_target_pairs={{0,1},{1,0},{2,3},{3,2},{4,5},{5,4},{6,7},{7,6},{8,9},{9,8},{10,11... | collective-permute-start | bytes 1769480 | tf_op jit(solution)/shard_map/ppermute | solution.py:790
  109.3 2.7 %copy-start.9 = (bf16[3,128,768]{2,1,0:T(8,128)(2,1)}, bf16[3,128,768]{2,1,0:T(8,128)(2,1)S(1)}, u32[]{:S(2)}) copy-start(bf16[3,128,768]{2,1,0:T(8,128)(2,1)S(1)} %collective-permute-done.9.refs_14_.refs_18_) | copy-start | bytes 1769476
  122.9 5.0 %copy-start.7 = (bf16[768,768]{1,0:T(8,128)(2,1)S(1)}, bf16[768,768]{1,0:T(8,128)(2,1)}, u32[]{:S(2)}) copy-start(bf16[768,768]{1,0:T(8,128)(2,1)} %get-tuple-element.121) | copy-start | bytes 3538948
  125.9 27.0 %collective-permute-start.13 = (bf16[384,768]{1,0:T(8,128)(2,1)}, bf16[384,768]{1,0:T(8,128)(2,1)}, u32[]{:S(2)}, u32[]{:S(2)}) collective-permute-start(bf16[384,768]{1,0:T(8,128)(2,1)} %get-tuple-element.165.refs_22_), channel_id=1, source_target_pairs={{0,8},{4,12},{8,0},{12,4},{16,24},{20,28},{24,16},{28,20},{1,9},{5... | collective-permute-start | bytes 1769480 | tf_op jit(solution)/shard_map/ppermute | solution.py:790
  126.4 29.4 %collective-permute-start.12 = (bf16[384,768]{1,0:T(8,128)(2,1)}, bf16[384,768]{1,0:T(8,128)(2,1)S(1)}, u32[]{:S(2)}, u32[]{:S(2)}) collective-permute-start(bf16[384,768]{1,0:T(8,128)(2,1)} %get-tuple-element.126), channel_id=1, source_target_pairs={{0,2},{1,3},{2,0},{3,1},{4,6},{5,7},{6,4},{7,5},{8,10},{9,11},{10,... | collective-permute-start | bytes 1769480 | tf_op jit(solution)/shard_map/ppermute | solution.py:790
  130.5 23.9 %collective-permute-start.14 = (bf16[384,768]{1,0:T(8,128)(2,1)}, bf16[384,768]{1,0:T(8,128)(2,1)}, u32[]{:S(2)}, u32[]{:S(2)}) collective-permute-start(bf16[384,768]{1,0:T(8,128)(2,1)} %get-tuple-element.163.refs_23_), channel_id=1, source_target_pairs={{0,4},{4,0},{8,12},{12,8},{16,20},{20,16},{24,28},{28,24},{1,5},{5... | collective-permute-start | bytes 1769480 | tf_op jit(solution)/shard_map/ppermute | solution.py:790
  152.8 8.5 %collective-permute-start.18 = (bf16[3,256,768]{2,1,0:T(8,128)(2,1)}, bf16[3,256,768]{2,1,0:T(8,128)(2,1)S(1)}, u32[]{:S(2)}, u32[]{:S(2)}) collective-permute-start(bf16[3,256,768]{2,1,0:T(8,128)(2,1)} %get-tuple-element.135), channel_id=1, source_target_pairs={{0,1},{1,0},{2,3},{3,2},{4,5},{5,4},{6,7},{7,6},{8,9},{9,8},{10,11... | collective-permute-start | bytes 3538952 | tf_op jit(solution)/shard_map/ppermute | solution.py:790
  152.9 1.5 copy-start.8
  155.7 1.1 copy-start.2
  155.7 1.2 copy-start.3
  155.7 1.2 copy-start.6
  156.9 4.4 %copy-start.14 = (bf16[3,256,768]{2,1,0:T(8,128)(2,1)S(1)}, bf16[3,256,768]{2,1,0:T(8,128)(2,1)}, u32[]{:S(2)}) copy-start(bf16[3,256,768]{2,1,0:T(8,128)(2,1)} %get-tuple-element.134) | copy-start | bytes 3538948
  157.6 15.8 %collective-permute-start.17 = (bf16[384,768]{1,0:T(8,128)(2,1)S(1)}, bf16[384,768]{1,0:T(8,128)(2,1)S(1)}, u32[]{:S(2)}, u32[]{:S(2)}) collective-permute-start(bf16[384,768]{1,0:T(8,128)(2,1)S(1)} %get-tuple-element.133), channel_id=1, source_target_pairs={{0,2},{1,3},{2,0},{3,1},{4,6},{5,7},{6,4},{7,5},{8,10},{9,11},{10,... | collective-permute-start | bytes 1769480 | tf_op jit(solution)/shard_map/ppermute | solution.py:790
  158.1 16.0 %collective-permute-start.15 = (bf16[400,768]{1,0:T(8,128)(2,1)S(1)}, bf16[400,768]{1,0:T(8,128)(2,1)S(1)}, u32[]{:S(2)}, u32[]{:S(2)}) collective-permute-start(bf16[400,768]{1,0:T(8,128)(2,1)S(1)} %get-tuple-element.130.refs_2_), channel_id=1, source_target_pairs={{0,4},{4,0},{8,12},{12,8},{16,20},{20,16},{24,28},{28,24},{1,5},{5... | collective-permute-start | bytes 1843208 | tf_op jit(solution)/shard_map/ppermute | solution.py:790
  159.7 13.8 %collective-permute-start.16 = (bf16[192,768]{1,0:T(8,128)(2,1)S(1)}, bf16[192,768]{1,0:T(8,128)(2,1)S(1)}, u32[]{:S(2)}, u32[]{:S(2)}) collective-permute-start(bf16[192,768]{1,0:T(8,128)(2,1)S(1)} %get-tuple-element.132), channel_id=1, source_target_pairs={{0,8},{4,12},{8,0},{12,4},{16,24},{20,28},{24,16},{28,20},{1,9},{5... | collective-permute-start | bytes 884744 | tf_op jit(solution)/shard_map/ppermute | solution.py:790
  161.6 12.4 %copy-start.4 = (bf16[384,768]{1,0:T(8,128)(2,1)S(1)}, bf16[384,768]{1,0:T(8,128)(2,1)}, u32[]{:S(2)}) copy-start(bf16[384,768]{1,0:T(8,128)(2,1)} %get-tuple-element.124.refs_0_) | copy-start | bytes 1769476
  174.8 16.6 %collective-permute-start.22 = (bf16[3,128,768]{2,1,0:T(8,128)(2,1)S(1)}, bf16[3,128,768]{2,1,0:T(8,128)(2,1)S(1)}, u32[]{:S(2)}, u32[]{:S(2)}) collective-permute-start(bf16[3,128,768]{2,1,0:T(8,128)(2,1)S(1)} %slice.143), channel_id=1, source_target_pairs={{0,2},{1,3},{2,0},{3,1},{4,6},{5,7},{6,4},{7,5},{8,10},{9,11},{10,... | collective-permute-start | bytes 1769480 | tf_op jit(solution)/shard_map/ppermute | solution.py:790
  176.5 14.9 %collective-permute-start.19 = (bf16[208,768]{1,0:T(8,128)(2,1)S(1)}, bf16[208,768]{1,0:T(8,128)(2,1)S(1)}, u32[]{:S(2)}, u32[]{:S(2)}) collective-permute-start(bf16[208,768]{1,0:T(8,128)(2,1)S(1)} %get-tuple-element.137.refs_2_), channel_id=1, source_target_pairs={{0,8},{4,12},{8,0},{12,4},{16,24},{20,28},{24,16},{28,20},{1,9},{5... | collective-permute-start | bytes 958472 | tf_op jit(solution)/shard_map/ppermute | solution.py:790
  178.1 12.4 %collective-permute-start.21 = (bf16[192,768]{1,0:T(8,128)(2,1)S(1)}, bf16[192,768]{1,0:T(8,128)(2,1)S(1)}, u32[]{:S(2)}, u32[]{:S(2)}) collective-permute-start(bf16[192,768]{1,0:T(8,128)(2,1)S(1)} %get-tuple-element.140), channel_id=1, source_target_pairs={{0,16},{4,20},{8,24},{12,28},{16,0},{20,4},{24,8},{28,12},{1,17},{... | collective-permute-start | bytes 884744 | tf_op jit(solution)/shard_map/ppermute | solution.py:790
  180.7 5.1 %collective-permute-start.20 = (bf16[96,768]{1,0:T(8,128)(2,1)S(1)}, bf16[96,768]{1,0:T(8,128)(2,1)S(1)}, u32[]{:S(2)}, u32[]{:S(2)}) collective-permute-start(bf16[96,768]{1,0:T(8,128)(2,1)S(1)} %get-tuple-element.139), channel_id=1, source_target_pairs={{0,4},{4,0},{8,12},{12,8},{16,20},{20,16},{24,28},{28,24},{1,5},{5... | collective-permute-start | bytes 442376 | tf_op jit(solution)/shard_map/ppermute | solution.py:790
  192.1 7.2 %collective-permute-start.25 = (bf16[192,768]{1,0:T(8,128)(2,1)S(1)}, bf16[192,768]{1,0:T(8,128)(2,1)S(1)}, u32[]{:S(2)}, u32[]{:S(2)}) collective-permute-start(bf16[192,768]{1,0:T(8,128)(2,1)S(1)} %get-tuple-element.146), channel_id=1, source_target_pairs={{0,2},{1,3},{2,0},{3,1},{4,6},{5,7},{6,4},{7,5},{8,10},{9,11},{10,... | collective-permute-start | bytes 884744 | tf_op jit(solution)/shard_map/ppermute | solution.py:790
  192.6 12.2 %collective-permute-start.23 = (bf16[112,768]{1,0:T(8,128)(2,1)S(1)}, bf16[112,768]{1,0:T(8,128)(2,1)S(1)}, u32[]{:S(2)}, u32[]{:S(2)}) collective-permute-start(bf16[112,768]{1,0:T(8,128)(2,1)S(1)} %get-tuple-element.143.refs_2_), channel_id=1, source_target_pairs={{0,16},{4,20},{8,24},{12,28},{16,0},{20,4},{24,8},{28,12},{1,17},{... | collective-permute-start | bytes 516104 | tf_op jit(solution)/shard_map/ppermute | solution.py:790
  195.3 9.5 %collective-permute-start.24 = (bf16[48,768]{1,0:T(8,128)(2,1)S(1)}, bf16[48,768]{1,0:T(8,128)(2,1)S(1)}, u32[]{:S(2)}, u32[]{:S(2)}) collective-permute-start(bf16[48,768]{1,0:T(8,128)(2,1)S(1)} %get-tuple-element.145), channel_id=1, source_target_pairs={{0,16},{4,20},{8,24},{12,28},{16,0},{20,4},{24,8},{28,12},{1,17},{... | collective-permute-start | bytes 221192 | tf_op jit(solution)/shard_map/ppermute | solution.py:790
  199.4 13.7 %collective-permute-start.30 = (bf16[2,192,768]{2,1,0:T(8,128)(2,1)S(1)}, bf16[2,192,768]{2,1,0:T(8,128)(2,1)S(1)}, u32[]{:S(2)}, u32[]{:S(2)}) collective-permute-start(bf16[2,192,768]{2,1,0:T(8,128)(2,1)S(1)} %reverse_select_fusion), channel_id=1, source_target_pairs={{0,1},{1,0},{2,3},{3,2},{4,5},{5,4},{6,7},{7,6},{8,9},{9,8},{10,11... | collective-permute-start | bytes 1769480 | tf_op jit(solution)/shard_map/ppermute | solution.py:790
  206.1 4.7 %collective-permute-start.26 = (bf16[48,768]{1,0:T(8,128)(2,1)S(1)}, bf16[48,768]{1,0:T(8,128)(2,1)S(1)}, u32[]{:S(2)}, u32[]{:S(2)}) collective-permute-start(bf16[48,768]{1,0:T(8,128)(2,1)S(1)} %get-tuple-element.147), channel_id=1, source_target_pairs={{0,2},{1,3},{2,0},{3,1},{4,6},{5,7},{6,4},{7,5},{8,10},{9,11},{10,... | collective-permute-start | bytes 221192 | tf_op jit(solution)/shard_map/ppermute | solution.py:790
  207.6 5.4 %collective-permute-start.27 = (bf16[112,768]{1,0:T(8,128)(2,1)S(1)}, bf16[112,768]{1,0:T(8,128)(2,1)S(1)}, u32[]{:S(2)}, u32[]{:S(2)}) collective-permute-start(bf16[112,768]{1,0:T(8,128)(2,1)S(1)} %get-tuple-element.148), channel_id=1, source_target_pairs={{0,2},{1,3},{2,0},{3,1},{4,6},{5,7},{6,4},{7,5},{8,10},{9,11},{10,... | collective-permute-start | bytes 516104 | tf_op jit(solution)/shard_map/ppermute | solution.py:790
  210.8 2.7 %collective-permute-start.28 = (bf16[96,768]{1,0:T(8,128)(2,1)S(1)}, bf16[96,768]{1,0:T(8,128)(2,1)S(1)}, u32[]{:S(2)}, u32[]{:S(2)}) collective-permute-start(bf16[96,768]{1,0:T(8,128)(2,1)S(1)} %pad_maximum_fusion.3.refs_0_), channel_id=1, source_target_pairs={{0,1},{1,0},{2,3},{3,2},{4,5},{5,4},{6,7},{7,6},{8,9},{9,8},{10,11... | collective-permute-start | bytes 442376 | tf_op jit(solution)/shard_map/ppermute | solution.py:790
  213.1 1.5 collective-permute-start.29
  213.4 4.0 %copy-start = (f32[96,3072]{1,0:T(8,128)}, f32[96,3072]{1,0:T(8,128)S(1)}, u32[]{:S(2)}) copy-start(f32[96,3072]{1,0:T(8,128)S(1)} %fusion.5.refs_7_) | copy-start | bytes 3538948
  213.5 3.9 %copy-start.1 = (f32[384,768]{1,0:T(8,128)}, f32[384,768]{1,0:T(8,128)S(1)}, u32[]{:S(2)}) copy-start(f32[384,768]{1,0:T(8,128)S(1)} %fusion.4.refs_6_) | copy-start | bytes 3538948

commit v5 on v4

--- a/solution.py
+++ b/solution.py
@@ -22,7 +22,7 @@
     return lax.dot_general(a, b, (((left,), (right,)), ((), ())), preferred_element_type=F32)
 
 
-def call(kernel, where, inputs, after, thread=None, *, grid, in_specs, out_specs, out_shape, us, name, scratch=(), mib=63):
+def call(kernel, where, inputs, after, thread=None, *, grid, in_specs, out_specs, out_shape, us, name, scratch=(), mib=62):
     plain = thread is None
     thread = thread or ()
     count = len(inputs)
@@ -492,13 +492,15 @@
         part = slice(h * HD, (h + 1) * HD)
         mixed = jnp.concatenate([mix_own[0, part], mix_sib[0, part]], axis=1)
         dm = jnp.concatenate([dm_own[0, part], dm_sib[0, part]], axis=1)
-        d_out = dm.astype(F32) * inv_ref[0, h : h + 1]
+        line = 8 * (h // 2) + h % 2
+        d_out = dm.astype(F32) * inv_ref[0, line : line + 1]
         delta = col_sum(d_out * mixed.astype(F32))
         d_low = d_out.astype(LOW)
         e = e_ref[0, h]
         dp = contract(v_ref[0, part], d_low, 0, 0)
         ds = (e.astype(F32) * (dp - delta)).astype(LOW)
-        at = lambda n: slice(n * tall + h * HD, n * tall + (h + 1) * HD)
+        base = (h // 2) * 6 * HD + (h % 2) * HD
+        at = lambda n: slice(base + 2 * n * HD, base + (2 * n + 1) * HD)
         grads[at(0)] = (contract(k_ref[0, part], ds, 1, 0) * scale).astype(LOW)
         grads[at(1)] = (contract(q_ref[0, part], ds, 1, 1) * scale).astype(LOW)
         grads[at(2)] = contract(d_low, e, 1, 1).astype(LOW)
@@ -556,45 +558,31 @@
     in_own, in_out, keep, send, result, grads, dq, dk, dv, acc, bias, packed, sems, room, join_sems = refs
     loads, stores = join_copies(where, out_own, out_got, room, result, join_sems)
     t = pl.program_id(0)
-    r = t // 2
-    width = acc.shape[1]
-    cols = grads.shape[1]
+    cols = acc.shape[1] // 2
     tall = cols // 3
-
     pl.when(t == 0)(lambda: begin(loads))
     pl.when(t == 1)(lambda: begin(stores, loads))
-    for p in range(2):
-
-        @pl.when(lax.rem(t, 2) == p)
-        def _():
-            lanes = slice(p * cols, (p + 1) * cols)
-            pair_back(step_refs, grads.at[p], acc.at[p], bias.at[:, lanes], r == 0)
-
-    @pl.when(lax.rem(t, 2) == 1)
-    def _():
-        for n, d in enumerate((dq, dk, dv)):
-            part = slice(n * tall, (n + 1) * tall)
-            d[:tall] = d0[0, part]
-            d[tall : 2 * tall] = grads[0, part]
-            d[2 * tall :] = grads[1, part]
-        back = contract(dq[...], wq[...], 0, 1)
-        back = back + contract(dk[...], wk[...], 0, 1) + contract(dv[...], wv[...], 0, 1)
-        half = back.shape[0] // 2
-        in_own[0] = (back[:half] + dbranch[0].astype(F32)).astype(LOW)
-        in_out[0] = back[half:].astype(LOW)
+    pair_back(step_refs, grads, acc, bias, t == 0)
+    for n, d in enumerate((dq, dk, dv)):
+        for p in range(2):
+            d[p * tall : (p + 1) * tall] = grads[p * cols + n * tall : p * cols + (n + 1) * tall]
+        d[2 * tall :] = d0[0, n * tall : (n + 1) * tall]
+    back = contract(dq[...], wq[...], 0, 1)
+    back = back + contract(dk[...], wk[...], 0, 1) + contract(dv[...], wv[...], 0, 1)
+    half = back.shape[0] // 2
+    in_own[0] = (back[:half] + dbranch[0].astype(F32)).astype(LOW)
+    in_out[0] = back[half:].astype(LOW)
 
     @pl.when(t == pl.num_programs(0) - 1)
     def _():
         core = where[0]
-        width = acc.shape[1]
-        for p in range(2):
-            spread(where, packed, acc.at[p], orders[3], 3, shards, slice(p * cols, (p + 1) * cols))
         wide = 2 * cols
+        spread(where, packed, acc, orders[3], 3, shards, slice(0, wide))
         lines = [vectors[:, n * wide : (n + 1) * wide] for n in range(vectors.shape[1] // wide)]
         zero = jnp.zeros((1, cols), F32)
         for n in (2, 0):
             at = lambda p: slice(p * cols + n * tall, p * cols + (n + 1) * tall)
-            line = jnp.concatenate([bias0[:1, n * tall : (n + 1) * tall], bias[:1, at(0)], bias[:1, at(1)]], axis=1)
+            line = jnp.concatenate([bias[:1, at(0)], bias[:1, at(1)], bias0[:1, n * tall : (n + 1) * tall]], axis=1)
             lines.append(jnp.concatenate([jnp.where(core == c, line, zero) for c in range(2)], axis=1))
         lines.append(jnp.zeros((TAIL - len(lines), wide), F32))
         packed[packed.shape[0] - TAIL :] = jnp.concatenate(lines, axis=0).astype(LOW)
@@ -602,24 +590,24 @@
         begin((), stores)
 
 
-def pair_specs(row, pair, x, attention):
+def pair_specs(pairs, at, x, attention):
     rows, cols, length = attention[0].shape
     width = x.shape[2]
-    step = 2
+    step = 2 * pairs
     tall = step * HD
-    row3 = lambda *s: pl.BlockSpec((1,) + s, lambda t, w: (row(t),) + (0,) * len(s))
-    big = pl.BlockSpec((1, tall, length), lambda t, w: (row(t), pair(t), 0))
-    small = pl.BlockSpec((1, tall, length // 2), lambda t, w: (row(t), pair(t), 0))
-    inv = pl.BlockSpec((1, 8, length), lambda t, w: (row(t), pair(t), 0))
+    row3 = lambda *s: pl.BlockSpec((1,) + s, lambda t, w: (t,) + (0,) * len(s))
+    big = pl.BlockSpec((1, tall, length), lambda t, w: (t, at, 0))
+    small = pl.BlockSpec((1, tall, length // 2), lambda t, w: (t, at, 0))
+    inv = pl.BlockSpec((1, 8 * pairs, length), lambda t, w: (t, at, 0))
     specs = [row3(length, width)] + [big] * 3
-    specs += [pl.BlockSpec((1, step, length, length), lambda t, w: (row(t), pair(t), 0, 0)), inv]
+    specs += [pl.BlockSpec((1, step, length, length), lambda t, w: (t, at, 0, 0)), inv]
     return specs + [small] * 4, row3
 
 
 def pair_grads(where, orders, shards, x, attention, o=(), after=(), thread=()):
     rows, cols, length = attention[0].shape
     width = x.shape[2]
-    specs, row3 = pair_specs(lambda t: t, lambda t: 0, x, attention)
+    specs, row3 = pair_specs(1, 2, x, attention)
     whole = lambda v: pl.BlockSpec(v.shape, lambda r, w: (0,) * len(v.shape))
     anywhere = pl.BlockSpec(memory_space=pl.ANY)
     total = cols + sum(v.shape[1] for v in o[:1])
@@ -642,7 +630,7 @@
 ):
     rows, cols, length = attention[0].shape
     width = x.shape[2]
-    specs, row3 = pair_specs(lambda t: t // 2, lambda t: 1 + t % 2, x, attention)
+    specs, row3 = pair_specs(2, 0, x, attention)
     whole = lambda v: pl.BlockSpec(v.shape, lambda t, w: (0,) * len(v.shape))
     weight = pl.BlockSpec((width, cols), lambda t, w: (0, w[0]), pipeline_mode=pl.Buffered(1))
     anywhere = pl.BlockSpec(memory_space=pl.ANY)
@@ -652,7 +640,7 @@
     return call(
         functools.partial(last_pairs_kernel, orders=orders, shards=shards), where,
         (x, *attention, d0, bias0, dbranch, *weights, vectors, out_own, out_got), after, thread,
-        grid=(2 * rows,),
+        grid=(rows,),
         in_specs=specs
         + [row3(cols, length), whole(bias0), row3(length // 2, width), weight, weight, weight, whole(vectors)]
         + [anywhere] * 2,
@@ -660,9 +648,9 @@
         out_shape=[SDS((rows, length // 2, width), LOW)] * 2
         + [SDS((half, 2 * cols), LOW), SDS((half + TAIL, 2 * cols), LOW)]
         + [SDS((2 * rows,) + out_own.shape[1:], LOW)],
-        scratch=[low(2, cols, length)]
+        scratch=[low(2 * cols, length)]
         + [low(cols, length)] * 3
-        + [pltpu.VMEM((2, width, cols), F32), pltpu.VMEM((8, 2 * cols), F32), low(width + TAIL, 2 * cols)]
+        + [pltpu.VMEM((width, 2 * cols), F32), pltpu.VMEM((8, 2 * cols), F32), low(width + TAIL, 2 * cols)]
         + [pltpu.SemaphoreType.DMA((2,)), low(2, *out_own.shape), pltpu.SemaphoreType.DMA((4,))],
         us=20,
         name="last_pair_grads",
@@ -747,8 +735,8 @@
 
     for n, ref in enumerate((gq, gk, gv)):
         for p in range(3):
-            mine, got = (a_mine, a_got) if p == 0 else (c_mine, c_got)
-            at = n * tall + (cols if p == 2 else 0)
+            mine, got = (a_mine, a_got) if p == 2 else (c_mine, c_got)
+            at = n * tall + (cols if p == 1 else 0)
             both(ref, p * tall, mine[:size, at : at + tall], got[:size, at : at + tall])
     both(go, 0, a_mine[:, cols:], a_got[:, cols:])
     total = c_mine[size:].astype(F32) + c_got[size:].astype(F32)
@@ -988,7 +976,7 @@
             tall = cols // 3
             whole_a = jnp.concatenate([a_keep, a_send], axis=0)
             whole_c = jnp.concatenate([c_keep, c_send[: c_keep.shape[0]]], axis=0)
-            groups = (whole_a, whole_c[:, :cols], whole_c[:, cols:])
+            groups = (whole_c[:, :cols], whole_c[:, cols:], whole_a)
             query_done, key_done, value_done = (
                 join(whole(jnp.concatenate([g[:, n * tall : (n + 1) * tall] for g in groups], axis=1)), 1)
                 for n in range(3)

time: 222 us -> 220 us (level)
  no operation moved by 1% of the time
where the time goes in v5:
time: 220 us; the launch traced here: 216 us
  Pallas kernels  106 us (48%)
  waiting for transfers between devices  59.6 us (27%)
  starting transfers between devices  28.5 us (13%)
  other arithmetic  13.1 us (6%)
  local copies, waits for them, and re-layouts  7.55 us (3%)
    pallas_call x11, Pallas kernels, call(): pl.pallas_call(body, grid_spec=pltpu.PrefetchScalarGridSpec(num_scalar_pr...  106 us
    ppermute x31, waiting for transfers between devices, swap(): return lax.ppermute(v, axis, [(i, i ^ mask) for i in range(size)])  59.6 us
    ppermute x31, starting transfers between devices, swap(): return lax.ppermute(v, axis, [(i, i ^ mask) for i in range(size)])  28.5 us
    convert_element_type x9, other arithmetic, add_low(): return (a.astype(F32) + b.astype(F32)).astype(LOW)  12.5 us
  transfers between devices with their start and end apart: 31, of which 15 were waited for; matrix products, arithmetic and copies ran while one was open for 7% of the time, Pallas kernels for 31%

profile of v5, /device:TPU:0, one launch (start us, length us, event | category | flops | bytes accessed | tf_op | source)
XLA Modules:
  0.0 216.1 jit_solution(15760326671345940798)
XLA Ops:
  0.7 1.4 constant_dynamic-slice_fusion.2
  2.1 3.0 %collective-permute-start = (bf16[3,128,768]{2,1,0:T(8,128)(2,1)S(1)}, bf16[3,128,768]{2,1,0:T(8,128)(2,1)S(1)}, u32[]{:S(2)}, u32[]{:S(2)}) collective-permute-start(bf16[3,128,768]{2,1,0:T(8,128)(2,1)S(1)} %get-tuple-element.179), channel_id=1, source_target_pairs={{0,2},{1,3},{2,0},{3,1},{4,6},{5,7},{6,4},{7,5},{8,10},{9,11},{10,... | collective-permute-start | bytes 1769480 | tf_op jit(solution)/shard_map/ppermute | solution.py:778
  5.1 13.3 %collective-permute-done.refs_1_ = bf16[3,128,768]{2,1,0:T(8,128)(2,1)S(1)} collective-permute-done((bf16[3,128,768]{2,1,0:T(8,128)(2,1)S(1)}, bf16[3,128,768]{2,1,0:T(8,128)(2,1)S(1)}, u32[]{:S(2)}, u32[]{:S(2)}) %collective-permute-start) | collective-permute-done | bytes 589856 | tf_op jit(solution)/shard_map/ppermute | solution.py:778
  18.5 1.2 constant_dynamic-slice_fusion
  19.7 1.8 collective-permute-start.4
  21.5 0.6 concatenate.38.w
  22.1 0.8 copy-done.21
  22.9 17.8 %attend.1 = (bf16[3,512,768]{2,1,0:T(8,128)(2,1)}, bf16[3,384,512]{2,1,0:T(8,128)(2,1)}, bf16[3,384,512]{2,1,0:T(8,128)(2,1)}, bf16[3,384,512]{2,1,0:T(8,128)(2,...) custom-call(s32[68]{0:T(128)} %concatenate.38.w, ...), custom_call_target="tpu_custom_call" | custom-call | flops 900000000 | tf_op jit(solution)/shard_map/attend/pallas_call | solution.py:37
  40.9 2.1 collective-permute-done.3.refs_1_
  43.1 0.8 copy-done.11
  43.9 33.9 %forward.1 = (f32[1,5376]{1,0:T(1,128)}, bf16[3,128,768]{2,1,0:T(8,128)(2,1)}, bf16[3,128,768]{2,1,0:T(8,128)(2,1)}, bf16[768,3072]{1,0:T(8,128)(2,1)}, f32[768,...) custom-call(s32[68]{0:T(128)} %concatenate.38.w, ...), custom_call_target="tpu_custom_call" | custom-call | flops 1350000000 | tf_op jit(solution)/shard_map/forward/pallas_call | solution.py:37
  77.8 0.2 collective-permute-start.5
  78.0 4.6 %collective-permute-done.5.refs_1_ = bf16[1536,768]{1,0:T(8,128)(2,1)S(1)} collective-permute-done((bf16[1536,768]{1,0:T(8,128)(2,1)}, bf16[1536,768]{1,0:T(8,128)(2,1)S(1)}, u32[]{:S(2)}, u32[]{:S(2)}) %collective-permute-start.5) | collective-permute-done | bytes 2359328 | tf_op jit(solution)/shard_map/ppermute | solution.py:778
  82.6 0.5 gate.1
  83.1 0.2 collective-permute-start.6
  83.3 0.9 copy-done.15
  84.4 2.1 fusion.1
  86.6 1.5 collective-permute-start.10
  88.2 0.6 collective-permute-start.9
  88.8 2.1 fusion
  90.9 1.6 collective-permute-start.11
  92.5 15.7 %branch.1 = (f32[1,7680]{1,0:T(1,128)}, bf16[768,768]{1,0:T(8,128)(2,1)}, bf16[3,384,256]{2,1,0:T(8,128)(2,1)}, bf16[3,384,256]{2,1,0:T(8,128)(2,1)}, bf16[16,48...) custom-call(s32[68]{0:T(128)} %concatenate.38.w, ...), custom_call_target="tpu_custom_call", output_to_operand_aliasing={{6}: (11, {}), {7}: (12, {}), {8}: (13, {})} | custom-call | flops 650000000 | tf_op jit(solution)/shard_map/branch/pallas_call | solution.py:37
  108.4 0.5 collective-permute-start.8
  108.9 1.8 collective-permute-done.7.refs_9_
  110.7 0.8 collective-permute-done.8.refs_11_
  111.5 10.9 %pair_grads.1 = (bf16[3,384,512]{2,1,0:T(8,128)(2,1)}, f32[8,384]{1,0:T(8,128)}, bf16[384,768]{1,0:T(8,128)(2,1)}, bf16[384,768]{1,0:T(8,128)(2,1)}, bf16[768,768]{1,0:T(8,128)(2,1)}, /*index=5*/bf16[768,768]{1,0:T(8,128)(2,1)}) custom-call(s32[68]{0:T(128)} %concatenate.38.w, ...), custom_call_target="tpu_custom_call", output_to_operand_aliasing={{4}: (13, {}), {5}: (14, {})} | custom-call | flops 400000000 | tf_op jit(solution)/shard_map/pair_grads/pallas_call | solution.py:37
  122.5 2.8 %add_convert_fusion.4 = (bf16[384,768]{1,0:T(8,128)(2,1)S(1)}, bf16[384,768]{1,0:T(8,128)(2,1)}) fusion(bf16[768,768]{1,0:T(8,128)(2,1)} %collective-permute-done.10, bf16[768,768]{1,0:T(8,128)(2,1)} %get-tuple-element.120), kind=kLoop, calls=%fused_computation.12 | loop fusion | flops 2359296 | bytes 3538944 | tf_op jit(solution)/shard_map/convert_element_type | solution.py:782
  125.3 0.4 collective-permute-start.13
  125.7 1.5 collective-permute-start.12
  127.3 2.4 %add_convert_fusion.3 = (bf16[384,768]{1,0:T(8,128)(2,1)S(1)}, bf16[384,768]{1,0:T(8,128)(2,1)}) fusion(bf16[768,768]{1,0:T(8,128)(2,1)} %collective-permute-done.11, bf16[768,768]{1,0:T(8,128)(2,1)S(1)} %copy-done.7), kind=kLoop, calls=%fused_computation.11 | loop fusion | flops 2359296 | bytes 3538944 | tf_op jit(solution)/shard_map/convert_element_type | solution.py:782
  129.7 0.8 collective-permute-start.14
  130.5 20.8 %last_pair_grads.1 = (bf16[3,256,768]{2,1,0:T(8,128)(2,1)}, bf16[3,256,768]{2,1,0:T(8,128)(2,1)}, bf16[384,768]{1,0:T(8,128)(2,1)}, bf16[400,768]{1,0:T(8,128)(2...) custom-call(s32[68]{0:T(128)} %concatenate.38.w, ...), custom_call_target="tpu_custom_call", output_to_operand_aliasing={{5}: (20, {}), {6}: (21, {}), {7}: (22, {})} | custom-call | flops 1000000000 | tf_op jit(solution)/shard_map/last_pair_grads/pallas_call | solution.py:37
  151.4 1.4 add_convert_fusion.2
  152.9 1.2 add_convert_fusion.1
  154.3 0.9 copy-done.2
  155.2 0.2 copy-done.3
  155.4 0.7 next_round.4
  156.1 0.6 collective-permute-start.17
  156.7 1.2 collective-permute-start.15
  157.9 1.6 collective-permute-start.16
  159.4 0.3 add_convert_fusion.refs_6_
  159.7 12.1 %collective-permute-done.17 = bf16[384,768]{1,0:T(8,128)(2,1)S(1)} collective-permute-done((bf16[384,768]{1,0:T(8,128)(2,1)S(1)}, bf16[384,768]{1,0:T(8,128)(2,1)S(1)}, u32[]{:S(2)}, u32[]{:S(2)}) %collective-permute-start.17) | collective-permute-done | bytes 589856 | tf_op jit(solution)/shard_map/ppermute | solution.py:778
  172.0 0.6 collective-permute-done.15.refs_1_
  172.6 0.7 next_round.5
  173.4 1.6 collective-permute-start.22
  175.0 1.6 collective-permute-start.19
  176.6 2.6 %collective-permute-start.21 = (bf16[192,768]{1,0:T(8,128)(2,1)S(1)}, bf16[192,768]{1,0:T(8,128)(2,1)S(1)}, u32[]{:S(2)}, u32[]{:S(2)}) collective-permute-start(bf16[192,768]{1,0:T(8,128)(2,1)S(1)} %get-tuple-element.140), channel_id=1, source_target_pairs={{0,16},{4,20},{8,24},{12,28},{16,0},{20,4},{24,8},{28,12},{1,17},{... | collective-permute-start | bytes 884744 | tf_op jit(solution)/shard_map/ppermute | solution.py:778
  179.2 1.2 collective-permute-start.20
  180.4 4.0 %collective-permute-done.20.refs_4_ = bf16[96,768]{1,0:T(8,128)(2,1)S(1)} collective-permute-done((bf16[96,768]{1,0:T(8,128)(2,1)S(1)}, bf16[96,768]{1,0:T(8,128)(2,1)S(1)}, u32[]{:S(2)}, u32[]{:S(2)}) %collective-permute-start.20) | collective-permute-done | bytes 147488 | tf_op jit(solution)/shard_map/ppermute | solution.py:778
  184.3 4.7 %collective-permute-done.21.refs_6_ = bf16[192,768]{1,0:T(8,128)(2,1)S(1)} collective-permute-done((bf16[192,768]{1,0:T(8,128)(2,1)S(1)}, bf16[192,768]{1,0:T(8,128)(2,1)S(1)}, u32[]{:S(2)}, u32[]{:S(2)}) %collective-permute-start.21) | collective-permute-done | bytes 294944 | tf_op jit(solution)/shard_map/ppermute | solution.py:778
  189.0 0.9 collective-permute-done.19.refs_1_
  189.9 0.7 next_round.6
  190.6 0.6 collective-permute-start.25
  191.2 2.6 %collective-permute-start.23 = (bf16[112,768]{1,0:T(8,128)(2,1)S(1)}, bf16[112,768]{1,0:T(8,128)(2,1)S(1)}, u32[]{:S(2)}, u32[]{:S(2)}) collective-permute-start(bf16[112,768]{1,0:T(8,128)(2,1)S(1)} %get-tuple-element.143.refs_2_), channel_id=1, source_target_pairs={{0,16},{4,20},{8,24},{12,28},{16,0},{20,4},{24,8},{28,12},{1,17},{... | collective-permute-start | bytes 516104 | tf_op jit(solution)/shard_map/ppermute | solution.py:778
  193.8 0.3 collective-permute-start.24
  194.1 3.7 %collective-permute-done.25.refs_5_ = bf16[192,768]{1,0:T(8,128)(2,1)S(1)} collective-permute-done((bf16[192,768]{1,0:T(8,128)(2,1)S(1)}, bf16[192,768]{1,0:T(8,128)(2,1)S(1)}, u32[]{:S(2)}, u32[]{:S(2)}) %collective-permute-start.25) | collective-permute-done | bytes 294944 | tf_op jit(solution)/shard_map/ppermute | solution.py:778
  198.1 5.2 %collective-permute-done.24.refs_4_ = bf16[48,768]{1,0:T(8,128)(2,1)S(1)} collective-permute-done((bf16[48,768]{1,0:T(8,128)(2,1)S(1)}, bf16[48,768]{1,0:T(8,128)(2,1)S(1)}, u32[]{:S(2)}, u32[]{:S(2)}) %collective-permute-start.24) | collective-permute-done | bytes 73760 | tf_op jit(solution)/shard_map/ppermute | solution.py:778
  203.3 1.3 next_round.7
  204.6 1.5 collective-permute-start.26
  206.0 0.5 collective-permute-start.27
  206.6 2.6 %collective-permute-done.26 = bf16[48,768]{1,0:T(8,128)(2,1)S(1)} collective-permute-done((bf16[48,768]{1,0:T(8,128)(2,1)S(1)}, bf16[48,768]{1,0:T(8,128)(2,1)S(1)}, u32[]{:S(2)}, u32[]{:S(2)}) %collective-permute-start.26) | collective-permute-done | bytes 73760 | tf_op jit(solution)/shard_map/ppermute | solution.py:778
  209.3 2.1 collective-permute-done.27
  212.0 1.0 collective-permute-done.29.refs_3_
  213.0 2.9 %finish.1 = (bf16[6,128,768]{2,1,0:T(8,128)(2,1)}, f32[96,768]{1,0:T(8,128)}, f32[96,768]{1,0:T(8,128)}, f32[96,768]{1,0:T(8,128)}, f32[96,768]{1,0:T(8,128)}, /...) custom-call(s32[68]{0:T(128)S(1)} %copy-done.6, ...), custom_call_target="tpu_custom_call" | custom-call | flops 100000000 | tf_op jit(solution)/shard_map/finish/pallas_call | solution.py:37
  (84 shorter events, 2.0 us)
Async XLA Ops:
  0.7 17.8 %copy-start.18 = (bf16[6,128,768]{2,1,0:T(8,128)(2,1)S(1)}, bf16[6,128,768]{2,1,0:T(8,128)(2,1)}, u32[]{:S(2)}) copy-start(bf16[6,128,768]{2,1,0:T(8,128)(2,1)} %param.35) | copy-start | bytes 3538948
  2.1 17.6 %copy-start.16 = (bf16[3,128,768]{2,1,0:T(8,128)(2,1)}, bf16[3,128,768]{2,1,0:T(8,128)(2,1)S(1)}, u32[]{:S(2)}) copy-start(bf16[3,128,768]{2,1,0:T(8,128)(2,1)S(1)} %get-tuple-element.180.refs_0_) | copy-start | bytes 1769476
  2.1 16.4 %collective-permute-start = (bf16[3,128,768]{2,1,0:T(8,128)(2,1)S(1)}, bf16[3,128,768]{2,1,0:T(8,128)(2,1)S(1)}, u32[]{:S(2)}, u32[]{:S(2)}) collective-permute-start(bf16[3,128,768]{2,1,0:T(8,128)(2,1)S(1)} %get-tuple-element.179), channel_id=1, source_target_pairs={{0,2},{1,3},{2,0},{3,1},{4,6},{5,7},{6,4},{7,5},{8,10},{9,11},{10,... | collective-permute-start | bytes 1769480 | tf_op jit(solution)/shard_map/ppermute | solution.py:778
  5.1 17.0 %collective-permute-start.1 = (bf16[3,128,768]{2,1,0:T(8,128)(2,1)S(1)}, bf16[3,128,768]{2,1,0:T(8,128)(2,1)S(1)}, u32[]{:S(2)}, u32[]{:S(2)}) collective-permute-start(bf16[3,128,768]{2,1,0:T(8,128)(2,1)S(1)} %get-tuple-element.180.refs_0_), channel_id=1, source_target_pairs={{0,1},{1,0},{2,3},{3,2},{4,5},{5,4},{6,7},{7,6},{8,9},{9,8},{10,11... | collective-permute-start | bytes 1769480 | tf_op jit(solution)/shard_map/ppermute | solution.py:778
  18.5 1.2 copy-start.20
  18.5 4.4 %collective-permute-start.2 = (bf16[3,128,768]{2,1,0:T(8,128)(2,1)S(1)}, bf16[3,128,768]{2,1,0:T(8,128)(2,1)}, u32[]{:S(2)}, u32[]{:S(2)}) collective-permute-start(bf16[3,128,768]{2,1,0:T(8,128)(2,1)S(1)} %collective-permute-done.refs_1_), channel_id=1, source_target_pairs={{0,1},{1,0},{2,3},{3,2},{4,5},{5,4},{6,7},{7,6},{8,9},{9,8},{10,11... | collective-permute-start | bytes 1769480 | tf_op jit(solution)/shard_map/ppermute | solution.py:778
  19.7 21.2 %collective-permute-start.4 = (bf16[3,128,768]{2,1,0:T(8,128)(2,1)}, bf16[3,128,768]{2,1,0:T(8,128)(2,1)S(1)}, u32[]{:S(2)}, u32[]{:S(2)}) collective-permute-start(bf16[3,128,768]{2,1,0:T(8,128)(2,1)} %get-tuple-element.177), channel_id=1, source_target_pairs={{0,2},{1,3},{2,0},{3,1},{4,6},{5,7},{6,4},{7,5},{8,10},{9,11},{10,... | collective-permute-start | bytes 1769480 | tf_op jit(solution)/shard_map/ppermute | solution.py:778
  22.1 0.8 copy-start.21
  40.8 2.3 %collective-permute-start.3 = (bf16[3,384,256]{2,1,0:T(8,128)(2,1)}, bf16[3,384,256]{2,1,0:T(8,128)(2,1)S(1)}, u32[]{:S(2)}, u32[]{:S(2)}) collective-permute-start(bf16[3,384,256]{2,1,0:T(8,128)(2,1)} %get-tuple-element.97.refs_7_), channel_id=1, source_target_pairs={{0,1},{1,0},{2,3},{3,2},{4,5},{5,4},{6,7},{7,6},{8,9},{9,8},{10,11... | collective-permute-start | bytes 1769480 | tf_op jit(solution)/shard_map/ppermute | solution.py:778
  40.9 2.1 copy-start.19
  43.0 0.8 copy-start.11
  43.9 38.7 %copy-start.5 = (s32[68]{0:T(128)S(1)}, s32[68]{0:T(128)}, u32[]{:S(2)}) copy-start(s32[68]{0:T(128)} %concatenate.38.w) | copy-start | bytes 820
  77.8 4.8 %collective-permute-start.5 = (bf16[1536,768]{1,0:T(8,128)(2,1)}, bf16[1536,768]{1,0:T(8,128)(2,1)S(1)}, u32[]{:S(2)}, u32[]{:S(2)}) collective-permute-start(bf16[1536,768]{1,0:T(8,128)(2,1)} %bitcast.64), channel_id=1, source_target_pairs={{0,1},{1,0},{2,3},{3,2},{4,5},{5,4},{6,7},{7,6},{8,9},{9,8},{10,11... | collective-permute-start | bytes 7077896 | tf_op jit(solution)/shard_map/ppermute | solution.py:778
  82.6 1.7 copy-start.15
  83.1 5.7 %collective-permute-start.6 = (bf16[1536,768]{1,0:T(8,128)(2,1)}, bf16[1536,768]{1,0:T(8,128)(2,1)S(1)}, u32[]{:S(2)}, u32[]{:S(2)}) collective-permute-start(bf16[1536,768]{1,0:T(8,128)(2,1)} %gate.1), channel_id=1, source_target_pairs={{0,1},{1,0},{2,3},{3,2},{4,5},{5,4},{6,7},{7,6},{8,9},{9,8},{10,11... | collective-permute-start | bytes 7077896 | tf_op jit(solution)/shard_map/ppermute | solution.py:778
  84.4 3.7 %copy-start.14 = (bf16[16,96,768]{2,1,0:T(8,128)(2,1)S(1)}, bf16[16,96,768]{2,1,0:T(8,128)(2,1)}, u32[]{:S(2)}) copy-start(bf16[16,96,768]{2,1,0:T(8,128)(2,1)} %get-tuple-element.106) | copy-start | bytes 7077892
  86.6 1.7 copy-start.9
  86.6 35.9 %collective-permute-start.10 = (bf16[768,768]{1,0:T(8,128)(2,1)S(1)}, bf16[768,768]{1,0:T(8,128)(2,1)}, u32[]{:S(2)}, u32[]{:S(2)}) collective-permute-start(bf16[768,768]{1,0:T(8,128)(2,1)S(1)} %get-tuple-element.171.refs_13_), channel_id=1, source_target_pairs={{0,4},{4,0},{8,12},{12,8},{16,20},{20,16},{24,28},{28,24},{1,5},{5... | collective-permute-start | bytes 3538952 | tf_op jit(solution)/shard_map/ppermute | solution.py:778
  88.2 20.6 %collective-permute-start.9 = (bf16[3,128,768]{2,1,0:T(8,128)(2,1)}, bf16[3,128,768]{2,1,0:T(8,128)(2,1)S(1)}, u32[]{:S(2)}, u32[]{:S(2)}) collective-permute-start(bf16[3,128,768]{2,1,0:T(8,128)(2,1)} %get-tuple-element.114), channel_id=1, source_target_pairs={{0,2},{1,3},{2,0},{3,1},{4,6},{5,7},{6,4},{7,5},{8,10},{9,11},{10,... | collective-permute-start | bytes 1769480 | tf_op jit(solution)/shard_map/ppermute | solution.py:778
  90.9 36.3 %collective-permute-start.11 = (bf16[768,768]{1,0:T(8,128)(2,1)}, bf16[768,768]{1,0:T(8,128)(2,1)}, u32[]{:S(2)}, u32[]{:S(2)}) collective-permute-start(bf16[768,768]{1,0:T(8,128)(2,1)} %get-tuple-element.167.refs_14_), channel_id=1, source_target_pairs={{0,8},{4,12},{8,0},{12,4},{16,24},{20,28},{24,16},{28,20},{1,9},{5... | collective-permute-start | bytes 3538952 | tf_op jit(solution)/shard_map/ppermute | solution.py:778
  108.3 2.4 %collective-permute-start.7 = (bf16[3,384,256]{2,1,0:T(8,128)(2,1)}, bf16[3,384,256]{2,1,0:T(8,128)(2,1)}, u32[]{:S(2)}, u32[]{:S(2)}) collective-permute-start(bf16[3,384,256]{2,1,0:T(8,128)(2,1)} %get-tuple-element.109), channel_id=1, source_target_pairs={{0,1},{1,0},{2,3},{3,2},{4,5},{5,4},{6,7},{7,6},{8,9},{9,8},{10,11... | collective-permute-start | bytes 1769480 | tf_op jit(solution)/shard_map/ppermute | solution.py:778
  108.4 3.2 %collective-permute-start.8 = (bf16[768,384]{1,0:T(8,128)(2,1)}, bf16[768,384]{1,0:T(8,128)(2,1)}, u32[]{:S(2)}, u32[]{:S(2)}) collective-permute-start(bf16[768,384]{1,0:T(8,128)(2,1)} %bitcast.65), channel_id=1, source_target_pairs={{0,1},{1,0},{2,3},{3,2},{4,5},{5,4},{6,7},{7,6},{8,9},{9,8},{10,11... | collective-permute-start | bytes 1769480 | tf_op jit(solution)/shard_map/ppermute | solution.py:778
  108.9 2.7 %copy-start.10 = (bf16[3,128,768]{2,1,0:T(8,128)(2,1)}, bf16[3,128,768]{2,1,0:T(8,128)(2,1)S(1)}, u32[]{:S(2)}) copy-start(bf16[3,128,768]{2,1,0:T(8,128)(2,1)S(1)} %collective-permute-done.9.refs_14_.refs_18_) | copy-start | bytes 1769476
  122.5 4.8 %copy-start.7 = (bf16[768,768]{1,0:T(8,128)(2,1)S(1)}, bf16[768,768]{1,0:T(8,128)(2,1)}, u32[]{:S(2)}) copy-start(bf16[768,768]{1,0:T(8,128)(2,1)} %get-tuple-element.121) | copy-start | bytes 3538948
  125.3 4.4 %copy-start.12 = (bf16[384,768]{1,0:T(8,128)(2,1)}, bf16[384,768]{1,0:T(8,128)(2,1)S(1)}, u32[]{:S(2)}) copy-start(bf16[384,768]{1,0:T(8,128)(2,1)S(1)} %get-tuple-element.165.refs_22_) | copy-start | bytes 1769476
  125.3 26.1 %collective-permute-start.13 = (bf16[384,768]{1,0:T(8,128)(2,1)S(1)}, bf16[384,768]{1,0:T(8,128)(2,1)}, u32[]{:S(2)}, u32[]{:S(2)}) collective-permute-start(bf16[384,768]{1,0:T(8,128)(2,1)S(1)} %get-tuple-element.165.refs_22_), channel_id=1, source_target_pairs={{0,8},{4,12},{8,0},{12,4},{16,24},{20,28},{24,16},{28,20},{1,9},{5... | collective-permute-start | bytes 1769480 | tf_op jit(solution)/shard_map/ppermute | solution.py:778
  125.7 28.6 %collective-permute-start.12 = (bf16[384,768]{1,0:T(8,128)(2,1)}, bf16[384,768]{1,0:T(8,128)(2,1)S(1)}, u32[]{:S(2)}, u32[]{:S(2)}) collective-permute-start(bf16[384,768]{1,0:T(8,128)(2,1)} %get-tuple-element.126), channel_id=1, source_target_pairs={{0,2},{1,3},{2,0},{3,1},{4,6},{5,7},{6,4},{7,5},{8,10},{9,11},{10,... | collective-permute-start | bytes 1769480 | tf_op jit(solution)/shard_map/ppermute | solution.py:778
  129.6 0.8 copy-start.13
  129.7 23.2 %collective-permute-start.14 = (bf16[384,768]{1,0:T(8,128)(2,1)S(1)}, bf16[384,768]{1,0:T(8,128)(2,1)}, u32[]{:S(2)}, u32[]{:S(2)}) collective-permute-start(bf16[384,768]{1,0:T(8,128)(2,1)S(1)} %get-tuple-element.163.refs_23_), channel_id=1, source_target_pairs={{0,4},{4,0},{8,12},{12,8},{16,20},{20,16},{24,28},{28,24},{1,5},{5... | collective-permute-start | bytes 1769480 | tf_op jit(solution)/shard_map/ppermute | solution.py:778
  151.3 8.2 %collective-permute-start.18 = (bf16[3,256,768]{2,1,0:T(8,128)(2,1)}, bf16[3,256,768]{2,1,0:T(8,128)(2,1)S(1)}, u32[]{:S(2)}, u32[]{:S(2)}) collective-permute-start(bf16[3,256,768]{2,1,0:T(8,128)(2,1)} %get-tuple-element.135), channel_id=1, source_target_pairs={{0,1},{1,0},{2,3},{3,2},{4,5},{5,4},{6,7},{7,6},{8,9},{9,8},{10,11... | collective-permute-start | bytes 3538952 | tf_op jit(solution)/shard_map/ppermute | solution.py:778
  151.4 1.5 copy-start.8
  154.2 1.1 copy-start.2
  154.2 1.2 copy-start.3
  154.2 1.2 copy-start.6
  155.4 4.0 %copy-start.17 = (bf16[3,256,768]{2,1,0:T(8,128)(2,1)S(1)}, bf16[3,256,768]{2,1,0:T(8,128)(2,1)}, u32[]{:S(2)}) copy-start(bf16[3,256,768]{2,1,0:T(8,128)(2,1)} %get-tuple-element.134) | copy-start | bytes 3538948
  156.1 15.8 %collective-permute-start.17 = (bf16[384,768]{1,0:T(8,128)(2,1)S(1)}, bf16[384,768]{1,0:T(8,128)(2,1)S(1)}, u32[]{:S(2)}, u32[]{:S(2)}) collective-permute-start(bf16[384,768]{1,0:T(8,128)(2,1)S(1)} %get-tuple-element.133), channel_id=1, source_target_pairs={{0,2},{1,3},{2,0},{3,1},{4,6},{5,7},{6,4},{7,5},{8,10},{9,11},{10,... | collective-permute-start | bytes 1769480 | tf_op jit(solution)/shard_map/ppermute | solution.py:778
  156.7 16.0 %collective-permute-start.15 = (bf16[400,768]{1,0:T(8,128)(2,1)S(1)}, bf16[400,768]{1,0:T(8,128)(2,1)S(1)}, u32[]{:S(2)}, u32[]{:S(2)}) collective-permute-start(bf16[400,768]{1,0:T(8,128)(2,1)S(1)} %get-tuple-element.130.refs_2_), channel_id=1, source_target_pairs={{0,4},{4,0},{8,12},{12,8},{16,20},{20,16},{24,28},{28,24},{1,5},{5... | collective-permute-start | bytes 1843208 | tf_op jit(solution)/shard_map/ppermute | solution.py:778
  157.9 14.2 %collective-permute-start.16 = (bf16[192,768]{1,0:T(8,128)(2,1)S(1)}, bf16[192,768]{1,0:T(8,128)(2,1)S(1)}, u32[]{:S(2)}, u32[]{:S(2)}) collective-permute-start(bf16[192,768]{1,0:T(8,128)(2,1)S(1)} %get-tuple-element.132), channel_id=1, source_target_pairs={{0,8},{4,12},{8,0},{12,4},{16,24},{20,28},{24,16},{28,20},{1,9},{5... | collective-permute-start | bytes 884744 | tf_op jit(solution)/shard_map/ppermute | solution.py:778
  159.7 12.9 %copy-start.4 = (bf16[384,768]{1,0:T(8,128)(2,1)S(1)}, bf16[384,768]{1,0:T(8,128)(2,1)}, u32[]{:S(2)}) copy-start(bf16[384,768]{1,0:T(8,128)(2,1)} %get-tuple-element.124.refs_0_) | copy-start | bytes 1769476
  173.4 16.4 %collective-permute-start.22 = (bf16[3,128,768]{2,1,0:T(8,128)(2,1)S(1)}, bf16[3,128,768]{2,1,0:T(8,128)(2,1)S(1)}, u32[]{:S(2)}, u32[]{:S(2)}) collective-permute-start(bf16[3,128,768]{2,1,0:T(8,128)(2,1)S(1)} %slice.143), channel_id=1, source_target_pairs={{0,2},{1,3},{2,0},{3,1},{4,6},{5,7},{6,4},{7,5},{8,10},{9,11},{10,... | collective-permute-start | bytes 1769480 | tf_op jit(solution)/shard_map/ppermute | solution.py:778
  175.0 14.9 %collective-permute-start.19 = (bf16[208,768]{1,0:T(8,128)(2,1)S(1)}, bf16[208,768]{1,0:T(8,128)(2,1)S(1)}, u32[]{:S(2)}, u32[]{:S(2)}) collective-permute-start(bf16[208,768]{1,0:T(8,128)(2,1)S(1)} %get-tuple-element.137.refs_2_), channel_id=1, source_target_pairs={{0,8},{4,12},{8,0},{12,4},{16,24},{20,28},{24,16},{28,20},{1,9},{5... | collective-permute-start | bytes 958472 | tf_op jit(solution)/shard_map/ppermute | solution.py:778
  176.6 12.4 %collective-permute-start.21 = (bf16[192,768]{1,0:T(8,128)(2,1)S(1)}, bf16[192,768]{1,0:T(8,128)(2,1)S(1)}, u32[]{:S(2)}, u32[]{:S(2)}) collective-permute-start(bf16[192,768]{1,0:T(8,128)(2,1)S(1)} %get-tuple-element.140), channel_id=1, source_target_pairs={{0,16},{4,20},{8,24},{12,28},{16,0},{20,4},{24,8},{28,12},{1,17},{... | collective-permute-start | bytes 884744 | tf_op jit(solution)/shard_map/ppermute | solution.py:778
  179.2 5.1 %collective-permute-start.20 = (bf16[96,768]{1,0:T(8,128)(2,1)S(1)}, bf16[96,768]{1,0:T(8,128)(2,1)S(1)}, u32[]{:S(2)}, u32[]{:S(2)}) collective-permute-start(bf16[96,768]{1,0:T(8,128)(2,1)S(1)} %get-tuple-element.139), channel_id=1, source_target_pairs={{0,4},{4,0},{8,12},{12,8},{16,20},{20,16},{24,28},{28,24},{1,5},{5... | collective-permute-start | bytes 442376 | tf_op jit(solution)/shard_map/ppermute | solution.py:778
  190.6 7.2 %collective-permute-start.25 = (bf16[192,768]{1,0:T(8,128)(2,1)S(1)}, bf16[192,768]{1,0:T(8,128)(2,1)S(1)}, u32[]{:S(2)}, u32[]{:S(2)}) collective-permute-start(bf16[192,768]{1,0:T(8,128)(2,1)S(1)} %get-tuple-element.146), channel_id=1, source_target_pairs={{0,2},{1,3},{2,0},{3,1},{4,6},{5,7},{6,4},{7,5},{8,10},{9,11},{10,... | collective-permute-start | bytes 884744 | tf_op jit(solution)/shard_map/ppermute | solution.py:778
  191.2 12.1 %collective-permute-start.23 = (bf16[112,768]{1,0:T(8,128)(2,1)S(1)}, bf16[112,768]{1,0:T(8,128)(2,1)S(1)}, u32[]{:S(2)}, u32[]{:S(2)}) collective-permute-start(bf16[112,768]{1,0:T(8,128)(2,1)S(1)} %get-tuple-element.143.refs_2_), channel_id=1, source_target_pairs={{0,16},{4,20},{8,24},{12,28},{16,0},{20,4},{24,8},{28,12},{1,17},{... | collective-permute-start | bytes 516104 | tf_op jit(solution)/shard_map/ppermute | solution.py:778
  193.8 9.5 %collective-permute-start.24 = (bf16[48,768]{1,0:T(8,128)(2,1)S(1)}, bf16[48,768]{1,0:T(8,128)(2,1)S(1)}, u32[]{:S(2)}, u32[]{:S(2)}) collective-permute-start(bf16[48,768]{1,0:T(8,128)(2,1)S(1)} %get-tuple-element.145), channel_id=1, source_target_pairs={{0,16},{4,20},{8,24},{12,28},{16,0},{20,4},{24,8},{28,12},{1,17},{... | collective-permute-start | bytes 221192 | tf_op jit(solution)/shard_map/ppermute | solution.py:778
  197.9 13.6 %collective-permute-start.30 = (bf16[2,192,768]{2,1,0:T(8,128)(2,1)S(1)}, bf16[2,192,768]{2,1,0:T(8,128)(2,1)S(1)}, u32[]{:S(2)}, u32[]{:S(2)}) collective-permute-start(bf16[2,192,768]{2,1,0:T(8,128)(2,1)S(1)} %reverse_select_fusion), channel_id=1, source_target_pairs={{0,1},{1,0},{2,3},{3,2},{4,5},{5,4},{6,7},{7,6},{8,9},{9,8},{10,11... | collective-permute-start | bytes 1769480 | tf_op jit(solution)/shard_map/ppermute | solution.py:778
  204.6 4.6 %collective-permute-start.26 = (bf16[48,768]{1,0:T(8,128)(2,1)S(1)}, bf16[48,768]{1,0:T(8,128)(2,1)S(1)}, u32[]{:S(2)}, u32[]{:S(2)}) collective-permute-start(bf16[48,768]{1,0:T(8,128)(2,1)S(1)} %get-tuple-element.147), channel_id=1, source_target_pairs={{0,2},{1,3},{2,0},{3,1},{4,6},{5,7},{6,4},{7,5},{8,10},{9,11},{10,... | collective-permute-start | bytes 221192 | tf_op jit(solution)/shard_map/ppermute | solution.py:778
  206.0 5.4 %collective-permute-start.27 = (bf16[112,768]{1,0:T(8,128)(2,1)S(1)}, bf16[112,768]{1,0:T(8,128)(2,1)S(1)}, u32[]{:S(2)}, u32[]{:S(2)}) collective-permute-start(bf16[112,768]{1,0:T(8,128)(2,1)S(1)} %get-tuple-element.148), channel_id=1, source_target_pairs={{0,2},{1,3},{2,0},{3,1},{4,6},{5,7},{6,4},{7,5},{8,10},{9,11},{10,... | collective-permute-start | bytes 516104 | tf_op jit(solution)/shard_map/ppermute | solution.py:778
  209.2 2.7 %collective-permute-start.28 = (bf16[96,768]{1,0:T(8,128)(2,1)S(1)}, bf16[96,768]{1,0:T(8,128)(2,1)S(1)}, u32[]{:S(2)}, u32[]{:S(2)}) collective-permute-start(bf16[96,768]{1,0:T(8,128)(2,1)S(1)} %pad_maximum_fusion.3.refs_0_), channel_id=1, source_target_pairs={{0,1},{1,0},{2,3},{3,2},{4,5},{5,4},{6,7},{7,6},{8,9},{9,8},{10,11... | collective-permute-start | bytes 442376 | tf_op jit(solution)/shard_map/ppermute | solution.py:778
  211.5 1.5 collective-permute-start.29
  211.8 4.0 %copy-start = (f32[96,3072]{1,0:T(8,128)}, f32[96,3072]{1,0:T(8,128)S(1)}, u32[]{:S(2)}) copy-start(f32[96,3072]{1,0:T(8,128)S(1)} %fusion.5.refs_7_) | copy-start | bytes 3538948
  212.0 3.9 %copy-start.1 = (f32[384,768]{1,0:T(8,128)}, f32[384,768]{1,0:T(8,128)S(1)}, u32[]{:S(2)}) copy-start(f32[384,768]{1,0:T(8,128)S(1)} %fusion.4.refs_6_) | copy-start | bytes 3538948
